TPU v7x, 128 devices: a whole 4x4x4 slice. The times are simulated.
128 devices in a mesh: azim: 32 (over x, y, core), axial: 4 (over z).
Axes of the slice: x: 4, y: 4, z: 4, core: 2. Of those that a mesh axis runs over, the one named last changes fastest.
Arguments:
- fluid_vel: float32 [3, 128, 64, 128], P(None, 'azim', 'axial'), may hold values from -6 to 6
- pressure: float32 [128, 64, 128], P('azim', 'axial'), may hold values from -6 to 6
- part_vel: float32 [65536, 3, 128], P(('azim', 'axial')), may hold values from -6 to 6
- part_vol: float32 [65536, 128], P(('azim', 'axial')), may hold values from 0.05 to 0.5
- part_drag: float32 [65536, 128], P(('azim', 'axial')), may hold values from 0.5 to 4
- cell_of: int32 [65536, 128], P(('azim', 'axial')), may hold values from 0 to 8191
- dest_of: int32 [65536, 1], P(('azim', 'axial')), may hold values from 0 to 31; in each aligned block of 512 rows (0 to 511, 512 to 1023, ...) at most 32 rows name the same one
Outputs:
- fluid_out: float32 [3, 128, 64, 128], P(None, 'azim', 'axial')
- part_out: float32 [65536, 3, 128], P(('azim', 'axial'))
Inputs may be any that keep to these rules, and one draw needn't show every extreme that they name: `dest_of`: among the 512 blocks of one device, at most 32 name the same owner, and in every draw some owner is named by exactly 32 of them.
All inputs are finite; a program needn't handle non-finite values.
Results may differ from a plain program's by a relative error of at most 0.00007.
Values sent between devices are 32-bit elements; how exact they have to be, the bound alone decides.
No kernel may reach another device: no remote copies, remote signals or barrier semaphores. Data moves between devices by JAX's collectives and lax.ppermute only.
A program may use at most 64 MiB of HBM per device.

v0:
```python
import jax
import jax.numpy as jnp
from jax import lax
from jax.sharding import PartitionSpec as P

TIME_STEP = 0.25
VISCOSITY = 0.5


def padded_2(value, sides, width, wrap):
    for axis, dim in sides:
        size, length = (lax.axis_size(axis), value.shape[dim])
        up = [(i, (i + 1) % size) for i in range(size if wrap else size - 1)]
        down = [(j, i) for i, j in up]
        last = lax.slice_in_dim(value, length - width, length, axis=dim)
        first = lax.slice_in_dim(value, 0, width, axis=dim)
        before = lax.ppermute(last, axis, up)
        after = lax.ppermute(first, axis, down)
        value = jnp.concatenate([before, value, after], axis=dim)
    return value


def combine(stacked, solid, source, neighbours):
    padded = jnp.pad(stacked, ((0, 0), (0, 0), (0, 0), (1, 1)))
    every = neighbours + [padded[..., 2:], padded[..., :-2]]
    voidage = stacked[0]
    flow = stacked[2:]
    spread = jnp.zeros_like(flow)
    for other in every:
        spread = spread + 0.5 * (voidage + other[0]) * (other[2:] - flow)
    slope = 0.5 * jnp.stack(
        [every[0][1] - every[1][1], every[2][1] - every[3][1], every[4][1] - every[5][1]]
    )
    return flow + TIME_STEP * ((1.0 + solid) * (VISCOSITY * spread + source) - slope)


def one_hots(cell_ids, rows_tile, radial):
    row_hot = (
        cell_ids[:, None] // radial == jnp.arange(rows_tile, dtype=jnp.int32)[None, :]
    ).astype(jnp.float32)
    col_hot = (cell_ids[:, None] % radial == jnp.arange(radial, dtype=jnp.int32)[None, :]).astype(
        jnp.float32
    )
    return (row_hot, col_hot)


def on_device(fluid_vel, pressure, part_vel, part_vol, part_drag, cell_of, dest_of):
    highest = lax.Precision.HIGHEST
    azim_count = lax.axis_size("azim")
    blocks, block_rows = part_vol.shape
    tile_azim, tile_axial, radial = pressure.shape
    rows_tile = tile_azim * tile_axial
    slot_count = 2 * blocks
    capacity = slot_count // azim_count
    destination = dest_of[:, 0]
    dest_hot = (destination[:, None] == jnp.arange(azim_count, dtype=jnp.int32)[None, :]).astype(
        jnp.int32
    )
    order_in = jnp.sum(
        (jnp.cumsum(dest_hot, axis=0, dtype=jnp.int32) - dest_hot) * dest_hot, axis=1
    )
    slot_index = destination * capacity + order_in
    send_vel = jnp.zeros((slot_count, 3, block_rows), jnp.float32).at[slot_index].set(part_vel)
    send_vol = jnp.zeros((slot_count, block_rows), jnp.float32).at[slot_index].set(part_vol)
    send_drag = jnp.zeros((slot_count, block_rows), jnp.float32).at[slot_index].set(part_drag)
    send_cell = jnp.zeros((slot_count, block_rows), jnp.int32).at[slot_index].set(cell_of)
    got_vel, got_vol, got_drag, got_cell = (
        lax.all_to_all(send_vel, "azim", split_axis=0, concat_axis=0, tiled=True),
        lax.all_to_all(send_vol, "azim", split_axis=0, concat_axis=0, tiled=True),
        lax.all_to_all(send_drag, "azim", split_axis=0, concat_axis=0, tiled=True),
        lax.all_to_all(send_cell, "azim", split_axis=0, concat_axis=0, tiled=True),
    )
    group_size = max(32, slot_count // 16)
    turn_count = slot_count // group_size
    turn_rows = group_size * block_rows
    cell_turns = got_cell.reshape(turn_count, turn_rows)
    vol_turns = got_vol.reshape(turn_count, turn_rows)
    drag_turns = got_drag.reshape(turn_count, turn_rows)
    vel_turns = jnp.transpose(
        got_vel.reshape(turn_count, group_size, 3, block_rows), (0, 2, 1, 3)
    ).reshape(turn_count, 3, turn_rows)

    def deposit(solid_sum, pieces):
        cell_ids, volume = pieces
        row_hot, col_hot = one_hots(cell_ids, rows_tile, radial)
        solid_sum = solid_sum + jnp.einsum(
            "pr,pc->rc", row_hot * volume[:, None], col_hot, precision=highest
        )
        return (solid_sum, None)

    solid_flat, _ = lax.scan(
        deposit, jnp.zeros((rows_tile, radial), jnp.float32), (cell_turns, vol_turns)
    )
    fields = jnp.concatenate([fluid_vel.reshape(3, rows_tile, radial), solid_flat[None]], 0)

    def interact(force_sum, pieces):
        cell_ids, volume, drag, velocity = pieces
        row_hot, col_hot = one_hots(cell_ids, rows_tile, radial)
        picked = jnp.einsum("pc,frc->fpr", col_hot, fields, precision=highest)
        at_cell = jnp.sum(picked * row_hot[None], axis=2)
        flow_here = at_cell[:3]
        drag_rate = drag * (1.0 + at_cell[3])
        new_vel = (velocity + TIME_STEP * drag_rate * flow_here) / (1.0 + TIME_STEP * drag_rate)
        push_force = volume * drag_rate * (new_vel - flow_here)
        force_sum = force_sum + jnp.einsum(
            "fpr,pc->frc", push_force[:, :, None] * row_hot[None], col_hot, precision=highest
        )
        return (force_sum, new_vel)

    source_flat, new_turns = lax.scan(
        interact,
        jnp.zeros((3, rows_tile, radial), jnp.float32),
        (cell_turns, vol_turns, drag_turns, vel_turns),
    )
    new_slots = jnp.transpose(
        new_turns.reshape(turn_count, 3, group_size, block_rows), (0, 2, 1, 3)
    ).reshape(slot_count, 3, block_rows)
    returned = lax.all_to_all(new_slots, "azim", split_axis=0, concat_axis=0, tiled=True)
    part_out = returned[slot_index]
    solid = solid_flat.reshape(tile_azim, tile_axial, radial)
    source = source_flat.reshape(3, tile_azim, tile_axial, radial)
    voidage = 1.0 / (1.0 + solid)
    stacked = jnp.concatenate([voidage[None], pressure[None], fluid_vel], 0)
    cycle_fields = padded_2(stacked, (("azim", 1),), 1, True)
    axial_fields = padded_2(stacked, (("axial", 2),), 1, False)
    neighbours = [
        cycle_fields[:, 2:],
        cycle_fields[:, :-2],
        axial_fields[:, :, 2:],
        axial_fields[:, :, :-2],
    ]
    fluid_out = combine(stacked, solid, source, neighbours)
    return (fluid_out, part_out)


def solution(mesh):
    in_specs = (
        P(None, "azim", "axial", None),
        P("azim", "axial", None),
        P(("azim", "axial"), None, None),
        P(("azim", "axial"), None),
        P(("azim", "axial"), None),
        P(("azim", "axial"), None),
        P(("azim", "axial"), None),
    )
    out_specs = (P(None, "azim", "axial", None), P(("azim", "axial"), None, None))
    return jax.shard_map(
        on_device, mesh=mesh, in_specs=in_specs, out_specs=out_specs, check_vma=False
    )
```

profile of v0, /device:TPU:0, one launch (start us, length us, event | category | flops | bytes accessed | tf_op | source)
XLA Modules:
  0.0 393.6 jit_solution(12152478225165701422)
XLA Ops:
  4.2 2.9 scatter_custom_fusion.1
  7.1 7.5 %all-to-all-start.1 = ((f32[32,32,128]{2,1,0:T(8,128)}), f32[32,32,128]{2,1,0:T(8,128)S(1)}, u32[]{:S(2)}, u32[]{:S(2)}) async-start(f32[32,32,128]{2,1,0:T(8,128)} %bitcast.6), calls=%async_computation.1 | async-start | bytes 1048576 | tf_op jit(solution)/shard_map/all_to_all | solution.py:69
  14.6 2.9 scatter_custom_fusion
  17.5 8.3 %all-to-all-done.1 = f32[32,32,128]{2,1,0:T(8,128)S(1)} async-done(((f32[32,32,128]{2,1,0:T(8,128)}), f32[32,32,128]{2,1,0:T(8,128)S(1)}, u32[]{:S(2)}, u32[]{:S(2)}) %all-to-all-start.1) | async-done | bytes 524320 | tf_op jit(solution)/shard_map/all_to_all | solution.py:69
  25.8 4.1 %all-to-all-start = ((s32[32,32,128]{2,1,0:T(8,128)}), s32[32,32,128]{2,1,0:T(8,128)S(1)}, u32[]{:S(2)}, u32[]{:S(2)}) async-start(s32[32,32,128]{2,1,0:T(8,128)} %bitcast.5), calls=%async_computation | async-start | bytes 1048576 | tf_op jit(solution)/shard_map/all_to_all | solution.py:71
  29.9 2.9 scatter_custom_fusion.2
  32.8 8.3 %all-to-all-done = s32[32,32,128]{2,1,0:T(8,128)S(1)} async-done(((s32[32,32,128]{2,1,0:T(8,128)}), s32[32,32,128]{2,1,0:T(8,128)S(1)}, u32[]{:S(2)}, u32[]{:S(2)}) %all-to-all-start) | async-done | bytes 524320 | tf_op jit(solution)/shard_map/all_to_all | solution.py:71
  41.1 4.1 %all-to-all-start.2 = ((f32[32,32,128]{2,1,0:T(8,128)}), f32[32,32,128]{2,1,0:T(8,128)S(1)}, u32[]{:S(2)}, u32[]{:S(2)}) async-start(f32[32,32,128]{2,1,0:T(8,128)} %bitcast.16), calls=%async_computation.2 | async-start | bytes 1048576 | tf_op jit(solution)/shard_map/all_to_all | solution.py:70
  47.3 47.5 %scatter_fusion = f32[1024,3,128]{2,1,0:T(4,128)} fusion(f32[1024,3,128]{2,1,0:T(4,128)} %broadcast_in_dim.46, s32[512]{0:T(512)S(1)} %bitcast.143, f32[512,3,128]{2,1,0:T(4,128)S(1)} %copy.17), kind=kCustom, calls=%fused_computation.4 | custom fusion | bytes 2361344 | tf_op jit(solution)/shard_map/scatter | solution.py:63
  95.9 7.7 %all-to-all-start.3 = ((f32[1024,3,128]{2,1,0:T(4,128)}), f32[1024,3,128]{2,1,0:T(4,128)S(1)}, u32[]{:S(2)}, u32[]{:S(2)}) async-start(f32[1024,3,128]{2,1,0:T(4,128)} %scatter_fusion), calls=%async_computation.3 | async-start | bytes 4194304 | tf_op jit(solution)/shard_map/all_to_all | solution.py:68
  103.6 49.2 %while.28 = (s32[]{:T(128)}, f32[64,128]{1,0:T(8,128)S(1)}, s32[16,8192]{1,0:T(8,128)S(1)}, f32[16,8192]{1,0:T(8,128)}, s32[]{:T(128)}, /*index=5*/s32[]{:T(128)}) while((s32[]{:T(128)}, f32[64,128]{1,0:T(8,128)S(1)}, s32[16,8192]{1,0:T(8,128)S(1)}, f32[16,8192]{1,0:T(8,128)}, s32[]{:T(128)}, /*index=5*/s32[]{:T(128)}) %tuple.84), condition=%wide.region_6.7_spmd.clone, body=%wide.region_5.6_spmd.clone.sunk | while | flops 807575552 | bytes 393311 | solution.py:91
  104.7 2.0 fusion.95
  107.8 2.0 fusion.95
  113.9 2.0 fusion.95
  117.0 2.0 fusion.95
  120.1 2.0 fusion.95
  123.1 2.0 fusion.95
  126.2 2.0 fusion.95
  129.3 2.0 fusion.95
  132.3 2.0 fusion.95
  138.5 2.0 fusion.95
  141.6 2.0 fusion.95
  147.7 2.0 fusion.95
  156.6 191.0 %while.29 = (s32[]{:T(128)}, f32[3,64,128]{2,1,0:T(8,128)S(1)}, f32[16,3,8192]{2,1,0:T(4,128)}, f32[16,8192]{1,0:T(8,128)}, f32[16,8192]{1,0:T(8,128)}, /*index=...) while((s32[]{:T(128)}, f32[3,64,128]{2,1,0:T(8,128)S(1)}, ...), condition=%wide.region_11.12_spmd.clone, body=%wide.region_9.11_spmd.clone.sunk | while | flops 5646475264 | bytes 8355979 | solution.py:110
  156.9 4.9 %fusion.101 = f32[8192,4]{0,1:T(4,128)S(1)} fusion(f32[8192,64]{0,1:T(8,128)S(1)} %fusion.100, f32[4,64,128]{2,1,0:T(8,128)S(1)} %get-tuple-element.409, s32[8192]{0:T(1024)S(1)} %get-tuple-element.359), kind=kOutput, calls=%fused_computation.32.clone.1 | convolution fusion | flops 3226435584 | bytes 2392064 | tf_op jit(solution)/shard_map/while/body/eval_jaxpr/pc,frc->fpr/dot_general | solution.py:99
  164.0 3.8 fusion.102
  168.8 4.9 %fusion.101 = f32[8192,4]{0,1:T(4,128)S(1)} fusion(f32[8192,64]{0,1:T(8,128)S(1)} %fusion.100, f32[4,64,128]{2,1,0:T(8,128)S(1)} %get-tuple-element.409, s32[8192]{0:T(1024)S(1)} %get-tuple-element.359), kind=kOutput, calls=%fused_computation.32.clone.1 | convolution fusion | flops 3226435584 | bytes 2392064 | tf_op jit(solution)/shard_map/while/body/eval_jaxpr/pc,frc->fpr/dot_general | solution.py:99
  175.9 3.8 fusion.102
  180.8 4.9 %fusion.101 = f32[8192,4]{0,1:T(4,128)S(1)} fusion(f32[8192,64]{0,1:T(8,128)S(1)} %fusion.100, f32[4,64,128]{2,1,0:T(8,128)S(1)} %get-tuple-element.409, s32[8192]{0:T(1024)S(1)} %get-tuple-element.359), kind=kOutput, calls=%fused_computation.32.clone.1 | convolution fusion | flops 3226435584 | bytes 2392064 | tf_op jit(solution)/shard_map/while/body/eval_jaxpr/pc,frc->fpr/dot_general | solution.py:99
  187.9 3.8 fusion.102
  192.7 4.9 %fusion.101 = f32[8192,4]{0,1:T(4,128)S(1)} fusion(f32[8192,64]{0,1:T(8,128)S(1)} %fusion.100, f32[4,64,128]{2,1,0:T(8,128)S(1)} %get-tuple-element.409, s32[8192]{0:T(1024)S(1)} %get-tuple-element.359), kind=kOutput, calls=%fused_computation.32.clone.1 | convolution fusion | flops 3226435584 | bytes 2392064 | tf_op jit(solution)/shard_map/while/body/eval_jaxpr/pc,frc->fpr/dot_general | solution.py:99
  199.8 3.8 fusion.102
  204.7 4.9 %fusion.101 = f32[8192,4]{0,1:T(4,128)S(1)} fusion(f32[8192,64]{0,1:T(8,128)S(1)} %fusion.100, f32[4,64,128]{2,1,0:T(8,128)S(1)} %get-tuple-element.409, s32[8192]{0:T(1024)S(1)} %get-tuple-element.359), kind=kOutput, calls=%fused_computation.32.clone.1 | convolution fusion | flops 3226435584 | bytes 2392064 | tf_op jit(solution)/shard_map/while/body/eval_jaxpr/pc,frc->fpr/dot_general | solution.py:99
  211.7 3.8 fusion.102
  216.6 4.9 %fusion.101 = f32[8192,4]{0,1:T(4,128)S(1)} fusion(f32[8192,64]{0,1:T(8,128)S(1)} %fusion.100, f32[4,64,128]{2,1,0:T(8,128)S(1)} %get-tuple-element.409, s32[8192]{0:T(1024)S(1)} %get-tuple-element.359), kind=kOutput, calls=%fused_computation.32.clone.1 | convolution fusion | flops 3226435584 | bytes 2392064 | tf_op jit(solution)/shard_map/while/body/eval_jaxpr/pc,frc->fpr/dot_general | solution.py:99
  223.7 3.8 fusion.102
  228.5 4.9 %fusion.101 = f32[8192,4]{0,1:T(4,128)S(1)} fusion(f32[8192,64]{0,1:T(8,128)S(1)} %fusion.100, f32[4,64,128]{2,1,0:T(8,128)S(1)} %get-tuple-element.409, s32[8192]{0:T(1024)S(1)} %get-tuple-element.359), kind=kOutput, calls=%fused_computation.32.clone.1 | convolution fusion | flops 3226435584 | bytes 2392064 | tf_op jit(solution)/shard_map/while/body/eval_jaxpr/pc,frc->fpr/dot_general | solution.py:99
  235.6 3.8 fusion.102
  240.5 4.9 %fusion.101 = f32[8192,4]{0,1:T(4,128)S(1)} fusion(f32[8192,64]{0,1:T(8,128)S(1)} %fusion.100, f32[4,64,128]{2,1,0:T(8,128)S(1)} %get-tuple-element.409, s32[8192]{0:T(1024)S(1)} %get-tuple-element.359), kind=kOutput, calls=%fused_computation.32.clone.1 | convolution fusion | flops 3226435584 | bytes 2392064 | tf_op jit(solution)/shard_map/while/body/eval_jaxpr/pc,frc->fpr/dot_general | solution.py:99
  247.5 3.8 fusion.102
  252.4 4.9 %fusion.101 = f32[8192,4]{0,1:T(4,128)S(1)} fusion(f32[8192,64]{0,1:T(8,128)S(1)} %fusion.100, f32[4,64,128]{2,1,0:T(8,128)S(1)} %get-tuple-element.409, s32[8192]{0:T(1024)S(1)} %get-tuple-element.359), kind=kOutput, calls=%fused_computation.32.clone.1 | convolution fusion | flops 3226435584 | bytes 2392064 | tf_op jit(solution)/shard_map/while/body/eval_jaxpr/pc,frc->fpr/dot_general | solution.py:99
  259.5 3.8 fusion.102
  264.3 4.9 %fusion.101 = f32[8192,4]{0,1:T(4,128)S(1)} fusion(f32[8192,64]{0,1:T(8,128)S(1)} %fusion.100, f32[4,64,128]{2,1,0:T(8,128)S(1)} %get-tuple-element.409, s32[8192]{0:T(1024)S(1)} %get-tuple-element.359), kind=kOutput, calls=%fused_computation.32.clone.1 | convolution fusion | flops 3226435584 | bytes 2392064 | tf_op jit(solution)/shard_map/while/body/eval_jaxpr/pc,frc->fpr/dot_general | solution.py:99
  271.4 3.8 fusion.102
  276.3 4.9 %fusion.101 = f32[8192,4]{0,1:T(4,128)S(1)} fusion(f32[8192,64]{0,1:T(8,128)S(1)} %fusion.100, f32[4,64,128]{2,1,0:T(8,128)S(1)} %get-tuple-element.409, s32[8192]{0:T(1024)S(1)} %get-tuple-element.359), kind=kOutput, calls=%fused_computation.32.clone.1 | convolution fusion | flops 3226435584 | bytes 2392064 | tf_op jit(solution)/shard_map/while/body/eval_jaxpr/pc,frc->fpr/dot_general | solution.py:99
  283.3 3.8 fusion.102
  288.2 4.9 %fusion.101 = f32[8192,4]{0,1:T(4,128)S(1)} fusion(f32[8192,64]{0,1:T(8,128)S(1)} %fusion.100, f32[4,64,128]{2,1,0:T(8,128)S(1)} %get-tuple-element.409, s32[8192]{0:T(1024)S(1)} %get-tuple-element.359), kind=kOutput, calls=%fused_computation.32.clone.1 | convolution fusion | flops 3226435584 | bytes 2392064 | tf_op jit(solution)/shard_map/while/body/eval_jaxpr/pc,frc->fpr/dot_general | solution.py:99
  295.3 3.8 fusion.102
  300.1 4.9 %fusion.101 = f32[8192,4]{0,1:T(4,128)S(1)} fusion(f32[8192,64]{0,1:T(8,128)S(1)} %fusion.100, f32[4,64,128]{2,1,0:T(8,128)S(1)} %get-tuple-element.409, s32[8192]{0:T(1024)S(1)} %get-tuple-element.359), kind=kOutput, calls=%fused_computation.32.clone.1 | convolution fusion | flops 3226435584 | bytes 2392064 | tf_op jit(solution)/shard_map/while/body/eval_jaxpr/pc,frc->fpr/dot_general | solution.py:99
  307.2 3.8 fusion.102
  312.1 4.9 %fusion.101 = f32[8192,4]{0,1:T(4,128)S(1)} fusion(f32[8192,64]{0,1:T(8,128)S(1)} %fusion.100, f32[4,64,128]{2,1,0:T(8,128)S(1)} %get-tuple-element.409, s32[8192]{0:T(1024)S(1)} %get-tuple-element.359), kind=kOutput, calls=%fused_computation.32.clone.1 | convolution fusion | flops 3226435584 | bytes 2392064 | tf_op jit(solution)/shard_map/while/body/eval_jaxpr/pc,frc->fpr/dot_general | solution.py:99
  319.1 3.8 fusion.102
  324.0 4.9 %fusion.101 = f32[8192,4]{0,1:T(4,128)S(1)} fusion(f32[8192,64]{0,1:T(8,128)S(1)} %fusion.100, f32[4,64,128]{2,1,0:T(8,128)S(1)} %get-tuple-element.409, s32[8192]{0:T(1024)S(1)} %get-tuple-element.359), kind=kOutput, calls=%fused_computation.32.clone.1 | convolution fusion | flops 3226435584 | bytes 2392064 | tf_op jit(solution)/shard_map/while/body/eval_jaxpr/pc,frc->fpr/dot_general | solution.py:99
  331.1 3.8 fusion.102
  335.9 4.9 %fusion.101 = f32[8192,4]{0,1:T(4,128)S(1)} fusion(f32[8192,64]{0,1:T(8,128)S(1)} %fusion.100, f32[4,64,128]{2,1,0:T(8,128)S(1)} %get-tuple-element.409, s32[8192]{0:T(1024)S(1)} %get-tuple-element.359), kind=kOutput, calls=%fused_computation.32.clone.1 | convolution fusion | flops 3226435584 | bytes 2392064 | tf_op jit(solution)/shard_map/while/body/eval_jaxpr/pc,frc->fpr/dot_general | solution.py:99
  343.0 3.8 fusion.102
  347.5 2.9 reshape.351
  350.6 2.4 copy.21
  353.0 7.3 %all-to-all-start.4 = ((f32[1024,3,128]{2,1,0:T(4,128)}), f32[1024,3,128]{2,1,0:T(4,128)S(1)}, u32[]{:S(2)}, u32[]{:S(2)}) async-start(f32[1024,3,128]{2,1,0:T(4,128)} %copy.21), calls=%async_computation.4 | async-start | bytes 4194304 | tf_op jit(solution)/shard_map/all_to_all | solution.py:118
  361.8 4.5 %collective-permute-start.3 = (f32[5,4,1,128]{3,2,1,0:T(1,128)S(1)}, f32[5,4,1,128]{3,2,1,0:T(1,128)S(1)}, u32[]{:S(2)}, u32[]{:S(2)}) collective-permute-start(f32[5,4,1,128]{3,2,1,0:T(1,128)S(1)} %get-tuple-element.272), channel_id=1, source_target_pairs={{0,1},{1,2},{2,3},{4,5},{5,6},{6,7},{8,9},{9,10},{10,11},{12,13},{... | collective-permute-start | bytes 30728 | tf_op jit(solution)/shard_map/ppermute | solution.py:17
  366.4 4.6 %collective-permute-start = (f32[5,1,16,128]{3,2,1,0:T(8,128)S(1)}, f32[5,1,16,128]{3,2,1,0:T(8,128)S(1)}, u32[]{:S(2)}, u32[]{:S(2)}) collective-permute-start(f32[5,1,16,128]{3,2,1,0:T(8,128)S(1)} %get-tuple-element.269), channel_id=1, source_target_pairs={{4,0},{8,4},{12,8},{16,12},{20,16},{24,20},{28,24},{32,28},{36,32}... | collective-permute-start | bytes 122888 | tf_op jit(solution)/shard_map/ppermute | solution.py:18
  371.1 10.2 %collective-permute-done = f32[5,1,16,128]{3,2,1,0:T(8,128)S(1)} collective-permute-done((f32[5,1,16,128]{3,2,1,0:T(8,128)S(1)}, f32[5,1,16,128]{3,2,1,0:T(8,128)S(1)}, u32[]{:S(2)}, u32[]{:S(2)}) %collective-permute-start) | collective-permute-done | bytes 40992 | tf_op jit(solution)/shard_map/ppermute | solution.py:18
  381.3 8.5 %collective-permute-done.1 = f32[5,1,16,128]{3,2,1,0:T(8,128)S(1)} collective-permute-done((f32[5,1,16,128]{3,2,1,0:T(8,128)S(1)}, f32[5,1,16,128]{3,2,1,0:T(8,128)S(1)}, u32[]{:S(2)}, u32[]{:S(2)}) %collective-permute-start.1) | collective-permute-done | bytes 40992 | tf_op jit(solution)/shard_map/ppermute | solution.py:17
  390.5 2.1 gather_fusion
  (224 shorter events, 90.6 us)
Async XLA Ops:
  7.1 38.1 %copy-start.1 = (f32[512,3,128]{2,0,1:T(8,128)S(1)}, f32[512,3,128]{2,0,1:T(8,128)}, u32[]{:S(2)}) copy-start(f32[512,3,128]{2,0,1:T(8,128)} %param.13) | copy-start | bytes 2359300
  7.1 18.7 %all-to-all-start.1 = ((f32[32,32,128]{2,1,0:T(8,128)}), f32[32,32,128]{2,1,0:T(8,128)S(1)}, u32[]{:S(2)}, u32[]{:S(2)}) async-start(f32[32,32,128]{2,1,0:T(8,128)} %bitcast.6), calls=%async_computation.1 | async-start | bytes 1048576 | tf_op jit(solution)/shard_map/all_to_all | solution.py:69
  25.8 15.3 %all-to-all-start = ((s32[32,32,128]{2,1,0:T(8,128)}), s32[32,32,128]{2,1,0:T(8,128)S(1)}, u32[]{:S(2)}, u32[]{:S(2)}) async-start(s32[32,32,128]{2,1,0:T(8,128)} %bitcast.5), calls=%async_computation | async-start | bytes 1048576 | tf_op jit(solution)/shard_map/all_to_all | solution.py:71
  41.1 54.8 %all-to-all-start.2 = ((f32[32,32,128]{2,1,0:T(8,128)}), f32[32,32,128]{2,1,0:T(8,128)S(1)}, u32[]{:S(2)}, u32[]{:S(2)}) async-start(f32[32,32,128]{2,1,0:T(8,128)} %bitcast.16), calls=%async_computation.2 | async-start | bytes 1048576 | tf_op jit(solution)/shard_map/all_to_all | solution.py:70
  95.9 57.8 %all-to-all-start.3 = ((f32[1024,3,128]{2,1,0:T(4,128)}), f32[1024,3,128]{2,1,0:T(4,128)S(1)}, u32[]{:S(2)}, u32[]{:S(2)}) async-start(f32[1024,3,128]{2,1,0:T(4,128)} %scatter_fusion), calls=%async_computation.3 | async-start | bytes 4194304 | tf_op jit(solution)/shard_map/all_to_all | solution.py:68
  103.6 50.1 %copy-start = (f32[3,4,16,128]{3,2,1,0:T(8,128)S(1)}, f32[3,4,16,128]{3,2,1,0:T(8,128)}, u32[]{:S(2)}) copy-start(f32[3,4,16,128]{3,2,1,0:T(8,128)} %param.11) | copy-start | bytes 294916
  154.9 1.6 copy-start.3
  353.0 7.4 %copy-start.2 = (f32[4,16,128]{2,1,0:T(8,128)S(1)}, f32[4,16,128]{2,1,0:T(8,128)}, u32[]{:S(2)}) copy-start(f32[4,16,128]{2,1,0:T(8,128)} %param.12) | copy-start | bytes 98308
  353.0 37.5 %all-to-all-start.4 = ((f32[1024,3,128]{2,1,0:T(4,128)}), f32[1024,3,128]{2,1,0:T(4,128)S(1)}, u32[]{:S(2)}, u32[]{:S(2)}) async-start(f32[1024,3,128]{2,1,0:T(4,128)} %copy.21), calls=%async_computation.4 | async-start | bytes 4194304 | tf_op jit(solution)/shard_map/all_to_all | solution.py:118
  360.5 10.6 %collective-permute-start.2 = (f32[5,4,1,128]{3,2,1,0:T(1,128)S(1)}, f32[5,4,1,128]{3,2,1,0:T(1,128)S(1)}, u32[]{:S(2)}, u32[]{:S(2)}) collective-permute-start(f32[5,4,1,128]{3,2,1,0:T(1,128)S(1)} %get-tuple-element.271), channel_id=1, source_target_pairs={{1,0},{2,1},{3,2},{5,4},{6,5},{7,6},{9,8},{10,9},{11,10},{13,12},{... | collective-permute-start | bytes 30728 | tf_op jit(solution)/shard_map/ppermute | solution.py:18
  361.8 9.3 %collective-permute-start.3 = (f32[5,4,1,128]{3,2,1,0:T(1,128)S(1)}, f32[5,4,1,128]{3,2,1,0:T(1,128)S(1)}, u32[]{:S(2)}, u32[]{:S(2)}) collective-permute-start(f32[5,4,1,128]{3,2,1,0:T(1,128)S(1)} %get-tuple-element.272), channel_id=1, source_target_pairs={{0,1},{1,2},{2,3},{4,5},{5,6},{6,7},{8,9},{9,10},{10,11},{12,13},{... | collective-permute-start | bytes 30728 | tf_op jit(solution)/shard_map/ppermute | solution.py:17
  366.4 14.8 %collective-permute-start = (f32[5,1,16,128]{3,2,1,0:T(8,128)S(1)}, f32[5,1,16,128]{3,2,1,0:T(8,128)S(1)}, u32[]{:S(2)}, u32[]{:S(2)}) collective-permute-start(f32[5,1,16,128]{3,2,1,0:T(8,128)S(1)} %get-tuple-element.269), channel_id=1, source_target_pairs={{4,0},{8,4},{12,8},{16,12},{20,16},{24,20},{28,24},{32,28},{36,32}... | collective-permute-start | bytes 122888 | tf_op jit(solution)/shard_map/ppermute | solution.py:18
  371.0 18.7 %collective-permute-start.1 = (f32[5,1,16,128]{3,2,1,0:T(8,128)S(1)}, f32[5,1,16,128]{3,2,1,0:T(8,128)S(1)}, u32[]{:S(2)}, u32[]{:S(2)}) collective-permute-start(f32[5,1,16,128]{3,2,1,0:T(8,128)S(1)} %get-tuple-element.270), channel_id=1, source_target_pairs={{0,4},{4,8},{8,12},{12,16},{16,20},{20,24},{24,28},{28,32},{32,36}... | collective-permute-start | bytes 122888 | tf_op jit(solution)/shard_map/ppermute | solution.py:17
where the time goes:
time: 397 us; the launch traced here: 394 us
  matrix products  170 us (43%)
  local copies, waits for them, and re-layouts  89.7 us (23%)
  other arithmetic  55.3 us (14%)
  starting transfers between devices  41.1 us (10%)
  waiting for transfers between devices  35.3 us (9%)
    dot_general x16, matrix products, interact(): picked = jnp.einsum('pc,frc->fpr', col_hot, fields, precision=highest)  78 us
    dot_general x16, matrix products, interact(): jnp.einsum('fpr,pc->frc', push_force[:, :, None] * row_hot[None], col_hot...  60 us
    scatter x1, local copies, waits for them, and re-layouts, on_device(): jnp.zeros((slot_count, 3, block_rows), jnp.float32).at[slot_index]  47.5 us
    dot_general x16, matrix products, deposit(): jnp.einsum('pr,pc->rc', row_hot * volume[:, None], col_hot, precision=hig...  31.7 us
    dynamic_slice x48, local copies, waits for them, and re-layouts, on_device(): lax.scan(deposit, jnp.zeros((rows_tile, radial), jnp.float32), (cell_turn...  16.7 us
    mul x16, other arithmetic, interact(): TIME_STEP * drag_rate * flow_here  16.5 us
    add x16, other arithmetic, interact(): 1.0 + TIME_STEP * drag_rate  16.3 us
    dynamic_update_slice x16, other arithmetic, on_device(): lax.scan(interact, jnp.zeros((3, rows_tile, radial), jnp.float32), (cell_...  12.3 us
  transfers between devices with their start and end apart: 9, of which 4 were waited for; matrix products, arithmetic and copies ran while one was open for 27% of the time, Pallas kernels for 0%

commit v1 on v0

v1 whole, which is shorter than its diff:
```python
import functools

import jax
import jax.numpy as jnp
from jax import lax
from jax.experimental import pallas as pl
from jax.experimental.pallas import tpu as pltpu
from jax.sharding import PartitionSpec as P

TIME_STEP = 0.25
VISCOSITY = 0.5
BF, F32, I32 = jnp.bfloat16, jnp.float32, jnp.int32
LANES = 128
HALF = 32
VMEM_LIMIT = 60 * 2**20


def row(ref, b):
    return ref[pl.ds(b, 1), :]


def two_parts(value):
    high = value.astype(BF)
    return high, (value - high.astype(F32)).astype(BF)


def columns_of(cell):
    return (cell & 127) | ((cell >> 12) << 7)


def scatter_rows(dest_ref, cell_ref, value_of, fields, out_ref, turned_ref, unroll):
    blocks = cell_ref.shape[0]
    groups = blocks // LANES
    out_ref[...] = jnp.zeros_like(out_ref)
    for g in range(groups):
        ids = columns_of(cell_ref[g * LANES : (g + 1) * LANES, :])
        turned_ref[g] = ids.astype(F32).T.astype(BF)
    lane = lax.broadcasted_iota(I32, (LANES, LANES), 1)
    lanes = [(lane + k * LANES).astype(F32).astype(BF) for k in range(2)]
    rows = lax.broadcasted_iota(I32, (HALF, LANES), 0).astype(F32).astype(BF)
    one, zero = jnp.ones((), BF), jnp.zeros((), BF)

    def product(g, j):
        b = g * LANES + j
        in_half = ((row(cell_ref, b) >> 7) & (HALF - 1)).astype(F32).astype(BF)
        mask = rows == jnp.broadcast_to(in_half, (HALF, LANES))
        parts = []
        for f in range(fields):
            high, low = two_parts(value_of(f, b))
            parts.append(jnp.where(mask, jnp.broadcast_to(high, (HALF, LANES)), zero))
            parts.append(jnp.where(mask, jnp.broadcast_to(low, (HALF, LANES)), zero))
        spread = jnp.broadcast_to(turned_ref[g][:, j : j + 1], (LANES, LANES))
        hot = jnp.concatenate([jnp.where(k == spread, one, zero) for k in lanes], axis=1)
        return jnp.dot(jnp.concatenate(parts, axis=0), hot, preferred_element_type=F32)

    def step(g, carry):
        for i in range(LANES // unroll):
            first = i * unroll
            got = [(first + u, product(g, first + u)) for u in range(unroll)]
            for j, res in got:
                d = dest_ref[g * LANES + j]
                for f in range(fields):
                    at = 2 * f * HALF
                    both = res[at : at + HALF] + res[at + HALF : at + 2 * HALF]
                    out_ref[d, f, 0:HALF, :] += both[:, :LANES]
                    out_ref[d, f, HALF : 2 * HALF, :] += both[:, LANES:]
        return carry

    lax.fori_loop(0, groups, step, 0)


def deposit_kernel(dest_ref, cell_ref, vol_ref, out_ref, turned_ref):
    scatter_rows(dest_ref, cell_ref, lambda f, b: row(vol_ref, b), 1, out_ref, turned_ref, 16)


def source_kernel(dest_ref, cell_ref, push_ref, out_ref, turned_ref):
    scatter_rows(
        dest_ref, cell_ref, lambda f, b: push_ref[f, pl.ds(b, 1), :], 3, out_ref, turned_ref, 8
    )


SMEM_SPEC = pl.BlockSpec(memory_space=pltpu.SMEM)
VMEM_SPEC = pl.BlockSpec(memory_space=pltpu.VMEM)
ANY_SPEC = pl.BlockSpec(memory_space=pl.ANY)


def scatter(kernel, dest, cell, values, fields, tiles, tile_rows):
    blocks = cell.shape[0]
    return pl.pallas_call(
        kernel,
        out_shape=jax.ShapeDtypeStruct((tiles, fields, tile_rows, LANES), F32),
        in_specs=[SMEM_SPEC, VMEM_SPEC, VMEM_SPEC],
        out_specs=VMEM_SPEC,
        scratch_shapes=[pltpu.VMEM((blocks // LANES, LANES, LANES), BF)],
        compiler_params=pltpu.CompilerParams(vmem_limit_bytes=VMEM_LIMIT),
    )(dest, cell, values)


def pick_rows(dest_ref, cell_ref, table_ref, fields, store, unroll):
    blocks = cell_ref.shape[0]
    eights = table_ref.shape[2] // 8
    sub = lax.broadcasted_iota(I32, (8, LANES), 0)

    def step(i, carry):
        for u in range(unroll):
            b = i * unroll + u
            d = dest_ref[b]
            cell = jnp.broadcast_to(row(cell_ref, b), (8, LANES))
            column = cell & 127
            top = cell >> 10
            low = (cell >> 7) & 7
            for f in range(fields):
                acc = None
                for q in range(eights):
                    got = jnp.take_along_axis(
                        table_ref[d, f, 8 * q : 8 * q + 8, :],
                        column,
                        axis=1,
                        mode="promise_in_bounds",
                    )
                    acc = got if acc is None else jnp.where(top == q, got, acc)
                store(f, b, jnp.sum(jnp.where(sub == low, acc, 0.0), axis=0, keepdims=True))
        return carry

    lax.fori_loop(0, blocks // unroll, step, 0)


def load_tables(same_ref, other_ref, table_ref, sems):
    near = same_ref.shape[0]
    copies = [
        pltpu.make_async_copy(same_ref, table_ref.at[pl.ds(0, near)], sems.at[0]),
        pltpu.make_async_copy(other_ref, table_ref.at[pl.ds(near, near)], sems.at[1]),
    ]
    for copy in copies:
        copy.start()
    for copy in copies:
        copy.wait()


def flow_kernel(dest_ref, cell_ref, same_ref, other_ref, out_ref, table_ref, sems):
    load_tables(same_ref, other_ref, table_ref, sems)

    def store(f, b, value):
        out_ref[f, pl.ds(b, 1), :] = value

    pick_rows(dest_ref, cell_ref, table_ref, 3, store, 16)


def particle_kernel(
    dest_ref, cell_ref, vol_ref, drag_ref, vel_ref, flow_ref, same_ref, other_ref,
    new_ref, push_ref, table_ref, solid_ref, sems,
):
    load_tables(same_ref, other_ref, table_ref, sems)

    def store(f, b, value):
        solid_ref[pl.ds(b, 1), :] = value

    pick_rows(dest_ref, cell_ref, table_ref, 1, store, 16)
    blocks = cell_ref.shape[0]
    chunk = 32

    def step(i, carry):
        at = pl.ds(pl.multiple_of(i * chunk, chunk), chunk)
        rate = drag_ref[at, :] * (1.0 + solid_ref[at, :])
        weight = vol_ref[at, :] * rate
        scaled = TIME_STEP * rate
        below = 1.0 / (1.0 + scaled)
        for f in range(3):
            here = flow_ref[f, at, :]
            new = (vel_ref[f, at, :] + scaled * here) * below
            new_ref[f, at, :] = new
            push_ref[f, at, :] = weight * (new - here)
        return carry

    lax.fori_loop(0, blocks // chunk, step, 0, unroll=2)


def combine(stacked, solid, source, neighbours):
    padded = jnp.pad(stacked, ((0, 0), (0, 0), (0, 0), (1, 1)))
    every = neighbours + [padded[..., 2:], padded[..., :-2]]
    voidage = stacked[0]
    flow = stacked[2:]
    spread = jnp.zeros_like(flow)
    for other in every:
        spread = spread + 0.5 * (voidage + other[0]) * (other[2:] - flow)
    slope = 0.5 * jnp.stack(
        [every[0][1] - every[1][1], every[2][1] - every[3][1], every[4][1] - every[5][1]]
    )
    return flow + TIME_STEP * ((1.0 + solid) * (VISCOSITY * spread + source) - slope)


def padded_2(value, sides, width, wrap):
    for axis, dim in sides:
        size, length = (lax.axis_size(axis), value.shape[dim])
        up = [(i, (i + 1) % size) for i in range(size if wrap else size - 1)]
        down = [(j, i) for i, j in up]
        last = lax.slice_in_dim(value, length - width, length, axis=dim)
        first = lax.slice_in_dim(value, 0, width, axis=dim)
        before = lax.ppermute(last, axis, up)
        after = lax.ppermute(first, axis, down)
        value = jnp.concatenate([before, value, after], axis=dim)
    return value


def on_device(fluid_vel, pressure, part_vel, part_vol, part_drag, cell_of, dest_of):
    size = lax.axis_size("azim")
    near = size // 2
    blocks, block_rows = part_vol.shape
    tile_azim, tile_axial, radial = pressure.shape
    tile_rows = tile_azim * tile_axial
    core = lax.axis_index("azim") % 2
    chips = [[2 * i + c for i in range(near)] for c in range(2)]
    twin = [(i, i ^ 1) for i in range(size)]
    dest = dest_of[:, 0]
    slot = ((dest & 1) ^ core) * near + (dest >> 1)

    def exchange(value):
        return lax.all_to_all(
            value, "azim", split_axis=0, concat_axis=0, tiled=True, axis_index_groups=chips
        )

    def summed(parts):
        other = lax.ppermute(parts[near:], "azim", twin)
        got = exchange(parts[:near] + other)
        return jnp.sum(got, axis=0)

    def gathered(tile):
        same = exchange(jnp.broadcast_to(tile[None], (near,) + tile.shape))
        return same, lax.ppermute(same, "azim", twin)

    flow_tile = fluid_vel.reshape(3, tile_rows, radial)
    flow_same, flow_other = gathered(flow_tile)
    solid_parts = scatter(deposit_kernel, slot, cell_of, part_vol, 1, size, tile_rows)
    solid_flat = summed(solid_parts)
    solid_same, solid_other = gathered(solid_flat)
    params = pltpu.CompilerParams(vmem_limit_bytes=VMEM_LIMIT)
    per_particle = jax.ShapeDtypeStruct((3, blocks, block_rows), F32)
    flow_here = pl.pallas_call(
        flow_kernel,
        out_shape=per_particle,
        in_specs=[SMEM_SPEC, VMEM_SPEC, ANY_SPEC, ANY_SPEC],
        out_specs=VMEM_SPEC,
        scratch_shapes=[
            pltpu.VMEM((size, 3, tile_rows, radial), F32),
            pltpu.SemaphoreType.DMA((2,)),
        ],
        compiler_params=params,
    )(slot, cell_of, flow_same, flow_other)
    new_vel, push = pl.pallas_call(
        particle_kernel,
        out_shape=(per_particle, per_particle),
        in_specs=[SMEM_SPEC] + [VMEM_SPEC] * 5 + [ANY_SPEC] * 2,
        out_specs=(VMEM_SPEC, VMEM_SPEC),
        scratch_shapes=[
            pltpu.VMEM((size, 1, tile_rows, radial), F32),
            pltpu.VMEM((blocks, block_rows), F32),
            pltpu.SemaphoreType.DMA((2,)),
        ],
        compiler_params=params,
    )(
        slot, cell_of, part_vol, part_drag, jnp.transpose(part_vel, (1, 0, 2)), flow_here,
        solid_same, solid_other,
    )
    source_parts = scatter(source_kernel, slot, cell_of, push, 3, size, tile_rows)
    source_flat = summed(source_parts)
    part_out = jnp.transpose(new_vel, (1, 0, 2))
    solid = solid_flat.reshape(tile_azim, tile_axial, radial)
    source = source_flat.reshape(3, tile_azim, tile_axial, radial)
    voidage = 1.0 / (1.0 + solid)
    stacked = jnp.concatenate([voidage[None], pressure[None], fluid_vel], 0)
    cycle_fields = padded_2(stacked, (("azim", 1),), 1, True)
    axial_fields = padded_2(stacked, (("axial", 2),), 1, False)
    neighbours = [
        cycle_fields[:, 2:],
        cycle_fields[:, :-2],
        axial_fields[:, :, 2:],
        axial_fields[:, :, :-2],
    ]
    fluid_out = combine(stacked, solid, source, neighbours)
    return (fluid_out, part_out)


def solution(mesh):
    in_specs = (
        P(None, "azim", "axial", None),
        P("azim", "axial", None),
        P(("azim", "axial"), None, None),
        P(("azim", "axial"), None),
        P(("azim", "axial"), None),
        P(("azim", "axial"), None),
        P(("azim", "axial"), None),
    )
    out_specs = (P(None, "azim", "axial", None), P(("azim", "axial"), None, None))
    return jax.shard_map(
        on_device, mesh=mesh, in_specs=in_specs, out_specs=out_specs, check_vma=False
    )
```

time: 397 us -> 154 us (0.39)
  matrix products: 170 us -> 0 us
  local copies, waits for them, and re-layouts: 89.7 us -> 5.86 us
  Pallas kernels: 0 us -> 64.5 us
  other arithmetic: 55.3 us -> 4.55 us
  blocking collectives: 0 us -> 29.3 us
  starting transfers between devices: 41.1 us -> 22 us
  waiting for transfers between devices: 35.3 us -> 26.6 us
    dot_general x48 -> x0, matrix products: 170 us -> none  [the longest x16 78 us: interact(): picked = jnp.einsum('pc,frc->fpr', col_hot, fields, precision=highest)]
    pallas_call x0 -> x4, Pallas kernels: none -> 64.5 us  [the longest x2 30.2 us: scatter(): pl.pallas_call(kernel, out_shape=jax.ShapeDtypeStruct((tiles, fields, til...]
    scatter x4 -> x0, local copies, waits for them, and re-layouts: 56.2 us -> none  [the longest x1 47.5 us: on_device(): jnp.zeros((slot_count, 3, block_rows), jnp.float32).at[slot_index]]
    all_to_all x0 -> x2, blocking collectives: none -> 29.3 us  [exchange(): lax.all_to_all(value, 'azim', split_axis=0, concat_axis=0, tiled=True, ax...]
    all_to_all x5 -> x2, starting transfers between devices: 30.7 us -> 11.1 us  [exchange(): lax.all_to_all(value, 'azim', split_axis=0, concat_axis=0, tiled=True, ax...]
    mul x32 -> x0, other arithmetic: 18.6 us -> none  [the longest x16 16.5 us: interact(): TIME_STEP * drag_rate * flow_here]
    dynamic_slice x64 -> x0, local copies, waits for them, and re-layouts: 17.9 us -> none  [the longest x48 16.7 us: on_device(): lax.scan(deposit, jnp.zeros((rows_tile, radial), jnp.float32), (cell_turn...]
    add x16 -> x3, other arithmetic: 16.3 us -> 3.49 us  [the longest x2 2.91 us: summed(): got = exchange(parts[:near] + other)]
  transfers between devices with their start and end apart: 9 -> 10, of which waited for: 4 -> 5; matrix products, arithmetic and copies ran while one was open for 27% -> 2% of each run, Pallas kernels for 0% -> 22%
where the time goes in v1:
time: 154 us
  Pallas kernels  64.5 us (42%)
  blocking collectives  29.3 us (19%)
  waiting for transfers between devices  26.6 us (17%)
  starting transfers between devices  22 us (14%)
  local copies, waits for them, and re-layouts  5.86 us (4%)
  other arithmetic  4.55 us (3%)
    pallas_call x2, Pallas kernels, scatter(): pl.pallas_call(kernel, out_shape=jax.ShapeDtypeStruct((tiles, fields, til...  30.2 us
    all_to_all x2, blocking collectives, exchange(): lax.all_to_all(value, 'azim', split_axis=0, concat_axis=0, tiled=True, ax...  29.3 us
    pallas_call x1, Pallas kernels, on_device(): pl.pallas_call(flow_kernel, out_shape=per_particle, in_specs=[SMEM_SPEC,...  20.9 us
    pallas_call x1, Pallas kernels, on_device(): pl.pallas_call(particle_kernel, out_shape=(per_particle, per_particle), i...  13.4 us
    all_to_all x2, starting transfers between devices, exchange(): lax.all_to_all(value, 'azim', split_axis=0, concat_axis=0, tiled=True, ax...  11.1 us
    all_to_all x2, waiting for transfers between devices, exchange(): lax.all_to_all(value, 'azim', split_axis=0, concat_axis=0, tiled=True, ax...  10.7 us
    ppermute x2, waiting for transfers between devices, padded_2(): after = lax.ppermute(first, axis, down)  8.23 us
    ppermute x2, starting transfers between devices, padded_2(): after = lax.ppermute(first, axis, down)  5.84 us
  transfers between devices with their start and end apart: 10, of which 5 were waited for; matrix products, arithmetic and copies ran while one was open for 2% of the time, Pallas kernels for 22%

profile of v1, /device:TPU:0, one launch (start us, length us, event | category | flops | bytes accessed | tf_op | source)
XLA Modules:
  0.0 153.6 jit_solution(3635039496745535422)
XLA Ops:
  0.6 2.3 %broadcast_in_dim.10 = f32[16,3,64,128]{3,2,1,0:T(8,128)} broadcast(f32[3,64,128]{2,1,0:T(8,128)} %bitcast.20), dimensions={1,2,3} | broadcast | bytes 1671168 | tf_op jit(solution)/shard_map/broadcast_in_dim | solution.py:228
  2.9 0.0 copy-start.6
  2.9 7.2 %all-to-all-start.1 = ((f32[16,3,64,128]{3,2,1,0:T(8,128)}), f32[16,3,64,128]{3,2,1,0:T(8,128)S(1)}, u32[]{:S(2)}, u32[]{:S(2)}) async-start(f32[16,3,64,128]{3,2,1,0:T(8,128)} %broadcast_in_dim.10), calls=%async_computation.1 | async-start | bytes 3145728 | tf_op jit(solution)/shard_map/all_to_all | solution.py:218
  10.2 0.0 copy-done.6
  10.2 0.6 shift-right-arithmetic_add_fusion
  10.7 12.9 %shard_map.86 = f32[32,1,64,128]{3,2,1,0:T(8,128)} custom-call(s32[512]{0:T(512)} %bitcast.33, s32[512,128]{1,0:T(8,128)} %cell_ref.7, f32[512,128]{1,0:T(8,128)} %vol_ref.3), custom_call_target="tpu_custom_call" | custom-call | tf_op jit(solution)/shard_map/pallas_call | solution.py:89
  23.7 1.1 slice.133
  24.8 0.1 collective-permute-start
  24.9 9.0 %all-to-all-done.1.same_ref = f32[16,3,64,128]{3,2,1,0:T(8,128)S(1)} async-done(((f32[16,3,64,128]{3,2,1,0:T(8,128)}), f32[16,3,64,128]{3,2,1,0:T(8,128)S(1)}, u32[]{:S(2)}, u32[]{:S(2)}) %all-to-all-start.1) | async-done | bytes 1572896 | tf_op jit(solution)/shard_map/all_to_all | solution.py:218
  33.9 0.0 copy-start.1
  33.9 0.0 collective-permute-start.5
  33.9 0.0 collective-permute-done
  33.9 1.5 slice_add_fusion.1
  35.4 15.5 %all_to_all.20 = f32[16,1,64,128]{3,2,1,0:T(8,128)S(1)} all-to-all(f32[16,1,64,128]{3,2,1,0:T(8,128)S(1)} %slice_add_fusion.1), channel_id=1, replica_groups={{0,8,16,24,32,40,48,56,64,72,80,88,96,104,112,120},{4,12,20,28,36,44,52..., dimensions={0} | all-to-all | bytes 1048576 | tf_op jit(solution)/shard_map/all_to_all | solution.py:218
  50.9 0.0 copy-done.1
  51.0 13.9 %all_to_all.21.same_ref = f32[16,1,64,128]{3,2,1,0:T(8,128)S(1)} all-to-all(f32[16,1,64,128]{3,2,1,0:T(8,128)S(1)} %broadcast_in_dim.11), channel_id=1, replica_groups={{0,8,16,24,32,40,48,56,64,72,80,88,96,104,112,120},{4,12,20,28,36,44,52..., dimensions={0} | all-to-all | bytes 1048576 | tf_op jit(solution)/shard_map/all_to_all | solution.py:218
  64.8 0.0 copy-start.3
  64.8 0.0 collective-permute-start.6
  64.8 0.0 collective-permute-done.5.other_ref
  64.9 20.9 %shard_map.87.flow_ref = f32[3,512,128]{2,1,0:T(8,128)} custom-call(s32[512]{0:T(512)} %bitcast.34, s32[512,128]{1,0:T(8,128)} %cell_ref.7, f32[16,3,64,128]{3,2,1,0:T(8,128)} %copy-done.1, f32[16,3,64,128]{3,2,1,0:T(8,128)} %collective-permute-done.5.other_ref), custom_call_target="tpu_custom_call" | custom-call | tf_op jit(solution)/shard_map/pallas_call | solution.py:238
  85.8 0.0 copy-done.3
  85.8 0.0 collective-permute-done.6.other_ref
  85.8 0.0 copy-start.4
  85.8 0.8 copy-done.4
  86.6 13.4 %shard_map.88 = (f32[3,512,128]{2,1,0:T(8,128)}, f32[3,512,128]{2,1,0:T(8,128)}) custom-call(s32[512]{0:T(512)} %bitcast.35, s32[512,128]{1,0:T(8,128)} %cell_ref.7, f32[512,128]{1,0:T(8,128)} %vol_ref.3, f32[512,128]{1,0:T(8,128)} %drag_ref.1, f32[3,512,128]{2,1,0:T(8,128)} %bitcast.26, f32[3,512,128]{2,1,0:T(8,128)} %shard_map.87.flow_ref, ...), custom_call_target="tpu_custom_call" | custom-call | tf_op jit(solution)/shard_map/pallas_call | solution.py:249
  100.0 17.2 %shard_map.89 = f32[32,3,64,128]{3,2,1,0:T(8,128)} custom-call(s32[512]{0:T(512)} %bitcast.36, s32[512,128]{1,0:T(8,128)} %cell_ref.7, f32[3,512,128]{2,1,0:T(8,128)} %get-tuple-element.4.push_ref), custom_call_target="tpu_custom_call" | custom-call | tf_op jit(solution)/shard_map/pallas_call | solution.py:89
  117.2 0.0 copy-start
  117.2 1.7 %slice.139 = f32[16,3,64,128]{3,2,1,0:T(8,128)S(1)} slice(f32[32,3,64,128]{3,2,1,0:T(8,128)} %shard_map.89), slice={[16:32], [0:3], [0:64], [0:128]} | slice | bytes 3145728 | tf_op jit(solution)/shard_map/slice | solution.py:223
  118.9 0.4 collective-permute-start.7
  119.3 3.1 %collective-permute-done.7 = f32[16,3,64,128]{3,2,1,0:T(8,128)S(1)} collective-permute-done((f32[16,3,64,128]{3,2,1,0:T(8,128)S(1)}, f32[16,3,64,128]{3,2,1,0:T(8,128)S(1)}, u32[]{:S(2)}, u32[]{:S(2)}) %collective-permute-start.7) | collective-permute-done | bytes 1572896 | tf_op jit(solution)/shard_map/ppermute | solution.py:223
  122.4 0.0 copy-done
  122.4 1.4 slice_add_fusion
  123.8 0.0 copy-start.2
  123.8 0.0 copy-start.5
  123.8 3.8 %all-to-all-start.3 = ((f32[16,3,64,128]{3,2,1,0:T(8,128)}), f32[16,3,64,128]{3,2,1,0:T(8,128)S(1)}, u32[]{:S(2)}, u32[]{:S(2)}) async-start(f32[16,3,64,128]{3,2,1,0:T(8,128)} %slice_add_fusion), calls=%async_computation.3 | async-start | bytes 3145728 | tf_op jit(solution)/shard_map/all_to_all | solution.py:218
  127.7 0.0 copy-done.2
  127.7 0.0 copy-done.5
  127.7 1.3 collective-permute-start.3
  129.0 4.5 %collective-permute-start.4 = (f32[5,4,1,128]{3,2,1,0:T(1,128)S(1)}, f32[5,4,1,128]{3,2,1,0:T(1,128)S(1)}, u32[]{:S(2)}, u32[]{:S(2)}) collective-permute-start(f32[5,4,1,128]{3,2,1,0:T(1,128)S(1)} %get-tuple-element.18), channel_id=1, source_target_pairs={{0,1},{1,2},{2,3},{4,5},{5,6},{6,7},{8,9},{9,10},{10,11},{12,13},{... | collective-permute-start | bytes 30728 | tf_op jit(solution)/shard_map/ppermute | solution.py:199
  133.6 0.1 fusion.21
  133.7 4.5 %collective-permute-start.1 = (f32[5,1,16,128]{3,2,1,0:T(8,128)S(1)}, f32[5,1,16,128]{3,2,1,0:T(8,128)S(1)}, u32[]{:S(2)}, u32[]{:S(2)}) collective-permute-start(f32[5,1,16,128]{3,2,1,0:T(8,128)S(1)} %get-tuple-element.15), channel_id=1, source_target_pairs={{4,0},{8,4},{12,8},{16,12},{20,16},{24,20},{28,24},{32,28},{36,32}... | collective-permute-start | bytes 122888 | tf_op jit(solution)/shard_map/ppermute | solution.py:200
  138.3 0.0 collective-permute-start.2
  138.3 0.0 collective-permute-done.3
  138.3 0.0 collective-permute-done.4
  138.3 8.2 %collective-permute-done.1 = f32[5,1,16,128]{3,2,1,0:T(8,128)S(1)} collective-permute-done((f32[5,1,16,128]{3,2,1,0:T(8,128)S(1)}, f32[5,1,16,128]{3,2,1,0:T(8,128)S(1)}, u32[]{:S(2)}, u32[]{:S(2)}) %collective-permute-start.1) | collective-permute-done | bytes 40992 | tf_op jit(solution)/shard_map/ppermute | solution.py:200
  146.5 4.6 %collective-permute-done.2 = f32[5,1,16,128]{3,2,1,0:T(8,128)S(1)} collective-permute-done((f32[5,1,16,128]{3,2,1,0:T(8,128)S(1)}, f32[5,1,16,128]{3,2,1,0:T(8,128)S(1)}, u32[]{:S(2)}, u32[]{:S(2)}) %collective-permute-start.2) | collective-permute-done | bytes 40992 | tf_op jit(solution)/shard_map/ppermute | solution.py:199
  151.1 1.6 %all-to-all-done.3 = f32[16,3,64,128]{3,2,1,0:T(8,128)S(1)} async-done(((f32[16,3,64,128]{3,2,1,0:T(8,128)}), f32[16,3,64,128]{3,2,1,0:T(8,128)S(1)}, u32[]{:S(2)}, u32[]{:S(2)}) %all-to-all-start.3) | async-done | bytes 1572896 | tf_op jit(solution)/shard_map/all_to_all | solution.py:218
  152.8 0.1 reduce_sum.19
  152.9 0.8 fusion.9
  (8 shorter events, 0.2 us)
Async XLA Ops:
  2.9 7.3 %copy-start.6 = (s32[512,1]{0,1:T(1,128)S(1)}, s32[512,1]{0,1:T(1,128)}, u32[]{:S(2)}) copy-start(s32[512,1]{0,1:T(1,128)} %param.13) | copy-start | bytes 6148
  2.9 31.0 %all-to-all-start.1 = ((f32[16,3,64,128]{3,2,1,0:T(8,128)}), f32[16,3,64,128]{3,2,1,0:T(8,128)S(1)}, u32[]{:S(2)}, u32[]{:S(2)}) async-start(f32[16,3,64,128]{3,2,1,0:T(8,128)} %broadcast_in_dim.10), calls=%async_computation.1 | async-start | bytes 3145728 | tf_op jit(solution)/shard_map/all_to_all | solution.py:218
  24.8 9.2 %collective-permute-start = (f32[16,1,64,128]{3,2,1,0:T(8,128)S(1)}, f32[16,1,64,128]{3,2,1,0:T(8,128)S(1)}, u32[]{:S(2)}, u32[]{:S(2)}) collective-permute-start(f32[16,1,64,128]{3,2,1,0:T(8,128)S(1)} %slice.133), channel_id=1, source_target_pairs={{0,4},{4,0},{8,12},{12,8},{16,20},{20,16},{24,28},{28,24},{32,36},... | collective-permute-start | bytes 1572872 | tf_op jit(solution)/shard_map/ppermute | solution.py:223
  33.9 17.0 %copy-start.1 = (f32[16,3,64,128]{3,2,1,0:T(8,128)}, f32[16,3,64,128]{3,2,1,0:T(8,128)S(1)}, u32[]{:S(2)}) copy-start(f32[16,3,64,128]{3,2,1,0:T(8,128)S(1)} %all-to-all-done.1.same_ref) | copy-start | bytes 4718596
  33.9 30.9 %collective-permute-start.5 = (f32[16,3,64,128]{3,2,1,0:T(8,128)S(1)}, f32[16,3,64,128]{3,2,1,0:T(8,128)}, u32[]{:S(2)}, u32[]{:S(2)}) collective-permute-start(f32[16,3,64,128]{3,2,1,0:T(8,128)S(1)} %all-to-all-done.1.same_ref), channel_id=1, source_target_pairs={{0,4},{4,0},{8,12},{12,8},{16,20},{20,16},{24,28},{28,24},{32,36},... | collective-permute-start | bytes 4718600 | tf_op jit(solution)/shard_map/ppermute | solution.py:229
  64.8 20.9 %copy-start.3 = (f32[16,1,64,128]{3,2,1,0:T(8,128)}, f32[16,1,64,128]{3,2,1,0:T(8,128)S(1)}, u32[]{:S(2)}) copy-start(f32[16,1,64,128]{3,2,1,0:T(8,128)S(1)} %all_to_all.21.same_ref) | copy-start | bytes 1572868
  64.8 20.9 %collective-permute-start.6 = (f32[16,1,64,128]{3,2,1,0:T(8,128)S(1)}, f32[16,1,64,128]{3,2,1,0:T(8,128)S(1)}, u32[]{:S(2)}, u32[]{:S(2)}) collective-permute-start(f32[16,1,64,128]{3,2,1,0:T(8,128)S(1)} %all_to_all.21.same_ref), channel_id=1, source_target_pairs={{0,4},{4,0},{8,12},{12,8},{16,20},{20,16},{24,28},{28,24},{32,36},... | collective-permute-start | bytes 1572872 | tf_op jit(solution)/shard_map/ppermute | solution.py:229
  85.8 0.8 copy-start.4
  117.2 5.2 %copy-start = (f32[32,3,64,128]{3,2,1,0:T(8,128)S(1)}, f32[32,3,64,128]{3,2,1,0:T(8,128)}, u32[]{:S(2)}) copy-start(f32[32,3,64,128]{3,2,1,0:T(8,128)} %shard_map.89) | copy-start | bytes 9437188
  118.9 3.5 %collective-permute-start.7 = (f32[16,3,64,128]{3,2,1,0:T(8,128)S(1)}, f32[16,3,64,128]{3,2,1,0:T(8,128)S(1)}, u32[]{:S(2)}, u32[]{:S(2)}) collective-permute-start(f32[16,3,64,128]{3,2,1,0:T(8,128)S(1)} %slice.139), channel_id=1, source_target_pairs={{0,4},{4,0},{8,12},{12,8},{16,20},{20,16},{24,28},{28,24},{32,36},... | collective-permute-start | bytes 4718600 | tf_op jit(solution)/shard_map/ppermute | solution.py:223
  123.8 3.9 %copy-start.2 = (f32[3,4,16,128]{3,2,1,0:T(8,128)S(1)}, f32[3,4,16,128]{3,2,1,0:T(8,128)}, u32[]{:S(2)}) copy-start(f32[3,4,16,128]{3,2,1,0:T(8,128)} %param.7) | copy-start | bytes 294916
  123.8 3.9 %copy-start.5 = (f32[4,16,128]{2,1,0:T(8,128)S(1)}, f32[4,16,128]{2,1,0:T(8,128)}, u32[]{:S(2)}) copy-start(f32[4,16,128]{2,1,0:T(8,128)} %param.8) | copy-start | bytes 98308
  123.8 29.0 %all-to-all-start.3 = ((f32[16,3,64,128]{3,2,1,0:T(8,128)}), f32[16,3,64,128]{3,2,1,0:T(8,128)S(1)}, u32[]{:S(2)}, u32[]{:S(2)}) async-start(f32[16,3,64,128]{3,2,1,0:T(8,128)} %slice_add_fusion), calls=%async_computation.3 | async-start | bytes 3145728 | tf_op jit(solution)/shard_map/all_to_all | solution.py:218
  127.7 10.5 %collective-permute-start.3 = (f32[5,4,1,128]{3,2,1,0:T(1,128)S(1)}, f32[5,4,1,128]{3,2,1,0:T(1,128)S(1)}, u32[]{:S(2)}, u32[]{:S(2)}) collective-permute-start(f32[5,4,1,128]{3,2,1,0:T(1,128)S(1)} %get-tuple-element.17), channel_id=1, source_target_pairs={{1,0},{2,1},{3,2},{5,4},{6,5},{7,6},{9,8},{10,9},{11,10},{13,12},{... | collective-permute-start | bytes 30728 | tf_op jit(solution)/shard_map/ppermute | solution.py:200
  129.0 9.2 %collective-permute-start.4 = (f32[5,4,1,128]{3,2,1,0:T(1,128)S(1)}, f32[5,4,1,128]{3,2,1,0:T(1,128)S(1)}, u32[]{:S(2)}, u32[]{:S(2)}) collective-permute-start(f32[5,4,1,128]{3,2,1,0:T(1,128)S(1)} %get-tuple-element.18), channel_id=1, source_target_pairs={{0,1},{1,2},{2,3},{4,5},{5,6},{6,7},{8,9},{9,10},{10,11},{12,13},{... | collective-permute-start | bytes 30728 | tf_op jit(solution)/shard_map/ppermute | solution.py:199
  133.7 12.8 %collective-permute-start.1 = (f32[5,1,16,128]{3,2,1,0:T(8,128)S(1)}, f32[5,1,16,128]{3,2,1,0:T(8,128)S(1)}, u32[]{:S(2)}, u32[]{:S(2)}) collective-permute-start(f32[5,1,16,128]{3,2,1,0:T(8,128)S(1)} %get-tuple-element.15), channel_id=1, source_target_pairs={{4,0},{8,4},{12,8},{16,12},{20,16},{24,20},{28,24},{32,28},{36,32}... | collective-permute-start | bytes 122888 | tf_op jit(solution)/shard_map/ppermute | solution.py:200
  138.3 12.9 %collective-permute-start.2 = (f32[5,1,16,128]{3,2,1,0:T(8,128)S(1)}, f32[5,1,16,128]{3,2,1,0:T(8,128)S(1)}, u32[]{:S(2)}, u32[]{:S(2)}) collective-permute-start(f32[5,1,16,128]{3,2,1,0:T(8,128)S(1)} %get-tuple-element.16), channel_id=1, source_target_pairs={{0,4},{4,8},{8,12},{12,16},{16,20},{20,24},{24,28},{28,32},{32,36}... | collective-permute-start | bytes 122888 | tf_op jit(solution)/shard_map/ppermute | solution.py:199

commit v2 on v1

v2 whole, which is shorter than its diff:
```python
import functools

import jax
import jax.numpy as jnp
from jax import lax
from jax.experimental import pallas as pl
from jax.experimental.pallas import tpu as pltpu
from jax.sharding import PartitionSpec as P

TIME_STEP = 0.25
VISCOSITY = 0.5
BF, F32, I32, I16 = jnp.bfloat16, jnp.float32, jnp.int32, jnp.int16
LANES = 128
HALF = 32
CHUNKS = 4
SIDE = 4
SMEM_SPEC = pl.BlockSpec(memory_space=pltpu.SMEM)
VMEM_SPEC = pl.BlockSpec(memory_space=pltpu.VMEM)
ANY_SPEC = pl.BlockSpec(memory_space=pl.ANY)
PARAMS = pltpu.CompilerParams(vmem_limit_bytes=60 * 2**20)


def cost(micros):
    return pl.CostEstimate(flops=0, transcendentals=0, bytes_accessed=int(micros * 3_000_000))


def row(ref, b):
    return ref[pl.ds(b, 1), :]


def two_parts(value):
    high = value.astype(BF)
    return high, (value - high.astype(F32)).astype(BF)


def columns_of(cell):
    return (cell & 127) | ((cell >> 12) << 7)


def ramps():
    lane = lax.broadcasted_iota(I32, (LANES, LANES), 1)
    lanes = [(lane + k * LANES).astype(I16) for k in range(2)]
    rows = lax.broadcasted_iota(I32, (HALF, LANES), 0).astype(F32).astype(BF)
    return lanes, rows


def weighted_rows(cell, values, rows):
    in_half = jnp.where(cell < 0, -1, (cell >> 7) & (HALF - 1)).astype(F32).astype(BF)
    mask = rows == jnp.broadcast_to(in_half, (HALF, LANES))
    zero = jnp.zeros((), BF)
    parts = []
    for value in values:
        for part in two_parts(value):
            parts.append(jnp.where(mask, jnp.broadcast_to(part, (HALF, LANES)), zero))
    return jnp.concatenate(parts, axis=0)


def hot_columns(words, j, lanes):
    one, zero = jnp.ones((), BF), jnp.zeros((), BF)
    word = jnp.broadcast_to(words[:, j : j + 1], (LANES, LANES)).astype(I16)
    both = (word & 255, lax.shift_right_logical(word, jnp.int16(8)))
    return [
        jnp.concatenate([jnp.where(k == ids, one, zero) for k in lanes], axis=1) for ids in both
    ]


def add_to(sum_ref, d, res, fields):
    for f in range(fields):
        at = 2 * f * HALF
        both = res[at : at + HALF] + res[at + HALF : at + 2 * HALF]
        sum_ref[d, f, 0:HALF, :] += both[:, :LANES]
        sum_ref[d, f, HALF : 2 * HALF, :] += both[:, LANES:]


def start_all(pairs, sems):
    copies = [pltpu.make_async_copy(a, b, sems.at[i]) for i, (a, b) in enumerate(pairs)]
    for copy in copies:
        copy.start()
    return copies


def wait_all(copies):
    for copy in copies:
        copy.wait()


def halves(ref):
    near = ref.shape[0] // 2
    return ref.at[pl.ds(0, near)], ref.at[pl.ds(near, near)]


def deposit_kernel(
    slot_ref, cell_ref, vol_ref, tile_ref, same_ref, other_ref, late_ref, sum_ref, words_ref, sems
):
    late_ref[...] = tile_ref[...]
    sum_ref[...] = jnp.zeros_like(sum_ref)
    blocks = cell_ref.shape[0]
    for g in range(blocks // 256):
        a = columns_of(cell_ref[g * 256 : g * 256 + 128, :])
        b = columns_of(cell_ref[g * 256 + 128 : g * 256 + 256, :])
        words_ref[g] = (a | (b << 8)).astype(F32).T.astype(I32)
    lanes, rows = ramps()
    unroll = 8

    def step(g, carry):
        for i in range(LANES // unroll):
            got = []
            for u in range(unroll):
                j = i * unroll + u
                hots = hot_columns(words_ref[g], j, lanes)
                for s in range(2):
                    b = g * 256 + s * 128 + j
                    left = weighted_rows(row(cell_ref, b), [row(vol_ref, b)], rows)
                    got.append((b, jnp.dot(left, hots[s], preferred_element_type=F32)))
            for b, res in got:
                add_to(sum_ref, slot_ref[b], res, 1)
        return carry

    lax.fori_loop(0, blocks // 256, step, 0)
    low, high = halves(sum_ref)
    out = [
        pltpu.make_async_copy(high, other_ref, sems.at[0]),
        pltpu.make_async_copy(low, same_ref, sems.at[1]),
    ]
    for copy in out:
        copy.start()
    wait_all(out)


def join_kernel(same_ref, other_ref, *refs):
    tile_refs, (parts_ref, tiles_ref) = refs[:-2], refs[-2:]
    for i, ref in enumerate(tile_refs):
        tiles_ref[pl.ds(i, 1)] = ref[...]
    parts_ref[...] = same_ref[...] + other_ref[...]


def owner_kernel(got_ref, *refs):
    total_ref, tiles_ref = refs[-2:]
    total = jnp.sum(got_ref[...], axis=0)
    total_ref[...] = total
    tiles_ref[...] = jnp.broadcast_to(total[None], tiles_ref.shape)


def order_of(slot, tiles):
    count = slot.shape[0]
    ids = jnp.arange(count, dtype=I32)
    names = jnp.arange(tiles, dtype=I32)
    held = jnp.sum((slot[:, None] == names[None]).astype(I32), axis=0)
    odd = held & 1
    same = (slot[None, :] == slot[:, None]) & (ids[None, :] < ids[:, None])
    before = (slot[None, :] < slot[:, None]) | same
    place = jnp.sum(before.astype(I32), axis=1) + jnp.sum(
        jnp.where(names[None] < slot[:, None], odd[None], 0), axis=1
    )
    places = jnp.arange(count + tiles, dtype=I32)
    block = (
        jnp.sum(jnp.where(place[None, :] == places[:, None], ids[None, :] + 1, 0), axis=1) - 1
    )
    ends = jnp.sum(jnp.where(names[:, None] >= names[None], (held + odd)[None], 0), axis=1)
    firsts = 2 * jnp.arange((count + tiles) // 2, dtype=I32)
    pair = jnp.sum((ends[None, :] <= firsts[:, None]).astype(I32), axis=1)
    return block, jnp.minimum(pair, tiles - 1)


def words_kernel(block_ref, cell_ref, words_ref, sorted_ref):
    per = block_ref.shape[0] // 2 // CHUNKS
    full = per // 8 * 8
    for c in range(CHUNKS):
        sorted_ref[c * LANES + full : (c + 1) * LANES, :] = jnp.zeros((LANES - full, LANES), F32)

        def move(i, carry):
            for u in range(4):
                j = i * 4 + u
                first = row(cell_ref, jnp.maximum(block_ref[2 * (c * per + j)], 0))
                second = row(cell_ref, jnp.maximum(block_ref[2 * (c * per + j) + 1], 0))
                word = columns_of(first) | (columns_of(second) << 8)
                sorted_ref[pl.ds(c * LANES + j, 1), :] = word.astype(F32)
            return carry

        lax.fori_loop(0, per // 4, move, 0)
        words_ref[c] = sorted_ref[c * LANES : (c + 1) * LANES, :].T.astype(I32)


def fold_8(values):
    sub = lax.broadcasted_iota(I32, (8, LANES), 0)
    for width in (4, 2, 1):
        keep = (sub & width) == 0
        count = len(values) // 2
        folded = []
        for i in range(count):
            a, b = values[i], values[i + count]
            kept, moved = jnp.where(keep, a, b), jnp.where(keep, b, a)
            if width == 4:
                folded.append(kept + pltpu.roll(moved, 4, 0))
            else:
                up, down = pltpu.roll(moved, 8 - width, 0), pltpu.roll(moved, width, 0)
                folded.append(kept + jnp.where(keep, up, down))
        values = folded
    return values[0]


def pick_rows(slot_ref, cell_ref, table_ref, fields, out_ref, groups):
    blocks = cell_ref.shape[0]
    sub = lax.broadcasted_iota(I32, (8, LANES), 0)

    def eight(base):
        picked = [[] for _ in range(fields)]
        for s in range(8):
            d = slot_ref[base + s]
            cell = jnp.broadcast_to(row(cell_ref, base + s), (8, LANES))
            column, top, low = cell & 127, cell >> 10, (cell >> 7) & 7
            for f in range(fields):
                acc = None
                for q in range(table_ref.shape[2] // 8):
                    got = jnp.take_along_axis(
                        table_ref[d, f, 8 * q : 8 * q + 8, :],
                        column,
                        axis=1,
                        mode="promise_in_bounds",
                    )
                    acc = got if acc is None else jnp.where(top == q, got, acc)
                picked[f].append(jnp.where(sub == low, acc, 0.0))
        for f in range(fields):
            out_ref[f, pl.ds(pl.multiple_of(base, 8), 8), :] = fold_8(picked[f])

    def step(i, carry):
        for u in range(groups):
            eight((i * groups + u) * 8)
        return carry

    lax.fori_loop(0, blocks // (8 * groups), step, 0)


def flow_kernel(slot_ref, cell_ref, *refs):
    group_refs, (_, out_ref, table_ref, sems) = refs[:-4], refs[-4:]
    size = group_refs[0].shape[0]
    wait_all(
        start_all(
            [(ref, table_ref.at[pl.ds(i * size, size)]) for i, ref in enumerate(group_refs)], sems
        )
    )
    pick_rows(slot_ref, cell_ref, table_ref, out_ref.shape[0], out_ref, 4)


def particle_kernel(
    dest_ref, block_ref, pair_ref, cell_ref, words_ref, vol_any, drag_any, vel_any, here_any,
    solid_any, tile_any,
    new_any, same_any, other_any, late_any,
    table_ref, solid_ref, vol_ref, drag_ref, vel_ref, here_ref, new_ref, push_ref, sum_ref, sems,
):
    tables = start_all([(solid_any, table_ref)], sems)
    rest = [
        (vol_any, vol_ref),
        (drag_any, drag_ref),
        (vel_any, vel_ref),
        (here_any, here_ref),
        (tile_any, late_any),
    ]
    others = [pltpu.make_async_copy(a, b, sems.at[1 + i]) for i, (a, b) in enumerate(rest)]
    for copy in others:
        copy.start()
    sum_ref[...] = jnp.zeros_like(sum_ref)
    wait_all(tables)
    pick_rows(dest_ref, cell_ref, table_ref, 1, solid_ref, 4)
    wait_all(others)
    blocks = cell_ref.shape[0]
    size = 32

    def react(i, carry):
        at = pl.ds(pl.multiple_of(i * size, size), size)
        rate = drag_ref[at, :] * (1.0 + solid_ref[0, at, :])
        weight = vol_ref[at, :] * rate
        scaled = TIME_STEP * rate
        below = 1.0 / (1.0 + scaled)
        for f in range(3):
            here = here_ref[f, at, :]
            new = (vel_ref[f, at, :] + scaled * here) * below
            new_ref[f, at, :] = new
            push_ref[f, at, :] = weight * (new - here)
        return carry

    lax.fori_loop(0, blocks // size, react, 0, unroll=2)
    leave = pltpu.make_async_copy(new_ref, new_any, sems.at[6])
    leave.start()
    lanes, rows = ramps()
    per = block_ref.shape[0] // 2 // CHUNKS
    unroll = 4

    def side(place):
        b = block_ref[place]
        at = jnp.maximum(b, 0)
        cell = jnp.where(b < 0, -1, row(cell_ref, at))
        return weighted_rows(cell, [push_ref[f, pl.ds(at, 1), :] for f in range(3)], rows)

    def step(c, carry):
        for i in range(per // unroll):
            got = []
            for u in range(unroll):
                j = i * unroll + u
                p = c * per + j
                left = jnp.concatenate([side(2 * p), side(2 * p + 1)], axis=1)
                right = jnp.concatenate(hot_columns(words_ref[c], j, lanes), axis=0)
                got.append((p, jnp.dot(left, right, preferred_element_type=F32)))
            for p, res in got:
                add_to(sum_ref, pair_ref[p], res, 3)
        return carry

    lax.fori_loop(0, CHUNKS, step, 0)
    low, high = halves(sum_ref)
    out = [
        pltpu.make_async_copy(high, other_any, sems.at[7]),
        pltpu.make_async_copy(low, same_any, sems.at[8]),
    ]
    for copy in out:
        copy.start()
    leave.wait()
    wait_all(out)


def combine(stacked, solid, source, neighbours):
    padded = jnp.pad(stacked, ((0, 0), (0, 0), (0, 0), (1, 1)))
    every = neighbours + [padded[..., 2:], padded[..., :-2]]
    voidage = stacked[0]
    flow = stacked[2:]
    spread = jnp.zeros_like(flow)
    for other in every:
        spread = spread + 0.5 * (voidage + other[0]) * (other[2:] - flow)
    slope = 0.5 * jnp.stack(
        [every[0][1] - every[1][1], every[2][1] - every[3][1], every[4][1] - every[5][1]]
    )
    return flow + TIME_STEP * ((1.0 + solid) * (VISCOSITY * spread + source) - slope)


def padded_2(value, sides, width, wrap):
    for axis, dim in sides:
        size, length = (lax.axis_size(axis), value.shape[dim])
        up = [(i, (i + 1) % size) for i in range(size if wrap else size - 1)]
        down = [(j, i) for i, j in up]
        last = lax.slice_in_dim(value, length - width, length, axis=dim)
        first = lax.slice_in_dim(value, 0, width, axis=dim)
        before = lax.ppermute(last, axis, up)
        after = lax.ppermute(first, axis, down)
        value = jnp.concatenate([before, value, after], axis=dim)
    return value


def along(stage, step):
    moves = []
    for i in range(2 * SIDE * SIDE):
        x, y, core = i // (2 * SIDE), (i // 2) % SIDE, i % 2
        if core == stage:
            y = (y + step) % SIDE
        else:
            x = (x + step) % SIDE
        moves.append((i, (x * SIDE + y) * 2 + core))
    return moves


def place_of(dest, me):
    x = (me // (2 * SIDE) - dest // (2 * SIDE)) % SIDE
    y = (me // 2 - dest // 2) % SIDE
    core = dest & 1
    first, second = jnp.where(core == 0, y, x), jnp.where(core == 0, x, y)
    return (core ^ (me & 1)) * SIDE * SIDE + second * SIDE + first


def on_device(fluid_vel, pressure, part_vel, part_vol, part_drag, cell_of, dest_of):
    size = lax.axis_size("azim")
    near = size // 2
    blocks, block_rows = part_vol.shape
    tile_azim, tile_axial, radial = pressure.shape
    tile_rows = tile_azim * tile_axial
    core = lax.axis_index("azim") % 2
    chips = [[2 * i + c for i in range(near)] for c in range(2)]
    twin = [(i, i ^ 1) for i in range(size)]
    dest = dest_of[:, 0]
    slot = ((dest & 1) ^ core) * near + (dest >> 1)
    arrays = lambda *shape: jax.ShapeDtypeStruct(shape, F32)
    dma = lambda count: pltpu.SemaphoreType.DMA((count,))

    def to_owners(parts):
        return lax.all_to_all(
            parts, "azim", split_axis=0, concat_axis=0, tiled=True, axis_index_groups=chips
        )

    one_sum = arrays(near, 1, tile_rows, radial)
    dep_same, dep_other, flow_tile = pl.pallas_call(
        deposit_kernel,
        out_shape=(one_sum, one_sum, arrays(1, 3, tile_rows, radial)),
        in_specs=[SMEM_SPEC] + [VMEM_SPEC] * 3,
        out_specs=(ANY_SPEC, ANY_SPEC, VMEM_SPEC),
        scratch_shapes=[
            pltpu.VMEM((size, 1, tile_rows, radial), F32),
            pltpu.VMEM((blocks // 256, LANES, LANES), I32),
            dma(2),
        ],
        compiler_params=PARAMS,
        cost_estimate=cost(7),
    )(slot, cell_of, part_vol, fluid_vel.reshape(1, 3, tile_rows, radial))

    steps = range(1, SIDE)
    dep_twin = lax.ppermute(dep_other, "azim", twin)
    tiles = [flow_tile] + [lax.ppermute(flow_tile, "azim", along(0, k)) for k in steps]
    dep_parts, first = pl.pallas_call(
        join_kernel,
        out_shape=(one_sum, arrays(SIDE, 3, tile_rows, radial)),
        in_specs=[VMEM_SPEC] * (2 + SIDE),
        out_specs=(VMEM_SPEC, VMEM_SPEC),
        compiler_params=PARAMS,
        cost_estimate=cost(2),
    )(dep_same, dep_twin, *tiles)
    groups = [first] + [lax.ppermute(first, "azim", along(1, k)) for k in steps]
    solid_flat, solid_tiles = pl.pallas_call(
        owner_kernel,
        out_shape=(arrays(1, tile_rows, radial), arrays(size, 1, tile_rows, radial)),
        in_specs=[VMEM_SPEC] + [ANY_SPEC] * (SIDE - 1),
        out_specs=(VMEM_SPEC, VMEM_SPEC),
        compiler_params=PARAMS,
        cost_estimate=cost(2),
    )(to_owners(dep_parts), *groups[1:])
    groups += [lax.ppermute(group, "azim", twin) for group in groups]
    solid_tiles = lax.all_to_all(solid_tiles, "azim", split_axis=0, concat_axis=0, tiled=True)

    block, pair = order_of(slot, size)
    words = pl.pallas_call(
        words_kernel,
        out_shape=jax.ShapeDtypeStruct((CHUNKS, LANES, LANES), I32),
        in_specs=[SMEM_SPEC, VMEM_SPEC],
        out_specs=VMEM_SPEC,
        scratch_shapes=[pltpu.VMEM((CHUNKS * LANES, LANES), F32)],
        compiler_params=PARAMS,
        cost_estimate=cost(2),
    )(block, cell_of)

    here = pl.pallas_call(
        flow_kernel,
        out_shape=arrays(3, blocks, block_rows),
        in_specs=[SMEM_SPEC, VMEM_SPEC] + [ANY_SPEC] * (2 * SIDE + 1),
        out_specs=VMEM_SPEC,
        scratch_shapes=[pltpu.VMEM((size, 3, tile_rows, radial), F32), dma(2 * SIDE)],
        compiler_params=PARAMS,
        cost_estimate=cost(18),
    )(place_of(dest, lax.axis_index("azim")), cell_of, *groups, solid_flat)
    three = (3, blocks, block_rows)
    three_sums = arrays(near, 3, tile_rows, radial)
    new_vel, src_same, src_other, solid_late = pl.pallas_call(
        particle_kernel,
        out_shape=(arrays(*three), three_sums, three_sums, arrays(1, tile_rows, radial)),
        in_specs=[SMEM_SPEC] * 3 + [VMEM_SPEC] * 2 + [ANY_SPEC] * 6,
        out_specs=(ANY_SPEC,) * 4,
        scratch_shapes=[
            pltpu.VMEM((size, 1, tile_rows, radial), F32),
            pltpu.VMEM((1, blocks, block_rows), F32),
            pltpu.VMEM((blocks, block_rows), F32),
            pltpu.VMEM((blocks, block_rows), F32),
            pltpu.VMEM(three, F32),
            pltpu.VMEM(three, F32),
            pltpu.VMEM(three, F32),
            pltpu.VMEM(three, F32),
            pltpu.VMEM((size, 3, tile_rows, radial), F32),
            dma(9),
        ],
        compiler_params=PARAMS,
        cost_estimate=cost(20),
    )(
        dest, block, pair, cell_of, words, part_vol, part_drag,
        jnp.transpose(part_vel, (1, 0, 2)), here, solid_tiles, solid_flat,
    )
    source_flat = jnp.sum(to_owners(src_same + lax.ppermute(src_other, "azim", twin)), axis=0)
    part_out = jnp.transpose(new_vel, (1, 0, 2))
    solid = solid_late.reshape(tile_azim, tile_axial, radial)
    source = source_flat.reshape(3, tile_azim, tile_axial, radial)
    voidage = 1.0 / (1.0 + solid)
    stacked = jnp.concatenate([voidage[None], pressure[None], fluid_vel], 0)
    cycle_fields = padded_2(stacked, (("azim", 1),), 1, True)
    axial_fields = padded_2(stacked, (("axial", 2),), 1, False)
    neighbours = [
        cycle_fields[:, 2:],
        cycle_fields[:, :-2],
        axial_fields[:, :, 2:],
        axial_fields[:, :, :-2],
    ]
    fluid_out = combine(stacked, solid, source, neighbours)
    return (fluid_out, part_out)


def solution(mesh):
    in_specs = (
        P(None, "azim", "axial", None),
        P("azim", "axial", None),
        P(("azim", "axial"), None, None),
        P(("azim", "axial"), None),
        P(("azim", "axial"), None),
        P(("azim", "axial"), None),
        P(("azim", "axial"), None),
    )
    out_specs = (P(None, "azim", "axial", None), P(("azim", "axial"), None, None))
    return jax.shard_map(
        on_device, mesh=mesh, in_specs=in_specs, out_specs=out_specs, check_vma=False
    )
```

time: 154 us -> 144 us (0.935)
  blocking collectives: 29.3 us -> 0 us
  starting transfers between devices: 22 us -> 42.7 us
  Pallas kernels: 64.5 us -> 56.4 us
  waiting for transfers between devices: 26.6 us -> 30.3 us
  other arithmetic: 4.55 us -> 7.97 us
    all_to_all x2 -> x0, blocking collectives: 29.3 us -> none  [exchange(): lax.all_to_all(value, 'azim', split_axis=0, concat_axis=0, tiled=True, ax...]
    ppermute x4 -> x12, waiting for transfers between devices: 3.1 us -> 16.3 us  [the longest x3 10.1 us: on_device(): groups = [first] + [lax.ppermute(first, 'azim', along(1, k)) for k in steps]]
    ppermute x4 -> x12, starting transfers between devices: 0.48 us -> 13.6 us  [the longest x3 6.13 us: on_device(): groups = [first] + [lax.ppermute(first, 'azim', along(1, k)) for k in steps]]
    all_to_all x2 -> x3, waiting for transfers between devices: 10.7 us -> 1.79 us  [the longest x2 1.79 us: to_owners(): lax.all_to_all(parts, 'azim', split_axis=0, concat_axis=0, tiled=True, ax...]
    ppermute x2, waiting for transfers between devices: 8.23 us -> 0.01 us  [padded_2(): after = lax.ppermute(first, axis, down)]
    pallas_call x4 -> x6, Pallas kernels: 64.5 us -> 56.4 us  [the longest x1 20.6 us: on_device(): pl.pallas_call(particle_kernel, out_shape=(arrays(*three), three_sums, th...]
    all_to_all x2 -> x3, starting transfers between devices: 11.1 us -> 18.9 us  [the longest x2 13.6 us: to_owners(): lax.all_to_all(parts, 'azim', split_axis=0, concat_axis=0, tiled=True, ax...]
    ppermute x2, waiting for transfers between devices: 4.59 us -> 12.3 us  [padded_2(): before = lax.ppermute(last, axis, up)]
  transfers between devices with their start and end apart: 10 -> 19, of which waited for: 5 -> 7; matrix products, arithmetic and copies ran while one was open for 2% -> 2% of each run, Pallas kernels for 22% -> 16%
where the time goes in v2:
time: 144 us; the launch traced here: 143 us
  Pallas kernels  56.4 us (39%)
  starting transfers between devices  42.7 us (30%)
  waiting for transfers between devices  30.3 us (21%)
  other arithmetic  7.97 us (6%)
  local copies, waits for them, and re-layouts  4.47 us (3%)
    pallas_call x1, Pallas kernels, on_device(): pl.pallas_call(particle_kernel, out_shape=(arrays(*three), three_sums, th...  20.6 us
    pallas_call x1, Pallas kernels, on_device(): pl.pallas_call(flow_kernel, out_shape=arrays(3, blocks, block_rows), in_s...  19.8 us
    all_to_all x2, starting transfers between devices, to_owners(): lax.all_to_all(parts, 'azim', split_axis=0, concat_axis=0, tiled=True, ax...  13.6 us
    ppermute x2, waiting for transfers between devices, padded_2(): before = lax.ppermute(last, axis, up)  12.3 us
    ppermute x3, waiting for transfers between devices, on_device(): groups = [first] + [lax.ppermute(first, 'azim', along(1, k)) for k in steps]  10.1 us
    pallas_call x1, Pallas kernels, on_device(): pl.pallas_call(deposit_kernel, out_shape=(one_sum, one_sum, arrays(1, 3,...  8.17 us
    ppermute x2, starting transfers between devices, padded_2(): after = lax.ppermute(first, axis, down)  6.34 us
    ppermute x3, starting transfers between devices, on_device(): groups = [first] + [lax.ppermute(first, 'azim', along(1, k)) for k in steps]  6.13 us
  transfers between devices with their start and end apart: 19, of which 7 were waited for; matrix products, arithmetic and copies ran while one was open for 2% of the time, Pallas kernels for 16%

profile of v2, /device:TPU:0, one launch (start us, length us, event | category | flops | bytes accessed | tf_op | source)
XLA Modules:
  0.0 142.9 jit_solution(11498434350874201544)
XLA Ops:
  0.7 1.3 select_add_fusion
  2.0 8.2 %shard_map.87 = (f32[16,1,64,128]{3,2,1,0:T(8,128)}, f32[16,1,64,128]{3,2,1,0:T(8,128)}, f32[1,3,64,128]{3,2,1,0:T(8,128)}) custom-call(s32[512]{0:T(512)} %get-tuple-element.40.slot_ref, s32[512,128]{1,0:T(8,128)} %cell_ref.7, f32[512,128]{1,0:T(8,128)} %vol_any.1, f32[1,3,64,128]{3,2,1,0:T(8,128)} %bitcast.21), custom_call_target="tpu_custom_call" | custom-call | bytes 21000000 | tf_op jit(solution)/shard_map/pallas_call | solution.py:387
  10.1 0.1 collective-permute-start
  10.2 1.7 %collective-permute-start.1 = (f32[1,3,64,128]{3,2,1,0:T(8,128)}, f32[1,3,64,128]{3,2,1,0:T(8,128)S(1)}, u32[]{:S(2)}, u32[]{:S(2)}) collective-permute-start(f32[1,3,64,128]{3,2,1,0:T(8,128)} %get-tuple-element.15.refs_0_), channel_id=1, source_target_pairs={{0,8},{4,36},{8,16},{12,44},{16,24},{20,52},{24,0},{28,60},{32,40}... | collective-permute-start | bytes 294920 | tf_op jit(solution)/shard_map/ppermute | solution.py:403
  12.0 2.9 %collective-permute-start.2 = (f32[1,3,64,128]{3,2,1,0:T(8,128)}, f32[1,3,64,128]{3,2,1,0:T(8,128)S(1)}, u32[]{:S(2)}, u32[]{:S(2)}) collective-permute-start(f32[1,3,64,128]{3,2,1,0:T(8,128)} %get-tuple-element.15.refs_0_), channel_id=1, source_target_pairs={{0,16},{4,68},{8,24},{12,76},{16,0},{20,84},{24,8},{28,92},{32,48}... | collective-permute-start | bytes 294920 | tf_op jit(solution)/shard_map/ppermute | solution.py:403
  14.9 1.3 collective-permute-start.3
  16.2 0.7 shift-right-arithmetic_add_fusion
  16.9 0.0 collective-permute-done.1.refs_1_
  16.9 1.8 %collective-permute-done.2.refs_2_ = f32[1,3,64,128]{3,2,1,0:T(8,128)S(1)} collective-permute-done((f32[1,3,64,128]{3,2,1,0:T(8,128)}, f32[1,3,64,128]{3,2,1,0:T(8,128)S(1)}, u32[]{:S(2)}, u32[]{:S(2)}) %collective-permute-start.2) | collective-permute-done | bytes 98336 | tf_op jit(solution)/shard_map/ppermute | solution.py:403
  18.7 1.0 collective-permute-done.3.refs_3_
  19.7 0.0 collective-permute-done.other_ref
  19.7 0.6 copy-done.17
  20.3 0.2 copy-done.9
  20.5 2.2 %shard_map.88 = (f32[16,1,64,128]{3,2,1,0:T(8,128)}, f32[4,3,64,128]{3,2,1,0:T(8,128)}) custom-call(f32[16,1,64,128]{3,2,1,0:T(8,128)} %get-tuple-element.13.same_ref, f32[16,1,64,128]{3,2,1,0:T(8,128)} %copy-done.9, f32[1,3,64,128]{3,2,1,0:T(8,128)} %get-tuple-element.15.refs_0_, f32[1,3,64,128]{3,2,1,0:T(8,128)} %copy-done.15, ...), custom_call_target="tpu_custom_call" | custom-call | bytes 6000000 | tf_op jit(solution)/shard_map/pallas_call | solution.py:404
  22.8 6.4 %all-to-all-start = ((f32[16,1,64,128]{3,2,1,0:T(8,128)}), f32[16,1,64,128]{3,2,1,0:T(8,128)S(1)}, u32[]{:S(2)}, u32[]{:S(2)}) async-start(f32[16,1,64,128]{3,2,1,0:T(8,128)} %get-tuple-element.17), calls=%async_computation | async-start | bytes 1048576 | tf_op jit(solution)/shard_map/all_to_all | solution.py:382
  29.2 0.1 convert_reduce_fusion.1
  29.3 2.0 %collective-permute-start.4 = (f32[4,3,64,128]{3,2,1,0:T(8,128)}, f32[4,3,64,128]{3,2,1,0:T(8,128)S(1)}, u32[]{:S(2)}, u32[]{:S(2)}) collective-permute-start(f32[4,3,64,128]{3,2,1,0:T(8,128)} %get-tuple-element.16.refs_0_), channel_id=1, source_target_pairs={{0,32},{4,12},{8,40},{12,20},{16,48},{20,28},{24,56},{28,4},{32,64... | collective-permute-start | bytes 1179656 | tf_op jit(solution)/shard_map/ppermute | solution.py:412
  31.3 2.7 %collective-permute-start.5 = (f32[4,3,64,128]{3,2,1,0:T(8,128)}, f32[4,3,64,128]{3,2,1,0:T(8,128)S(1)}, u32[]{:S(2)}, u32[]{:S(2)}) collective-permute-start(f32[4,3,64,128]{3,2,1,0:T(8,128)} %get-tuple-element.16.refs_0_), channel_id=1, source_target_pairs={{0,64},{4,20},{8,72},{12,28},{16,80},{20,4},{24,88},{28,12},{32,96... | collective-permute-start | bytes 1179656 | tf_op jit(solution)/shard_map/ppermute | solution.py:412
  34.0 1.5 %collective-permute-start.6 = (f32[4,3,64,128]{3,2,1,0:T(8,128)}, f32[4,3,64,128]{3,2,1,0:T(8,128)S(1)}, u32[]{:S(2)}, u32[]{:S(2)}) collective-permute-start(f32[4,3,64,128]{3,2,1,0:T(8,128)} %get-tuple-element.16.refs_0_), channel_id=1, source_target_pairs={{0,96},{4,28},{8,104},{12,4},{16,112},{20,12},{24,120},{28,20},{32... | collective-permute-start | bytes 1179656 | tf_op jit(solution)/shard_map/ppermute | solution.py:412
  35.4 0.1 select_reduce_fusion.1
  35.5 0.3 convert_reduce_fusion
  35.9 5.9 %collective-permute-done.4.refs_0_.refs_1_ = f32[4,3,64,128]{3,2,1,0:T(8,128)S(1)} collective-permute-done((f32[4,3,64,128]{3,2,1,0:T(8,128)}, f32[4,3,64,128]{3,2,1,0:T(8,128)S(1)}, u32[]{:S(2)}, u32[]{:S(2)}) %collective-permute-start.4) | collective-permute-done | bytes 393248 | tf_op jit(solution)/shard_map/ppermute | solution.py:412
  41.8 4.2 %collective-permute-done.5.refs_1_.refs_2_ = f32[4,3,64,128]{3,2,1,0:T(8,128)S(1)} collective-permute-done((f32[4,3,64,128]{3,2,1,0:T(8,128)}, f32[4,3,64,128]{3,2,1,0:T(8,128)S(1)}, u32[]{:S(2)}, u32[]{:S(2)}) %collective-permute-start.5) | collective-permute-done | bytes 393248 | tf_op jit(solution)/shard_map/ppermute | solution.py:412
  46.0 0.0 all-to-all-done.got_ref
  46.0 0.7 copy-done.5
  46.7 0.1 copy-done.7
  46.9 0.8 copy-done.2
  47.7 2.2 %shard_map.89 = (f32[1,64,128]{2,1,0:T(8,128)}, f32[32,1,64,128]{3,2,1,0:T(8,128)}) custom-call(f32[16,1,64,128]{3,2,1,0:T(8,128)} %copy-done.2, f32[4,3,64,128]{3,2,1,0:T(8,128)} %copy-done.3, f32[4,3,64,128]{3,2,1,0:T(8,128)} %copy-done.5, f32[4,3,64,128]{3,2,1,0:T(8,128)} %copy-done.7), custom_call_target="tpu_custom_call" | custom-call | bytes 6000000 | tf_op jit(solution)/shard_map/pallas_call | solution.py:413
  49.8 5.3 %all-to-all-start.1 = ((f32[32,1,64,128]{3,2,1,0:T(8,128)}), f32[32,1,64,128]{3,2,1,0:T(8,128)S(1)}, u32[]{:S(2)}, u32[]{:S(2)}) async-start(f32[32,1,64,128]{3,2,1,0:T(8,128)} %get-tuple-element.19), calls=%async_computation.1 | async-start | bytes 2097152 | tf_op jit(solution)/shard_map/all_to_all | solution.py:422
  55.1 0.1 select_reduce_fusion.2
  55.3 0.2 select_reduce_fusion
  55.5 0.6 broadcast_add_fusion.1.block_ref
  56.1 0.3 collective-permute-start.7
  56.4 0.2 collective-permute-start.8
  56.6 0.3 collective-permute-start.9
  56.9 0.3 collective-permute-start.10
  57.1 3.5 %shard_map.86.words_ref = s32[4,128,128]{2,1,0:T(8,128)} custom-call(s32[544]{0:T(1024)} %broadcast_add_fusion.1.block_ref, s32[512,128]{1,0:T(8,128)} %cell_ref.7), custom_call_target="tpu_custom_call" | custom-call | bytes 6000000 | tf_op jit(solution)/shard_map/pallas_call | solution.py:425
  60.6 0.1 convert_reduce_fusion.2
  60.7 0.6 broadcast_minimum_fusion.pair_ref
  61.3 0.0 collective-permute-done.8.refs_5_
  61.3 0.0 collective-permute-done.9.refs_6_
  61.3 0.7 copy-done.12
  62.0 0.1 copy-done.13
  62.2 0.1 copy-done.14
  62.3 19.8 %shard_map.90.here_any = f32[3,512,128]{2,1,0:T(8,128)} custom-call(s32[512]{0:T(512)} %get-tuple-element.39.slot_ref, s32[512,128]{1,0:T(8,128)} %cell_ref.7, f32[4,3,64,128]{3,2,1,0:T(8,128)} %get-tuple-element.16.refs_0_, f32[4,3,64,128]{3,2,1,0:T(8,128)} %copy-done.3, f32[4,3,64,128]{3,2,1,0:T(8,128)} %copy-done.5, f32[4,3,64,128]{3,2,1,0:T(8,128)} %copy-done.7, ...), custom_call_target="tpu_custom_call" | custom-call | bytes 54000000 | tf_op jit(solution)/shard_map/pallas_call | solution.py:435
  82.1 0.0 all-to-all-done.1.solid_any
  82.1 1.0 copy-done
  83.0 20.6 %shard_map.91 = (f32[3,512,128]{2,1,0:T(8,128)}, f32[16,3,64,128]{3,2,1,0:T(8,128)}, f32[16,3,64,128]{3,2,1,0:T(8,128)}, f32[1,64,128]{2,1,0:T(8,128)}) custom-call(s32[512]{0:T(512)} %bitcast.35, s32[544]{0:T(1024)} %broadcast_add_fusion.1.block_ref, s32[272]{0:T(512)} %broadcast_minimum_fusion.pair_ref, s32[512,128]{1,0:T(8,128)} %cell_ref.7, ...), custom_call_target="tpu_custom_call" | custom-call | bytes 60000000 | tf_op jit(solution)/shard_map/pallas_call | solution.py:446
  103.7 0.3 collective-permute-start.15
  104.0 3.4 %collective-permute-done.15 = f32[16,3,64,128]{3,2,1,0:T(8,128)S(1)} collective-permute-done((f32[16,3,64,128]{3,2,1,0:T(8,128)}, f32[16,3,64,128]{3,2,1,0:T(8,128)S(1)}, u32[]{:S(2)}, u32[]{:S(2)}) %collective-permute-start.15) | collective-permute-done | bytes 1572896 | tf_op jit(solution)/shard_map/ppermute | solution.py:469
  107.4 2.8 %add.150 = f32[16,3,64,128]{3,2,1,0:T(8,128)} add(f32[16,3,64,128]{3,2,1,0:T(8,128)} %get-tuple-element.21, f32[16,3,64,128]{3,2,1,0:T(8,128)S(1)} %collective-permute-done.15) | non-fusion elementwise | flops 393216 | bytes 4718592 | tf_op jit(solution)/shard_map/add | solution.py:469
  110.2 7.2 %all-to-all-start.2 = ((f32[16,3,64,128]{3,2,1,0:T(8,128)}), f32[16,3,64,128]{3,2,1,0:T(8,128)S(1)}, u32[]{:S(2)}, u32[]{:S(2)}) async-start(f32[16,3,64,128]{3,2,1,0:T(8,128)} %add.150), calls=%async_computation.2 | async-start | bytes 3145728 | tf_op jit(solution)/shard_map/all_to_all | solution.py:382
  117.5 3.8 %collective-permute-start.14 = (f32[5,4,1,128]{3,2,1,0:T(1,128)S(1)}, f32[5,4,1,128]{3,2,1,0:T(1,128)S(1)}, u32[]{:S(2)}, u32[]{:S(2)}) collective-permute-start(f32[5,4,1,128]{3,2,1,0:T(1,128)S(1)} %get-tuple-element.36), channel_id=1, source_target_pairs={{0,1},{1,2},{2,3},{4,5},{5,6},{6,7},{8,9},{9,10},{10,11},{12,13},{... | collective-permute-start | bytes 30728 | tf_op jit(solution)/shard_map/ppermute | solution.py:341
  121.3 1.3 collective-permute-start.13
  122.6 0.1 fusion.23
  122.8 0.1 collective-permute-start.12
  122.8 5.1 %collective-permute-start.11 = (f32[5,1,16,128]{3,2,1,0:T(8,128)S(1)}, f32[5,1,16,128]{3,2,1,0:T(8,128)S(1)}, u32[]{:S(2)}, u32[]{:S(2)}) collective-permute-start(f32[5,1,16,128]{3,2,1,0:T(8,128)S(1)} %get-tuple-element.33), channel_id=1, source_target_pairs={{4,0},{8,4},{12,8},{16,12},{20,16},{24,20},{28,24},{32,28},{36,32}... | collective-permute-start | bytes 122888 | tf_op jit(solution)/shard_map/ppermute | solution.py:342
  127.9 0.0 collective-permute-done.14
  127.9 0.0 collective-permute-done.13
  127.9 12.3 %collective-permute-done.12 = f32[5,1,16,128]{3,2,1,0:T(8,128)S(1)} collective-permute-done((f32[5,1,16,128]{3,2,1,0:T(8,128)S(1)}, f32[5,1,16,128]{3,2,1,0:T(8,128)S(1)}, u32[]{:S(2)}, u32[]{:S(2)}) %collective-permute-start.12) | collective-permute-done | bytes 40992 | tf_op jit(solution)/shard_map/ppermute | solution.py:341
  140.2 0.0 collective-permute-done.11
  140.2 1.8 %all-to-all-done.2 = f32[16,3,64,128]{3,2,1,0:T(8,128)S(1)} async-done(((f32[16,3,64,128]{3,2,1,0:T(8,128)}), f32[16,3,64,128]{3,2,1,0:T(8,128)S(1)}, u32[]{:S(2)}, u32[]{:S(2)}) %all-to-all-start.2) | async-done | bytes 1572896 | tf_op jit(solution)/shard_map/all_to_all | solution.py:382
  142.0 0.1 reduce_sum.69
  142.1 0.8 fusion.11
  (44 shorter events, 0.2 us)
Async XLA Ops:
  2.0 33.6 %copy-start.19 = (s32[512]{0:T(512)S(1)}, s32[512]{0:T(512)}, u32[]{:S(2)}) copy-start(s32[512]{0:T(512)} %get-tuple-element.40.slot_ref) | copy-start | bytes 6148
  10.1 9.6 %collective-permute-start = (f32[16,1,64,128]{3,2,1,0:T(8,128)}, f32[16,1,64,128]{3,2,1,0:T(8,128)S(1)}, u32[]{:S(2)}, u32[]{:S(2)}) collective-permute-start(f32[16,1,64,128]{3,2,1,0:T(8,128)} %get-tuple-element.14), channel_id=1, source_target_pairs={{0,4},{4,0},{8,12},{12,8},{16,20},{20,16},{24,28},{28,24},{32,36},... | collective-permute-start | bytes 1572872 | tf_op jit(solution)/shard_map/ppermute | solution.py:402
  10.2 6.7 %collective-permute-start.1 = (f32[1,3,64,128]{3,2,1,0:T(8,128)}, f32[1,3,64,128]{3,2,1,0:T(8,128)S(1)}, u32[]{:S(2)}, u32[]{:S(2)}) collective-permute-start(f32[1,3,64,128]{3,2,1,0:T(8,128)} %get-tuple-element.15.refs_0_), channel_id=1, source_target_pairs={{0,8},{4,36},{8,16},{12,44},{16,24},{20,52},{24,0},{28,60},{32,40}... | collective-permute-start | bytes 294920 | tf_op jit(solution)/shard_map/ppermute | solution.py:403
  12.0 6.8 %collective-permute-start.2 = (f32[1,3,64,128]{3,2,1,0:T(8,128)}, f32[1,3,64,128]{3,2,1,0:T(8,128)S(1)}, u32[]{:S(2)}, u32[]{:S(2)}) collective-permute-start(f32[1,3,64,128]{3,2,1,0:T(8,128)} %get-tuple-element.15.refs_0_), channel_id=1, source_target_pairs={{0,16},{4,68},{8,24},{12,76},{16,0},{20,84},{24,8},{28,92},{32,48}... | collective-permute-start | bytes 294920 | tf_op jit(solution)/shard_map/ppermute | solution.py:403
  14.9 4.8 %collective-permute-start.3 = (f32[1,3,64,128]{3,2,1,0:T(8,128)}, f32[1,3,64,128]{3,2,1,0:T(8,128)S(1)}, u32[]{:S(2)}, u32[]{:S(2)}) collective-permute-start(f32[1,3,64,128]{3,2,1,0:T(8,128)} %get-tuple-element.15.refs_0_), channel_id=1, source_target_pairs={{0,24},{4,100},{8,0},{12,108},{16,8},{20,116},{24,16},{28,124},{32... | collective-permute-start | bytes 294920 | tf_op jit(solution)/shard_map/ppermute | solution.py:403
  16.9 2.8 %copy-start.15 = (f32[1,3,64,128]{3,2,1,0:T(8,128)}, f32[1,3,64,128]{3,2,1,0:T(8,128)S(1)}, u32[]{:S(2)}) copy-start(f32[1,3,64,128]{3,2,1,0:T(8,128)S(1)} %collective-permute-done.1.refs_1_) | copy-start | bytes 294916
  18.7 1.0 copy-start.16
  19.7 0.6 copy-start.17
  19.7 0.8 copy-start.9
  22.8 23.2 %all-to-all-start = ((f32[16,1,64,128]{3,2,1,0:T(8,128)}), f32[16,1,64,128]{3,2,1,0:T(8,128)S(1)}, u32[]{:S(2)}, u32[]{:S(2)}) async-start(f32[16,1,64,128]{3,2,1,0:T(8,128)} %get-tuple-element.17), calls=%async_computation | async-start | bytes 1048576 | tf_op jit(solution)/shard_map/all_to_all | solution.py:382
  29.3 12.5 %collective-permute-start.4 = (f32[4,3,64,128]{3,2,1,0:T(8,128)}, f32[4,3,64,128]{3,2,1,0:T(8,128)S(1)}, u32[]{:S(2)}, u32[]{:S(2)}) collective-permute-start(f32[4,3,64,128]{3,2,1,0:T(8,128)} %get-tuple-element.16.refs_0_), channel_id=1, source_target_pairs={{0,32},{4,12},{8,40},{12,20},{16,48},{20,28},{24,56},{28,4},{32,64... | collective-permute-start | bytes 1179656 | tf_op jit(solution)/shard_map/ppermute | solution.py:412
  31.3 14.7 %collective-permute-start.5 = (f32[4,3,64,128]{3,2,1,0:T(8,128)}, f32[4,3,64,128]{3,2,1,0:T(8,128)S(1)}, u32[]{:S(2)}, u32[]{:S(2)}) collective-permute-start(f32[4,3,64,128]{3,2,1,0:T(8,128)} %get-tuple-element.16.refs_0_), channel_id=1, source_target_pairs={{0,64},{4,20},{8,72},{12,28},{16,80},{20,4},{24,88},{28,12},{32,96... | collective-permute-start | bytes 1179656 | tf_op jit(solution)/shard_map/ppermute | solution.py:412
  34.0 12.0 %collective-permute-start.6 = (f32[4,3,64,128]{3,2,1,0:T(8,128)}, f32[4,3,64,128]{3,2,1,0:T(8,128)S(1)}, u32[]{:S(2)}, u32[]{:S(2)}) collective-permute-start(f32[4,3,64,128]{3,2,1,0:T(8,128)} %get-tuple-element.16.refs_0_), channel_id=1, source_target_pairs={{0,96},{4,28},{8,104},{12,4},{16,112},{20,12},{24,120},{28,20},{32... | collective-permute-start | bytes 1179656 | tf_op jit(solution)/shard_map/ppermute | solution.py:412
  35.9 20.2 %copy-start.11 = (f32[4,3,64,128]{3,2,1,0:T(8,128)S(1)}, f32[4,3,64,128]{3,2,1,0:T(8,128)}, u32[]{:S(2)}) copy-start(f32[4,3,64,128]{3,2,1,0:T(8,128)} %get-tuple-element.16.refs_0_) | copy-start | bytes 1179652
  41.8 4.2 %copy-start.3 = (f32[4,3,64,128]{3,2,1,0:T(8,128)}, f32[4,3,64,128]{3,2,1,0:T(8,128)S(1)}, u32[]{:S(2)}) copy-start(f32[4,3,64,128]{3,2,1,0:T(8,128)S(1)} %collective-permute-done.4.refs_0_.refs_1_) | copy-start | bytes 1179652
  46.0 0.7 copy-start.5
  46.0 0.9 copy-start.7
  46.9 0.8 copy-start.2
  49.8 6.5 %copy-start.4 = (f32[4,3,64,128]{3,2,1,0:T(8,128)S(1)}, f32[4,3,64,128]{3,2,1,0:T(8,128)}, u32[]{:S(2)}) copy-start(f32[4,3,64,128]{3,2,1,0:T(8,128)} %copy-done.3) | copy-start | bytes 1179652
  49.8 6.8 %copy-start.6 = (f32[4,3,64,128]{3,2,1,0:T(8,128)S(1)}, f32[4,3,64,128]{3,2,1,0:T(8,128)}, u32[]{:S(2)}) copy-start(f32[4,3,64,128]{3,2,1,0:T(8,128)} %copy-done.5) | copy-start | bytes 1179652
  49.8 7.0 %copy-start.8 = (f32[4,3,64,128]{3,2,1,0:T(8,128)S(1)}, f32[4,3,64,128]{3,2,1,0:T(8,128)}, u32[]{:S(2)}) copy-start(f32[4,3,64,128]{3,2,1,0:T(8,128)} %copy-done.7) | copy-start | bytes 1179652
  49.8 32.2 %all-to-all-start.1 = ((f32[32,1,64,128]{3,2,1,0:T(8,128)}), f32[32,1,64,128]{3,2,1,0:T(8,128)S(1)}, u32[]{:S(2)}, u32[]{:S(2)}) async-start(f32[32,1,64,128]{3,2,1,0:T(8,128)} %get-tuple-element.19), calls=%async_computation.1 | async-start | bytes 2097152 | tf_op jit(solution)/shard_map/all_to_all | solution.py:422
  56.1 5.2 %collective-permute-start.7 = (f32[4,3,64,128]{3,2,1,0:T(8,128)S(1)}, f32[4,3,64,128]{3,2,1,0:T(8,128)S(1)}, u32[]{:S(2)}, u32[]{:S(2)}) collective-permute-start(f32[4,3,64,128]{3,2,1,0:T(8,128)S(1)} %copy-done.11), channel_id=1, source_target_pairs={{0,4},{4,0},{8,12},{12,8},{16,20},{20,16},{24,28},{28,24},{32,36},... | collective-permute-start | bytes 1179656 | tf_op jit(solution)/shard_map/ppermute | solution.py:421
  56.4 4.9 %collective-permute-start.8 = (f32[4,3,64,128]{3,2,1,0:T(8,128)S(1)}, f32[4,3,64,128]{3,2,1,0:T(8,128)S(1)}, u32[]{:S(2)}, u32[]{:S(2)}) collective-permute-start(f32[4,3,64,128]{3,2,1,0:T(8,128)S(1)} %copy-done.4), channel_id=1, source_target_pairs={{0,4},{4,0},{8,12},{12,8},{16,20},{20,16},{24,28},{28,24},{32,36},... | collective-permute-start | bytes 1179656 | tf_op jit(solution)/shard_map/ppermute | solution.py:421
  56.6 4.7 %collective-permute-start.9 = (f32[4,3,64,128]{3,2,1,0:T(8,128)S(1)}, f32[4,3,64,128]{3,2,1,0:T(8,128)S(1)}, u32[]{:S(2)}, u32[]{:S(2)}) collective-permute-start(f32[4,3,64,128]{3,2,1,0:T(8,128)S(1)} %copy-done.6), channel_id=1, source_target_pairs={{0,4},{4,0},{8,12},{12,8},{16,20},{20,16},{24,28},{28,24},{32,36},... | collective-permute-start | bytes 1179656 | tf_op jit(solution)/shard_map/ppermute | solution.py:421
  56.9 4.5 %collective-permute-start.10 = (f32[4,3,64,128]{3,2,1,0:T(8,128)S(1)}, f32[4,3,64,128]{3,2,1,0:T(8,128)}, u32[]{:S(2)}, u32[]{:S(2)}) collective-permute-start(f32[4,3,64,128]{3,2,1,0:T(8,128)S(1)} %copy-done.8), channel_id=1, source_target_pairs={{0,4},{4,0},{8,12},{12,8},{16,20},{20,16},{24,28},{28,24},{32,36},... | collective-permute-start | bytes 1179656 | tf_op jit(solution)/shard_map/ppermute | solution.py:421
  61.3 0.7 copy-start.12
  61.3 0.9 copy-start.13
  61.3 1.0 copy-start.14
  82.1 1.0 copy-start
  103.7 3.7 %collective-permute-start.15 = (f32[16,3,64,128]{3,2,1,0:T(8,128)}, f32[16,3,64,128]{3,2,1,0:T(8,128)S(1)}, u32[]{:S(2)}, u32[]{:S(2)}) collective-permute-start(f32[16,3,64,128]{3,2,1,0:T(8,128)} %get-tuple-element.22), channel_id=1, source_target_pairs={{0,4},{4,0},{8,12},{12,8},{16,20},{20,16},{24,28},{28,24},{32,36},... | collective-permute-start | bytes 4718600 | tf_op jit(solution)/shard_map/ppermute | solution.py:469
  110.2 7.2 %copy-start.18 = (f32[1,64,128]{2,1,0:T(8,128)S(1)}, f32[1,64,128]{2,1,0:T(8,128)}, u32[]{:S(2)}) copy-start(f32[1,64,128]{2,1,0:T(8,128)} %get-tuple-element.20) | copy-start | bytes 98308
  110.2 7.3 %copy-start.1 = (f32[3,4,16,128]{3,2,1,0:T(8,128)S(1)}, f32[3,4,16,128]{3,2,1,0:T(8,128)}, u32[]{:S(2)}) copy-start(f32[3,4,16,128]{3,2,1,0:T(8,128)} %param.7) | copy-start | bytes 294916
  110.2 7.3 %copy-start.10 = (f32[4,16,128]{2,1,0:T(8,128)S(1)}, f32[4,16,128]{2,1,0:T(8,128)}, u32[]{:S(2)}) copy-start(f32[4,16,128]{2,1,0:T(8,128)} %param.8) | copy-start | bytes 98308
  110.2 31.8 %all-to-all-start.2 = ((f32[16,3,64,128]{3,2,1,0:T(8,128)}), f32[16,3,64,128]{3,2,1,0:T(8,128)S(1)}, u32[]{:S(2)}, u32[]{:S(2)}) async-start(f32[16,3,64,128]{3,2,1,0:T(8,128)} %add.150), calls=%async_computation.2 | async-start | bytes 3145728 | tf_op jit(solution)/shard_map/all_to_all | solution.py:382
  117.5 10.4 %collective-permute-start.14 = (f32[5,4,1,128]{3,2,1,0:T(1,128)S(1)}, f32[5,4,1,128]{3,2,1,0:T(1,128)S(1)}, u32[]{:S(2)}, u32[]{:S(2)}) collective-permute-start(f32[5,4,1,128]{3,2,1,0:T(1,128)S(1)} %get-tuple-element.36), channel_id=1, source_target_pairs={{0,1},{1,2},{2,3},{4,5},{5,6},{6,7},{8,9},{9,10},{10,11},{12,13},{... | collective-permute-start | bytes 30728 | tf_op jit(solution)/shard_map/ppermute | solution.py:341
  121.3 6.6 %collective-permute-start.13 = (f32[5,4,1,128]{3,2,1,0:T(1,128)S(1)}, f32[5,4,1,128]{3,2,1,0:T(1,128)S(1)}, u32[]{:S(2)}, u32[]{:S(2)}) collective-permute-start(f32[5,4,1,128]{3,2,1,0:T(1,128)S(1)} %get-tuple-element.35), channel_id=1, source_target_pairs={{1,0},{2,1},{3,2},{5,4},{6,5},{7,6},{9,8},{10,9},{11,10},{13,12},{... | collective-permute-start | bytes 30728 | tf_op jit(solution)/shard_map/ppermute | solution.py:342
  122.8 17.4 %collective-permute-start.12 = (f32[5,1,16,128]{3,2,1,0:T(8,128)S(1)}, f32[5,1,16,128]{3,2,1,0:T(8,128)S(1)}, u32[]{:S(2)}, u32[]{:S(2)}) collective-permute-start(f32[5,1,16,128]{3,2,1,0:T(8,128)S(1)} %get-tuple-element.34), channel_id=1, source_target_pairs={{0,4},{4,8},{8,12},{12,16},{16,20},{20,24},{24,28},{28,32},{32,36}... | collective-permute-start | bytes 122888 | tf_op jit(solution)/shard_map/ppermute | solution.py:341
  122.8 17.3 %collective-permute-start.11 = (f32[5,1,16,128]{3,2,1,0:T(8,128)S(1)}, f32[5,1,16,128]{3,2,1,0:T(8,128)S(1)}, u32[]{:S(2)}, u32[]{:S(2)}) collective-permute-start(f32[5,1,16,128]{3,2,1,0:T(8,128)S(1)} %get-tuple-element.33), channel_id=1, source_target_pairs={{4,0},{8,4},{12,8},{16,12},{20,16},{24,20},{28,24},{32,28},{36,32}... | collective-permute-start | bytes 122888 | tf_op jit(solution)/shard_map/ppermute | solution.py:342

commit v3 on v2

--- a/solution.py
+++ b/solution.py
@@ -90,9 +90,8 @@
 
 
 def deposit_kernel(
-    slot_ref, cell_ref, vol_ref, tile_ref, same_ref, other_ref, late_ref, sum_ref, words_ref, sems
+    slot_ref, cell_ref, vol_ref, same_ref, other_ref, sum_ref, words_ref, sems
 ):
-    late_ref[...] = tile_ref[...]
     sum_ref[...] = jnp.zeros_like(sum_ref)
     blocks = cell_ref.shape[0]
     for g in range(blocks // 256):
@@ -384,11 +383,12 @@
         )
 
     one_sum = arrays(near, 1, tile_rows, radial)
-    dep_same, dep_other, flow_tile = pl.pallas_call(
+    flow_tile = fluid_vel.reshape(1, 3, tile_rows, radial)
+    dep_same, dep_other = pl.pallas_call(
         deposit_kernel,
-        out_shape=(one_sum, one_sum, arrays(1, 3, tile_rows, radial)),
-        in_specs=[SMEM_SPEC] + [VMEM_SPEC] * 3,
-        out_specs=(ANY_SPEC, ANY_SPEC, VMEM_SPEC),
+        out_shape=(one_sum, one_sum),
+        in_specs=[SMEM_SPEC] + [VMEM_SPEC] * 2,
+        out_specs=(ANY_SPEC, ANY_SPEC),
         scratch_shapes=[
             pltpu.VMEM((size, 1, tile_rows, radial), F32),
             pltpu.VMEM((blocks // 256, LANES, LANES), I32),
@@ -396,7 +396,7 @@
         ],
         compiler_params=PARAMS,
         cost_estimate=cost(7),
-    )(slot, cell_of, part_vol, fluid_vel.reshape(1, 3, tile_rows, radial))
+    )(slot, cell_of, part_vol)
 
     steps = range(1, SIDE)
     dep_twin = lax.ppermute(dep_other, "azim", twin)
@@ -410,17 +410,6 @@
         cost_estimate=cost(2),
     )(dep_same, dep_twin, *tiles)
     groups = [first] + [lax.ppermute(first, "azim", along(1, k)) for k in steps]
-    solid_flat, solid_tiles = pl.pallas_call(
-        owner_kernel,
-        out_shape=(arrays(1, tile_rows, radial), arrays(size, 1, tile_rows, radial)),
-        in_specs=[VMEM_SPEC] + [ANY_SPEC] * (SIDE - 1),
-        out_specs=(VMEM_SPEC, VMEM_SPEC),
-        compiler_params=PARAMS,
-        cost_estimate=cost(2),
-    )(to_owners(dep_parts), *groups[1:])
-    groups += [lax.ppermute(group, "azim", twin) for group in groups]
-    solid_tiles = lax.all_to_all(solid_tiles, "azim", split_axis=0, concat_axis=0, tiled=True)
-
     block, pair = order_of(slot, size)
     words = pl.pallas_call(
         words_kernel,
@@ -431,6 +420,17 @@
         compiler_params=PARAMS,
         cost_estimate=cost(2),
     )(block, cell_of)
+
+    groups += [lax.ppermute(group, "azim", twin) for group in groups]
+    solid_flat, solid_tiles = pl.pallas_call(
+        owner_kernel,
+        out_shape=(arrays(1, tile_rows, radial), arrays(size, 1, tile_rows, radial)),
+        in_specs=[VMEM_SPEC] + [ANY_SPEC] * (SIDE + 2),
+        out_specs=(VMEM_SPEC, VMEM_SPEC),
+        compiler_params=PARAMS,
+        cost_estimate=cost(2),
+    )(to_owners(dep_parts), words, pair, *groups[SIDE:])
+    solid_tiles = lax.all_to_all(solid_tiles, "azim", split_axis=0, concat_axis=0, tiled=True)
 
     here = pl.pallas_call(
         flow_kernel,

time: 144 us -> 133 us (0.924)
  waiting for transfers between devices: 30.3 us -> 22.6 us
  starting transfers between devices: 42.7 us -> 40.9 us
    ppermute x3, waiting for transfers between devices: 10.1 us -> 3.91 us  [on_device(): groups = [first] + [lax.ppermute(first, 'azim', along(1, k)) for k in steps]]
    all_to_all x2, starting transfers between devices: 13.6 us -> 10.6 us  [to_owners(): lax.all_to_all(parts, 'azim', split_axis=0, concat_axis=0, tiled=True, ax...]
    ppermute x3, waiting for transfers between devices: 2.78 us -> 0.01 us  [on_device(): lax.ppermute(flow_tile, 'azim', along(0, k))]
    ppermute x4, starting transfers between devices: 1.05 us -> 2.83 us  [on_device(): groups += [lax.ppermute(group, 'azim', twin) for group in groups]]
    unnamed x40 -> x32, local copies, waits for them, and re-layouts: 4.44 us -> 3.55 us
  transfers between devices with their start and end apart: 19 -> 19, of which waited for: 7 -> 7; matrix products, arithmetic and copies ran while one was open for 2% -> 4% of each run, Pallas kernels for 16% -> 23%
where the time goes in v3:
time: 133 us
  Pallas kernels  55.9 us (42%)
  starting transfers between devices  40.9 us (31%)
  waiting for transfers between devices  22.6 us (17%)
  other arithmetic  8.63 us (6%)
  local copies, waits for them, and re-layouts  3.58 us (3%)
    pallas_call x1, Pallas kernels, on_device(): pl.pallas_call(particle_kernel, out_shape=(arrays(*three), three_sums, th...  20.6 us
    pallas_call x1, Pallas kernels, on_device(): pl.pallas_call(flow_kernel, out_shape=arrays(3, blocks, block_rows), in_s...  19.8 us
    ppermute x2, waiting for transfers between devices, padded_2(): before = lax.ppermute(last, axis, up)  12 us
    all_to_all x2, starting transfers between devices, to_owners(): lax.all_to_all(parts, 'azim', split_axis=0, concat_axis=0, tiled=True, ax...  10.6 us
    pallas_call x1, Pallas kernels, on_device(): pl.pallas_call(deposit_kernel, out_shape=(one_sum, one_sum), in_specs=[SM...  7.51 us
    ppermute x2, starting transfers between devices, padded_2(): after = lax.ppermute(first, axis, down)  6.34 us
    ppermute x3, starting transfers between devices, on_device(): lax.ppermute(flow_tile, 'azim', along(0, k))  5.98 us
    ppermute x3, starting transfers between devices, on_device(): groups = [first] + [lax.ppermute(first, 'azim', along(1, k)) for k in steps]  5.66 us
  transfers between devices with their start and end apart: 19, of which 7 were waited for; matrix products, arithmetic and copies ran while one was open for 4% of the time, Pallas kernels for 23%

profile of v3, /device:TPU:0, one launch (start us, length us, event | category | flops | bytes accessed | tf_op | source)
XLA Modules:
  0.0 132.5 jit_solution(2842274294208897809)
XLA Ops:
  0.6 1.7 %collective-permute-start.1 = (f32[1,3,64,128]{3,2,1,0:T(8,128)}, f32[1,3,64,128]{3,2,1,0:T(8,128)S(1)}, u32[]{:S(2)}, u32[]{:S(2)}) collective-permute-start(f32[1,3,64,128]{3,2,1,0:T(8,128)} %bitcast.21), channel_id=1, source_target_pairs={{0,8},{4,36},{8,16},{12,44},{16,24},{20,52},{24,0},{28,60},{32,40}... | collective-permute-start | bytes 294920 | tf_op jit(solution)/shard_map/ppermute | solution.py:403
  2.4 2.9 %collective-permute-start.2 = (f32[1,3,64,128]{3,2,1,0:T(8,128)}, f32[1,3,64,128]{3,2,1,0:T(8,128)S(1)}, u32[]{:S(2)}, u32[]{:S(2)}) collective-permute-start(f32[1,3,64,128]{3,2,1,0:T(8,128)} %bitcast.22), channel_id=1, source_target_pairs={{0,16},{4,68},{8,24},{12,76},{16,0},{20,84},{24,8},{28,92},{32,48}... | collective-permute-start | bytes 294920 | tf_op jit(solution)/shard_map/ppermute | solution.py:403
  5.3 1.3 %collective-permute-start.3 = (f32[1,3,64,128]{3,2,1,0:T(8,128)}, f32[1,3,64,128]{3,2,1,0:T(8,128)S(1)}, u32[]{:S(2)}, u32[]{:S(2)}) collective-permute-start(f32[1,3,64,128]{3,2,1,0:T(8,128)} %bitcast.23), channel_id=1, source_target_pairs={{0,24},{4,100},{8,0},{12,108},{16,8},{20,116},{24,16},{28,124},{32... | collective-permute-start | bytes 294920 | tf_op jit(solution)/shard_map/ppermute | solution.py:403
  6.6 1.3 select_add_fusion
  7.9 7.5 %shard_map.87 = (f32[16,1,64,128]{3,2,1,0:T(8,128)}, f32[16,1,64,128]{3,2,1,0:T(8,128)}) custom-call(s32[512]{0:T(512)} %get-tuple-element.38.slot_ref, s32[512,128]{1,0:T(8,128)} %cell_ref.7, f32[512,128]{1,0:T(8,128)} %vol_any.1), custom_call_target="tpu_custom_call" | custom-call | bytes 21000000 | tf_op jit(solution)/shard_map/pallas_call | solution.py:387
  15.4 0.1 collective-permute-start
  15.5 0.7 shift-right-arithmetic_add_fusion
  16.2 0.1 convert_reduce_fusion.1
  16.3 0.1 select_reduce_fusion.1
  16.4 1.0 convert_reduce_fusion
  17.4 0.0 collective-permute-done.1.refs_1_
  17.4 0.0 copy-start.12
  17.4 0.0 collective-permute-done.2.refs_2_
  17.5 0.0 collective-permute-done.3.refs_3_
  17.5 0.1 collective-permute-done.other_ref
  17.6 0.5 copy-done.12
  18.1 0.0 copy-done.13
  18.1 0.0 copy-done.14
  18.1 0.3 copy-done.7
  18.4 2.3 %shard_map.88 = (f32[16,1,64,128]{3,2,1,0:T(8,128)}, f32[4,3,64,128]{3,2,1,0:T(8,128)}) custom-call(f32[16,1,64,128]{3,2,1,0:T(8,128)} %get-tuple-element.12.same_ref, f32[16,1,64,128]{3,2,1,0:T(8,128)} %copy-done.7, f32[1,3,64,128]{3,2,1,0:T(8,128)} %bitcast.24, f32[1,3,64,128]{3,2,1,0:T(8,128)} %copy-done.12, f32[1,3,64,128]{3,2,1,0:T(8,128)} %copy-done.13, ...), custom_call_target="tpu_custom_call" | custom-call | bytes 6000000 | tf_op jit(solution)/shard_map/pallas_call | solution.py:404
  20.7 1.5 %collective-permute-start.4 = (f32[4,3,64,128]{3,2,1,0:T(8,128)}, f32[4,3,64,128]{3,2,1,0:T(8,128)S(1)}, u32[]{:S(2)}, u32[]{:S(2)}) collective-permute-start(f32[4,3,64,128]{3,2,1,0:T(8,128)} %get-tuple-element.14.refs_0_), channel_id=1, source_target_pairs={{0,32},{4,12},{8,40},{12,20},{16,48},{20,28},{24,56},{28,4},{32,64... | collective-permute-start | bytes 1179656 | tf_op jit(solution)/shard_map/ppermute | solution.py:412
  22.2 2.7 %collective-permute-start.5 = (f32[4,3,64,128]{3,2,1,0:T(8,128)}, f32[4,3,64,128]{3,2,1,0:T(8,128)S(1)}, u32[]{:S(2)}, u32[]{:S(2)}) collective-permute-start(f32[4,3,64,128]{3,2,1,0:T(8,128)} %get-tuple-element.14.refs_0_), channel_id=1, source_target_pairs={{0,64},{4,20},{8,72},{12,28},{16,80},{20,4},{24,88},{28,12},{32,96... | collective-permute-start | bytes 1179656 | tf_op jit(solution)/shard_map/ppermute | solution.py:412
  24.9 1.4 %collective-permute-start.6 = (f32[4,3,64,128]{3,2,1,0:T(8,128)}, f32[4,3,64,128]{3,2,1,0:T(8,128)S(1)}, u32[]{:S(2)}, u32[]{:S(2)}) collective-permute-start(f32[4,3,64,128]{3,2,1,0:T(8,128)} %get-tuple-element.14.refs_0_), channel_id=1, source_target_pairs={{0,96},{4,28},{8,104},{12,4},{16,112},{20,12},{24,120},{28,20},{32... | collective-permute-start | bytes 1179656 | tf_op jit(solution)/shard_map/ppermute | solution.py:412
  26.4 0.2 select_reduce_fusion
  26.6 0.6 broadcast_add_fusion.1.block_ref
  27.2 3.6 %all-to-all-start = ((f32[16,1,64,128]{3,2,1,0:T(8,128)}), f32[16,1,64,128]{3,2,1,0:T(8,128)S(1)}, u32[]{:S(2)}, u32[]{:S(2)}) async-start(f32[16,1,64,128]{3,2,1,0:T(8,128)} %get-tuple-element.15), calls=%async_computation | async-start | bytes 1048576 | tf_op jit(solution)/shard_map/all_to_all | solution.py:381
  30.7 0.1 select_reduce_fusion.2
  30.9 0.2 collective-permute-start.7
  31.0 0.0 collective-permute-done.4.refs_1_
  31.0 2.7 %collective-permute-start.8 = (f32[4,3,64,128]{3,2,1,0:T(8,128)S(1)}, f32[4,3,64,128]{3,2,1,0:T(8,128)S(1)}, u32[]{:S(2)}, u32[]{:S(2)}) collective-permute-start(f32[4,3,64,128]{3,2,1,0:T(8,128)S(1)} %collective-permute-done.4.refs_1_), channel_id=1, source_target_pairs={{0,4},{4,0},{8,12},{12,8},{16,20},{20,16},{24,28},{28,24},{32,36},... | collective-permute-start | bytes 1179656 | tf_op jit(solution)/shard_map/ppermute | solution.py:424
  33.7 1.5 %collective-permute-done.5.refs_2_ = f32[4,3,64,128]{3,2,1,0:T(8,128)S(1)} collective-permute-done((f32[4,3,64,128]{3,2,1,0:T(8,128)}, f32[4,3,64,128]{3,2,1,0:T(8,128)S(1)}, u32[]{:S(2)}, u32[]{:S(2)}) %collective-permute-start.5) | collective-permute-done | bytes 393248 | tf_op jit(solution)/shard_map/ppermute | solution.py:412
  35.1 0.0 collective-permute-start.9
  35.1 2.5 %collective-permute-done.6.refs_3_ = f32[4,3,64,128]{3,2,1,0:T(8,128)S(1)} collective-permute-done((f32[4,3,64,128]{3,2,1,0:T(8,128)}, f32[4,3,64,128]{3,2,1,0:T(8,128)S(1)}, u32[]{:S(2)}, u32[]{:S(2)}) %collective-permute-start.6) | collective-permute-done | bytes 393248 | tf_op jit(solution)/shard_map/ppermute | solution.py:412
  37.6 0.0 collective-permute-start.10
  37.6 3.6 %shard_map.86.refs_0_.words_ref = s32[4,128,128]{2,1,0:T(8,128)} custom-call(s32[544]{0:T(1024)} %broadcast_add_fusion.1.block_ref, s32[512,128]{1,0:T(8,128)} %cell_ref.7), custom_call_target="tpu_custom_call" | custom-call | bytes 6000000 | tf_op jit(solution)/shard_map/pallas_call | solution.py:414
  41.2 0.1 convert_reduce_fusion.2
  41.3 0.6 broadcast_minimum_fusion.refs_1_.pair_ref
  41.9 0.0 collective-permute-done.7.refs_2_.refs_4_
  41.9 1.1 all-to-all-done.got_ref
  43.1 0.7 copy-done.2
  43.8 0.1 copy-done.4
  44.0 0.1 copy-done.5
  44.1 0.7 copy-done.6
  44.8 2.2 %shard_map.89 = (f32[1,64,128]{2,1,0:T(8,128)}, f32[32,1,64,128]{3,2,1,0:T(8,128)}) custom-call(f32[16,1,64,128]{3,2,1,0:T(8,128)} %copy-done.2, s32[4,128,128]{2,1,0:T(8,128)} %shard_map.86.refs_0_.words_ref, s32[272]{0:T(512)} %broadcast_minimum_fusion.refs_1_.pair_ref, f32[4,3,64,128]{3,2,1,0:T(8,128)} %copy-done.3, f32[4,3,64,128]{3,2,1,0:T(8,128)} %copy-done.4, ...), custom_call_target="tpu_custom_call" | custom-call | bytes 6000000 | tf_op jit(solution)/shard_map/pallas_call | solution.py:425
  47.0 5.3 %all-to-all-start.1 = ((f32[32,1,64,128]{3,2,1,0:T(8,128)}), f32[32,1,64,128]{3,2,1,0:T(8,128)S(1)}, u32[]{:S(2)}, u32[]{:S(2)}) async-start(f32[32,1,64,128]{3,2,1,0:T(8,128)} %get-tuple-element.17), calls=%async_computation.1 | async-start | bytes 2097152 | tf_op jit(solution)/shard_map/all_to_all | solution.py:433
  52.3 19.8 %shard_map.90.here_any = f32[3,512,128]{2,1,0:T(8,128)} custom-call(s32[512]{0:T(512)} %get-tuple-element.37.slot_ref, s32[512,128]{1,0:T(8,128)} %cell_ref.7, f32[4,3,64,128]{3,2,1,0:T(8,128)} %get-tuple-element.14.refs_0_, f32[4,3,64,128]{3,2,1,0:T(8,128)} %copy-done.9, f32[4,3,64,128]{3,2,1,0:T(8,128)} %copy-done.10, f32[4,3,64,128]{3,2,1,0:T(8,128)} %copy-done.11, ...), custom_call_target="tpu_custom_call" | custom-call | bytes 54000000 | tf_op jit(solution)/shard_map/pallas_call | solution.py:435
  72.1 0.0 all-to-all-done.1.solid_any
  72.1 0.9 copy-done
  73.0 20.6 %shard_map.91 = (f32[3,512,128]{2,1,0:T(8,128)}, f32[16,3,64,128]{3,2,1,0:T(8,128)}, f32[16,3,64,128]{3,2,1,0:T(8,128)}, f32[1,64,128]{2,1,0:T(8,128)}) custom-call(s32[512]{0:T(512)} %bitcast.38, s32[544]{0:T(1024)} %broadcast_add_fusion.1.block_ref, s32[272]{0:T(512)} %broadcast_minimum_fusion.refs_1_.pair_ref, s32[512,128]{1,0:T(8,128)} %cell_ref.7, ...), custom_call_target="tpu_custom_call" | custom-call | bytes 60000000 | tf_op jit(solution)/shard_map/pallas_call | solution.py:446
  93.7 0.2 collective-permute-start.15
  93.9 3.5 %collective-permute-done.15 = f32[16,3,64,128]{3,2,1,0:T(8,128)S(1)} collective-permute-done((f32[16,3,64,128]{3,2,1,0:T(8,128)}, f32[16,3,64,128]{3,2,1,0:T(8,128)S(1)}, u32[]{:S(2)}, u32[]{:S(2)}) %collective-permute-start.15) | collective-permute-done | bytes 1572896 | tf_op jit(solution)/shard_map/ppermute | solution.py:469
  97.4 2.8 %add.150 = f32[16,3,64,128]{3,2,1,0:T(8,128)} add(f32[16,3,64,128]{3,2,1,0:T(8,128)} %get-tuple-element.19, f32[16,3,64,128]{3,2,1,0:T(8,128)S(1)} %collective-permute-done.15) | non-fusion elementwise | flops 393216 | bytes 4718592 | tf_op jit(solution)/shard_map/add | solution.py:469
  100.2 7.1 %all-to-all-start.2 = ((f32[16,3,64,128]{3,2,1,0:T(8,128)}), f32[16,3,64,128]{3,2,1,0:T(8,128)S(1)}, u32[]{:S(2)}, u32[]{:S(2)}) async-start(f32[16,3,64,128]{3,2,1,0:T(8,128)} %add.150), calls=%async_computation.2 | async-start | bytes 3145728 | tf_op jit(solution)/shard_map/all_to_all | solution.py:381
  107.4 3.8 %collective-permute-start.14 = (f32[5,4,1,128]{3,2,1,0:T(1,128)S(1)}, f32[5,4,1,128]{3,2,1,0:T(1,128)S(1)}, u32[]{:S(2)}, u32[]{:S(2)}) collective-permute-start(f32[5,4,1,128]{3,2,1,0:T(1,128)S(1)} %get-tuple-element.34), channel_id=1, source_target_pairs={{0,1},{1,2},{2,3},{4,5},{5,6},{6,7},{8,9},{9,10},{10,11},{12,13},{... | collective-permute-start | bytes 30728 | tf_op jit(solution)/shard_map/ppermute | solution.py:340
  111.2 1.3 collective-permute-start.13
  112.5 0.1 fusion.23
  112.6 0.1 collective-permute-start.12
  112.7 5.1 %collective-permute-start.11 = (f32[5,1,16,128]{3,2,1,0:T(8,128)S(1)}, f32[5,1,16,128]{3,2,1,0:T(8,128)S(1)}, u32[]{:S(2)}, u32[]{:S(2)}) collective-permute-start(f32[5,1,16,128]{3,2,1,0:T(8,128)S(1)} %get-tuple-element.31), channel_id=1, source_target_pairs={{4,0},{8,4},{12,8},{16,12},{20,16},{24,20},{28,24},{32,28},{36,32}... | collective-permute-start | bytes 122888 | tf_op jit(solution)/shard_map/ppermute | solution.py:341
  117.7 0.0 collective-permute-done.14
  117.7 0.0 collective-permute-done.13
  117.8 12.0 %collective-permute-done.12 = f32[5,1,16,128]{3,2,1,0:T(8,128)S(1)} collective-permute-done((f32[5,1,16,128]{3,2,1,0:T(8,128)S(1)}, f32[5,1,16,128]{3,2,1,0:T(8,128)S(1)}, u32[]{:S(2)}, u32[]{:S(2)}) %collective-permute-start.12) | collective-permute-done | bytes 40992 | tf_op jit(solution)/shard_map/ppermute | solution.py:340
  129.8 1.8 %all-to-all-done.2 = f32[16,3,64,128]{3,2,1,0:T(8,128)S(1)} async-done(((f32[16,3,64,128]{3,2,1,0:T(8,128)}), f32[16,3,64,128]{3,2,1,0:T(8,128)S(1)}, u32[]{:S(2)}, u32[]{:S(2)}) %all-to-all-start.2) | async-done | bytes 1572896 | tf_op jit(solution)/shard_map/all_to_all | solution.py:381
  131.7 0.1 reduce_sum.69
  131.7 0.8 fusion.11
  (36 shorter events, 0.2 us)
Async XLA Ops:
  0.6 16.8 %collective-permute-start.1 = (f32[1,3,64,128]{3,2,1,0:T(8,128)}, f32[1,3,64,128]{3,2,1,0:T(8,128)S(1)}, u32[]{:S(2)}, u32[]{:S(2)}) collective-permute-start(f32[1,3,64,128]{3,2,1,0:T(8,128)} %bitcast.21), channel_id=1, source_target_pairs={{0,8},{4,36},{8,16},{12,44},{16,24},{20,52},{24,0},{28,60},{32,40}... | collective-permute-start | bytes 294920 | tf_op jit(solution)/shard_map/ppermute | solution.py:403
  2.4 15.1 %collective-permute-start.2 = (f32[1,3,64,128]{3,2,1,0:T(8,128)}, f32[1,3,64,128]{3,2,1,0:T(8,128)S(1)}, u32[]{:S(2)}, u32[]{:S(2)}) collective-permute-start(f32[1,3,64,128]{3,2,1,0:T(8,128)} %bitcast.22), channel_id=1, source_target_pairs={{0,16},{4,68},{8,24},{12,76},{16,0},{20,84},{24,8},{28,92},{32,48}... | collective-permute-start | bytes 294920 | tf_op jit(solution)/shard_map/ppermute | solution.py:403
  5.3 12.2 %collective-permute-start.3 = (f32[1,3,64,128]{3,2,1,0:T(8,128)}, f32[1,3,64,128]{3,2,1,0:T(8,128)S(1)}, u32[]{:S(2)}, u32[]{:S(2)}) collective-permute-start(f32[1,3,64,128]{3,2,1,0:T(8,128)} %bitcast.23), channel_id=1, source_target_pairs={{0,24},{4,100},{8,0},{12,108},{16,8},{20,116},{24,16},{28,124},{32... | collective-permute-start | bytes 294920 | tf_op jit(solution)/shard_map/ppermute | solution.py:403
  15.4 2.2 %collective-permute-start = (f32[16,1,64,128]{3,2,1,0:T(8,128)}, f32[16,1,64,128]{3,2,1,0:T(8,128)S(1)}, u32[]{:S(2)}, u32[]{:S(2)}) collective-permute-start(f32[16,1,64,128]{3,2,1,0:T(8,128)} %get-tuple-element.13), channel_id=1, source_target_pairs={{0,4},{4,0},{8,12},{12,8},{16,20},{20,16},{24,28},{28,24},{32,36},... | collective-permute-start | bytes 1572872 | tf_op jit(solution)/shard_map/ppermute | solution.py:402
  17.4 0.6 copy-start.12
  17.5 0.6 copy-start.13
  17.5 0.7 copy-start.14
  17.6 0.8 copy-start.7
  20.7 10.3 %collective-permute-start.4 = (f32[4,3,64,128]{3,2,1,0:T(8,128)}, f32[4,3,64,128]{3,2,1,0:T(8,128)S(1)}, u32[]{:S(2)}, u32[]{:S(2)}) collective-permute-start(f32[4,3,64,128]{3,2,1,0:T(8,128)} %get-tuple-element.14.refs_0_), channel_id=1, source_target_pairs={{0,32},{4,12},{8,40},{12,20},{16,48},{20,28},{24,56},{28,4},{32,64... | collective-permute-start | bytes 1179656 | tf_op jit(solution)/shard_map/ppermute | solution.py:412
  22.2 12.9 %collective-permute-start.5 = (f32[4,3,64,128]{3,2,1,0:T(8,128)}, f32[4,3,64,128]{3,2,1,0:T(8,128)S(1)}, u32[]{:S(2)}, u32[]{:S(2)}) collective-permute-start(f32[4,3,64,128]{3,2,1,0:T(8,128)} %get-tuple-element.14.refs_0_), channel_id=1, source_target_pairs={{0,64},{4,20},{8,72},{12,28},{16,80},{20,4},{24,88},{28,12},{32,96... | collective-permute-start | bytes 1179656 | tf_op jit(solution)/shard_map/ppermute | solution.py:412
  24.9 12.7 %collective-permute-start.6 = (f32[4,3,64,128]{3,2,1,0:T(8,128)}, f32[4,3,64,128]{3,2,1,0:T(8,128)S(1)}, u32[]{:S(2)}, u32[]{:S(2)}) collective-permute-start(f32[4,3,64,128]{3,2,1,0:T(8,128)} %get-tuple-element.14.refs_0_), channel_id=1, source_target_pairs={{0,96},{4,28},{8,104},{12,4},{16,112},{20,12},{24,120},{28,20},{32... | collective-permute-start | bytes 1179656 | tf_op jit(solution)/shard_map/ppermute | solution.py:412
  27.2 15.9 %all-to-all-start = ((f32[16,1,64,128]{3,2,1,0:T(8,128)}), f32[16,1,64,128]{3,2,1,0:T(8,128)S(1)}, u32[]{:S(2)}, u32[]{:S(2)}) async-start(f32[16,1,64,128]{3,2,1,0:T(8,128)} %get-tuple-element.15), calls=%async_computation | async-start | bytes 1048576 | tf_op jit(solution)/shard_map/all_to_all | solution.py:381
  30.9 11.0 %collective-permute-start.7 = (f32[4,3,64,128]{3,2,1,0:T(8,128)}, f32[4,3,64,128]{3,2,1,0:T(8,128)S(1)}, u32[]{:S(2)}, u32[]{:S(2)}) collective-permute-start(f32[4,3,64,128]{3,2,1,0:T(8,128)} %get-tuple-element.14.refs_0_), channel_id=1, source_target_pairs={{0,4},{4,0},{8,12},{12,8},{16,20},{20,16},{24,28},{28,24},{32,36},... | collective-permute-start | bytes 1179656 | tf_op jit(solution)/shard_map/ppermute | solution.py:424
  31.0 16.0 %copy-start.9 = (f32[4,3,64,128]{3,2,1,0:T(8,128)}, f32[4,3,64,128]{3,2,1,0:T(8,128)S(1)}, u32[]{:S(2)}) copy-start(f32[4,3,64,128]{3,2,1,0:T(8,128)S(1)} %collective-permute-done.4.refs_1_) | copy-start | bytes 1179652
  31.0 12.0 %collective-permute-start.8 = (f32[4,3,64,128]{3,2,1,0:T(8,128)S(1)}, f32[4,3,64,128]{3,2,1,0:T(8,128)S(1)}, u32[]{:S(2)}, u32[]{:S(2)}) collective-permute-start(f32[4,3,64,128]{3,2,1,0:T(8,128)S(1)} %collective-permute-done.4.refs_1_), channel_id=1, source_target_pairs={{0,4},{4,0},{8,12},{12,8},{16,20},{20,16},{24,28},{28,24},{32,36},... | collective-permute-start | bytes 1179656 | tf_op jit(solution)/shard_map/ppermute | solution.py:424
  35.1 17.1 %copy-start.10 = (f32[4,3,64,128]{3,2,1,0:T(8,128)}, f32[4,3,64,128]{3,2,1,0:T(8,128)S(1)}, u32[]{:S(2)}) copy-start(f32[4,3,64,128]{3,2,1,0:T(8,128)S(1)} %collective-permute-done.5.refs_2_) | copy-start | bytes 1179652
  35.1 7.9 %collective-permute-start.9 = (f32[4,3,64,128]{3,2,1,0:T(8,128)S(1)}, f32[4,3,64,128]{3,2,1,0:T(8,128)S(1)}, u32[]{:S(2)}, u32[]{:S(2)}) collective-permute-start(f32[4,3,64,128]{3,2,1,0:T(8,128)S(1)} %collective-permute-done.5.refs_2_), channel_id=1, source_target_pairs={{0,4},{4,0},{8,12},{12,8},{16,20},{20,16},{24,28},{28,24},{32,36},... | collective-permute-start | bytes 1179656 | tf_op jit(solution)/shard_map/ppermute | solution.py:424
  37.6 14.7 %copy-start.11 = (f32[4,3,64,128]{3,2,1,0:T(8,128)}, f32[4,3,64,128]{3,2,1,0:T(8,128)S(1)}, u32[]{:S(2)}) copy-start(f32[4,3,64,128]{3,2,1,0:T(8,128)S(1)} %collective-permute-done.6.refs_3_) | copy-start | bytes 1179652
  37.6 5.5 %collective-permute-start.10 = (f32[4,3,64,128]{3,2,1,0:T(8,128)S(1)}, f32[4,3,64,128]{3,2,1,0:T(8,128)S(1)}, u32[]{:S(2)}, u32[]{:S(2)}) collective-permute-start(f32[4,3,64,128]{3,2,1,0:T(8,128)S(1)} %collective-permute-done.6.refs_3_), channel_id=1, source_target_pairs={{0,4},{4,0},{8,12},{12,8},{16,20},{20,16},{24,28},{28,24},{32,36},... | collective-permute-start | bytes 1179656 | tf_op jit(solution)/shard_map/ppermute | solution.py:424
  41.9 1.2 copy-start.3
  43.0 0.8 copy-start.2
  43.0 0.9 copy-start.4
  43.1 1.0 copy-start.5
  44.1 0.7 copy-start.6
  47.0 25.1 %all-to-all-start.1 = ((f32[32,1,64,128]{3,2,1,0:T(8,128)}), f32[32,1,64,128]{3,2,1,0:T(8,128)S(1)}, u32[]{:S(2)}, u32[]{:S(2)}) async-start(f32[32,1,64,128]{3,2,1,0:T(8,128)} %get-tuple-element.17), calls=%async_computation.1 | async-start | bytes 2097152 | tf_op jit(solution)/shard_map/all_to_all | solution.py:433
  72.1 1.0 copy-start
  93.7 3.7 %collective-permute-start.15 = (f32[16,3,64,128]{3,2,1,0:T(8,128)}, f32[16,3,64,128]{3,2,1,0:T(8,128)S(1)}, u32[]{:S(2)}, u32[]{:S(2)}) collective-permute-start(f32[16,3,64,128]{3,2,1,0:T(8,128)} %get-tuple-element.20), channel_id=1, source_target_pairs={{0,4},{4,0},{8,12},{12,8},{16,20},{20,16},{24,28},{28,24},{32,36},... | collective-permute-start | bytes 4718600 | tf_op jit(solution)/shard_map/ppermute | solution.py:469
  100.2 7.1 %copy-start.15 = (f32[1,64,128]{2,1,0:T(8,128)S(1)}, f32[1,64,128]{2,1,0:T(8,128)}, u32[]{:S(2)}) copy-start(f32[1,64,128]{2,1,0:T(8,128)} %get-tuple-element.18) | copy-start | bytes 98308
  100.2 7.1 %copy-start.1 = (f32[3,4,16,128]{3,2,1,0:T(8,128)S(1)}, f32[3,4,16,128]{3,2,1,0:T(8,128)}, u32[]{:S(2)}) copy-start(f32[3,4,16,128]{3,2,1,0:T(8,128)} %param.7) | copy-start | bytes 294916
  100.2 7.1 %copy-start.8 = (f32[4,16,128]{2,1,0:T(8,128)S(1)}, f32[4,16,128]{2,1,0:T(8,128)}, u32[]{:S(2)}) copy-start(f32[4,16,128]{2,1,0:T(8,128)} %param.8) | copy-start | bytes 98308
  100.2 31.5 %all-to-all-start.2 = ((f32[16,3,64,128]{3,2,1,0:T(8,128)}), f32[16,3,64,128]{3,2,1,0:T(8,128)S(1)}, u32[]{:S(2)}, u32[]{:S(2)}) async-start(f32[16,3,64,128]{3,2,1,0:T(8,128)} %add.150), calls=%async_computation.2 | async-start | bytes 3145728 | tf_op jit(solution)/shard_map/all_to_all | solution.py:381
  107.4 10.4 %collective-permute-start.14 = (f32[5,4,1,128]{3,2,1,0:T(1,128)S(1)}, f32[5,4,1,128]{3,2,1,0:T(1,128)S(1)}, u32[]{:S(2)}, u32[]{:S(2)}) collective-permute-start(f32[5,4,1,128]{3,2,1,0:T(1,128)S(1)} %get-tuple-element.34), channel_id=1, source_target_pairs={{0,1},{1,2},{2,3},{4,5},{5,6},{6,7},{8,9},{9,10},{10,11},{12,13},{... | collective-permute-start | bytes 30728 | tf_op jit(solution)/shard_map/ppermute | solution.py:340
  111.2 6.6 %collective-permute-start.13 = (f32[5,4,1,128]{3,2,1,0:T(1,128)S(1)}, f32[5,4,1,128]{3,2,1,0:T(1,128)S(1)}, u32[]{:S(2)}, u32[]{:S(2)}) collective-permute-start(f32[5,4,1,128]{3,2,1,0:T(1,128)S(1)} %get-tuple-element.33), channel_id=1, source_target_pairs={{1,0},{2,1},{3,2},{5,4},{6,5},{7,6},{9,8},{10,9},{11,10},{13,12},{... | collective-permute-start | bytes 30728 | tf_op jit(solution)/shard_map/ppermute | solution.py:341
  112.6 17.2 %collective-permute-start.12 = (f32[5,1,16,128]{3,2,1,0:T(8,128)S(1)}, f32[5,1,16,128]{3,2,1,0:T(8,128)S(1)}, u32[]{:S(2)}, u32[]{:S(2)}) collective-permute-start(f32[5,1,16,128]{3,2,1,0:T(8,128)S(1)} %get-tuple-element.32), channel_id=1, source_target_pairs={{0,4},{4,8},{8,12},{12,16},{16,20},{20,24},{24,28},{28,32},{32,36}... | collective-permute-start | bytes 122888 | tf_op jit(solution)/shard_map/ppermute | solution.py:340
  112.7 17.1 %collective-permute-start.11 = (f32[5,1,16,128]{3,2,1,0:T(8,128)S(1)}, f32[5,1,16,128]{3,2,1,0:T(8,128)S(1)}, u32[]{:S(2)}, u32[]{:S(2)}) collective-permute-start(f32[5,1,16,128]{3,2,1,0:T(8,128)S(1)} %get-tuple-element.31), channel_id=1, source_target_pairs={{4,0},{8,4},{12,8},{16,12},{20,16},{24,20},{28,24},{32,28},{36,32}... | collective-permute-start | bytes 122888 | tf_op jit(solution)/shard_map/ppermute | solution.py:341

commit v4 on v3

--- a/solution.py
+++ b/solution.py
@@ -90,8 +90,9 @@
 
 
 def deposit_kernel(
-    slot_ref, cell_ref, vol_ref, same_ref, other_ref, sum_ref, words_ref, sems
+    dest_ref, core_ref, cell_ref, vol_ref, same_ref, other_ref, sum_ref, words_ref, sems
 ):
+    near, core = same_ref.shape[0], core_ref[0]
     sum_ref[...] = jnp.zeros_like(sum_ref)
     blocks = cell_ref.shape[0]
     for g in range(blocks // 256):
@@ -112,7 +113,8 @@
                     left = weighted_rows(row(cell_ref, b), [row(vol_ref, b)], rows)
                     got.append((b, jnp.dot(left, hots[s], preferred_element_type=F32)))
             for b, res in got:
-                add_to(sum_ref, slot_ref[b], res, 1)
+                d = dest_ref[b]
+                add_to(sum_ref, ((d & 1) ^ core) * near + (d >> 1), res, 1)
         return carry
 
     lax.fori_loop(0, blocks // 256, step, 0)
@@ -198,25 +200,50 @@
     return values[0]
 
 
-def pick_rows(slot_ref, cell_ref, table_ref, fields, out_ref, groups):
+def pick_rows(place_ref, cell_ref, table_ref, pieces_ref, out_ref, by_product):
     blocks = cell_ref.shape[0]
+    fields, tile_rows = table_ref.shape[1:3]
+    groups = 8
     sub = lax.broadcasted_iota(I32, (8, LANES), 0)
+    columns = lax.broadcasted_iota(I32, (LANES, LANES), 0).astype(I16)
+    one, zero = jnp.ones((), BF), jnp.zeros((), BF)
+    multiplied = [f for f in range(fields) if any(by_product(f, s) for s in range(8))]
+
+    def prepare(d, carry):
+        for i, f in enumerate(multiplied):
+            high, low = two_parts(table_ref[d, f])
+            pieces_ref[d, i, 0:tile_rows, :] = high
+            pieces_ref[d, i, tile_rows : 2 * tile_rows, :] = low
+        return carry
+
+    lax.fori_loop(0, table_ref.shape[0], prepare, 0, unroll=8)
 
     def eight(base):
         picked = [[] for _ in range(fields)]
         for s in range(8):
-            d = slot_ref[base + s]
+            d = place_ref[base + s]
             cell = jnp.broadcast_to(row(cell_ref, base + s), (8, LANES))
             column, top, low = cell & 127, cell >> 10, (cell >> 7) & 7
+            if any(by_product(f, s) for f in range(fields)):
+                pair = jnp.concatenate([column, column], axis=0).astype(I16)
+                hot = jnp.where(columns == jnp.concatenate([pair] * 8, axis=0), one, zero)
             for f in range(fields):
                 acc = None
-                for q in range(table_ref.shape[2] // 8):
-                    got = jnp.take_along_axis(
-                        table_ref[d, f, 8 * q : 8 * q + 8, :],
-                        column,
-                        axis=1,
-                        mode="promise_in_bounds",
+                if by_product(f, s):
+                    both = jnp.dot(
+                        pieces_ref[d, multiplied.index(f)], hot, preferred_element_type=F32
                     )
+                for q in range(tile_rows // 8):
+                    at = 8 * q
+                    if by_product(f, s):
+                        got = both[at : at + 8] + both[tile_rows + at : tile_rows + at + 8]
+                    else:
+                        got = jnp.take_along_axis(
+                            table_ref[d, f, at : at + 8, :],
+                            column,
+                            axis=1,
+                            mode="promise_in_bounds",
+                        )
                     acc = got if acc is None else jnp.where(top == q, got, acc)
                 picked[f].append(jnp.where(sub == low, acc, 0.0))
         for f in range(fields):
@@ -231,21 +258,21 @@
 
 
 def flow_kernel(slot_ref, cell_ref, *refs):
-    group_refs, (_, out_ref, table_ref, sems) = refs[:-4], refs[-4:]
+    group_refs, (_, out_ref, table_ref, pieces_ref, sems) = refs[:-5], refs[-5:]
     size = group_refs[0].shape[0]
     wait_all(
         start_all(
             [(ref, table_ref.at[pl.ds(i * size, size)]) for i, ref in enumerate(group_refs)], sems
         )
     )
-    pick_rows(slot_ref, cell_ref, table_ref, out_ref.shape[0], out_ref, 4)
+    pick_rows(slot_ref, cell_ref, table_ref, pieces_ref, out_ref, lambda f, s: f > 0)
 
 
 def particle_kernel(
     dest_ref, block_ref, pair_ref, cell_ref, words_ref, vol_any, drag_any, vel_any, here_any,
     solid_any, tile_any,
     new_any, same_any, other_any, late_any,
-    table_ref, solid_ref, vol_ref, drag_ref, vel_ref, here_ref, new_ref, push_ref, sum_ref, sems,
+    table_ref, pieces_ref, solid_ref, vol_ref, drag_ref, vel_ref, here_ref, new_ref, push_ref, sum_ref, sems,
 ):
     tables = start_all([(solid_any, table_ref)], sems)
     rest = [
@@ -260,7 +287,7 @@
         copy.start()
     sum_ref[...] = jnp.zeros_like(sum_ref)
     wait_all(tables)
-    pick_rows(dest_ref, cell_ref, table_ref, 1, solid_ref, 4)
+    pick_rows(dest_ref, cell_ref, table_ref, pieces_ref, solid_ref, lambda f, s: s % 2 == 0)
     wait_all(others)
     blocks = cell_ref.shape[0]
     size = 32
@@ -387,7 +414,7 @@
     dep_same, dep_other = pl.pallas_call(
         deposit_kernel,
         out_shape=(one_sum, one_sum),
-        in_specs=[SMEM_SPEC] + [VMEM_SPEC] * 2,
+        in_specs=[SMEM_SPEC] * 2 + [VMEM_SPEC] * 2,
         out_specs=(ANY_SPEC, ANY_SPEC),
         scratch_shapes=[
             pltpu.VMEM((size, 1, tile_rows, radial), F32),
@@ -396,7 +423,7 @@
         ],
         compiler_params=PARAMS,
         cost_estimate=cost(7),
-    )(slot, cell_of, part_vol)
+    )(dest, core.reshape(1), cell_of, part_vol)
 
     steps = range(1, SIDE)
     dep_twin = lax.ppermute(dep_other, "azim", twin)
@@ -437,7 +464,11 @@
         out_shape=arrays(3, blocks, block_rows),
         in_specs=[SMEM_SPEC, VMEM_SPEC] + [ANY_SPEC] * (2 * SIDE + 1),
         out_specs=VMEM_SPEC,
-        scratch_shapes=[pltpu.VMEM((size, 3, tile_rows, radial), F32), dma(2 * SIDE)],
+        scratch_shapes=[
+            pltpu.VMEM((size, 3, tile_rows, radial), F32),
+            pltpu.VMEM((size, 2, 2 * tile_rows, radial), BF),
+            dma(2 * SIDE),
+        ],
         compiler_params=PARAMS,
         cost_estimate=cost(18),
     )(place_of(dest, lax.axis_index("azim")), cell_of, *groups, solid_flat)
@@ -450,6 +481,7 @@
         out_specs=(ANY_SPEC,) * 4,
         scratch_shapes=[
             pltpu.VMEM((size, 1, tile_rows, radial), F32),
+            pltpu.VMEM((size, 1, 2 * tile_rows, radial), BF),
             pltpu.VMEM((1, blocks, block_rows), F32),
             pltpu.VMEM((blocks, block_rows), F32),
             pltpu.VMEM((blocks, block_rows), F32),

time: 133 us -> 124 us (0.932)
  Pallas kernels: 55.9 us -> 47 us
  starting transfers between devices: 40.9 us -> 38.8 us
  waiting for transfers between devices: 22.6 us -> 24.6 us
    pallas_call x1, Pallas kernels: 19.8 us -> 14.2 us  [on_device(): pl.pallas_call(flow_kernel, out_shape=arrays(3, blocks, block_rows), in_s...]
    pallas_call x1, Pallas kernels: 20.6 us -> 17.3 us  [on_device(): pl.pallas_call(particle_kernel, out_shape=(arrays(*three), three_sums, th...]
    all_to_all x2, starting transfers between devices: 10.6 us -> 8.18 us  [to_owners(): lax.all_to_all(parts, 'azim', split_axis=0, concat_axis=0, tiled=True, ax...]
    all_to_all x1, waiting for transfers between devices: 0.01 us -> 2.43 us  [on_device(): lax.all_to_all(solid_tiles, 'azim', split_axis=0, concat_axis=0, tiled=True)]
  transfers between devices with their start and end apart: 19 -> 19, of which waited for: 7 -> 7; matrix products, arithmetic and copies ran while one was open for 4% -> 3% of each run, Pallas kernels for 23% -> 21%
where the time goes in v4:
time: 124 us; the launch traced here: 123 us
  Pallas kernels  47 us (38%)
  starting transfers between devices  38.8 us (31%)
  waiting for transfers between devices  24.6 us (20%)
  other arithmetic  7.95 us (6%)
  local copies, waits for them, and re-layouts  3.61 us (3%)
    pallas_call x1, Pallas kernels, on_device(): pl.pallas_call(particle_kernel, out_shape=(arrays(*three), three_sums, th...  17.3 us
    pallas_call x1, Pallas kernels, on_device(): pl.pallas_call(flow_kernel, out_shape=arrays(3, blocks, block_rows), in_s...  14.2 us
    ppermute x2, waiting for transfers between devices, padded_2(): before = lax.ppermute(last, axis, up)  12 us
    all_to_all x2, starting transfers between devices, to_owners(): lax.all_to_all(parts, 'azim', split_axis=0, concat_axis=0, tiled=True, ax...  8.18 us
    pallas_call x1, Pallas kernels, on_device(): pl.pallas_call(deposit_kernel, out_shape=(one_sum, one_sum), in_specs=[SM...  7.51 us
    ppermute x2, starting transfers between devices, padded_2(): after = lax.ppermute(first, axis, down)  6.34 us
    ppermute x3, starting transfers between devices, on_device(): lax.ppermute(flow_tile, 'azim', along(0, k))  5.98 us
    ppermute x3, starting transfers between devices, on_device(): groups = [first] + [lax.ppermute(first, 'azim', along(1, k)) for k in steps]  5.66 us
  transfers between devices with their start and end apart: 19, of which 7 were waited for; matrix products, arithmetic and copies ran while one was open for 3% of the time, Pallas kernels for 21%

profile of v4, /device:TPU:0, one launch (start us, length us, event | category | flops | bytes accessed | tf_op | source)
XLA Modules:
  0.0 122.9 jit_solution(17447111505751903283)
XLA Ops:
  0.6 1.7 %collective-permute-start.1 = (f32[1,3,64,128]{3,2,1,0:T(8,128)}, f32[1,3,64,128]{3,2,1,0:T(8,128)S(1)}, u32[]{:S(2)}, u32[]{:S(2)}) collective-permute-start(f32[1,3,64,128]{3,2,1,0:T(8,128)} %bitcast.22), channel_id=1, source_target_pairs={{0,8},{4,36},{8,16},{12,44},{16,24},{20,52},{24,0},{28,60},{32,40}... | collective-permute-start | bytes 294920 | tf_op jit(solution)/shard_map/ppermute | solution.py:430
  2.4 2.9 %collective-permute-start.2 = (f32[1,3,64,128]{3,2,1,0:T(8,128)}, f32[1,3,64,128]{3,2,1,0:T(8,128)S(1)}, u32[]{:S(2)}, u32[]{:S(2)}) collective-permute-start(f32[1,3,64,128]{3,2,1,0:T(8,128)} %bitcast.23), channel_id=1, source_target_pairs={{0,16},{4,68},{8,24},{12,76},{16,0},{20,84},{24,8},{28,92},{32,48}... | collective-permute-start | bytes 294920 | tf_op jit(solution)/shard_map/ppermute | solution.py:430
  5.3 1.3 %collective-permute-start.3 = (f32[1,3,64,128]{3,2,1,0:T(8,128)}, f32[1,3,64,128]{3,2,1,0:T(8,128)S(1)}, u32[]{:S(2)}, u32[]{:S(2)}) collective-permute-start(f32[1,3,64,128]{3,2,1,0:T(8,128)} %bitcast.24), channel_id=1, source_target_pairs={{0,24},{4,100},{8,0},{12,108},{16,8},{20,116},{24,16},{28,124},{32... | collective-permute-start | bytes 294920 | tf_op jit(solution)/shard_map/ppermute | solution.py:430
  6.6 7.5 %shard_map.87 = (f32[16,1,64,128]{3,2,1,0:T(8,128)}, f32[16,1,64,128]{3,2,1,0:T(8,128)}) custom-call(s32[512]{0:T(512)} %bitcast.38, s32[1]{0:T(128)} %bitcast.3.core_ref, s32[512,128]{1,0:T(8,128)} %cell_ref.7, f32[512,128]{1,0:T(8,128)} %vol_any.1), custom_call_target="tpu_custom_call" | custom-call | bytes 21000000 | tf_op jit(solution)/shard_map/pallas_call | solution.py:414
  14.1 0.1 collective-permute-start
  14.2 0.7 shift-right-arithmetic_add_fusion
  14.9 0.1 convert_reduce_fusion.1
  15.0 0.1 select_reduce_fusion.1
  15.1 1.3 %select_add_fusion = (s32[512]{0:T(512)}, s32[512]{0:T(512)S(1)}) fusion(s32[512]{0:T(512)} %bitcast.39, s32[]{:T(128)S(6)} %select_n.57, s32[]{:T(128)S(6)} %select_n.54, s32[]{:T(128)S(6)} %and.69, s32[]{:T(128)} %select_n.50), kind=kLoop, calls=%fused_computation.98 | loop fusion | flops 31744 | bytes 6160 | tf_op jit(solution)/shard_map/add | solution.py:390
  16.4 0.3 convert_reduce_fusion
  16.8 0.0 collective-permute-done.1.refs_1_
  16.8 0.0 copy-start.12
  16.8 0.0 collective-permute-done.other_ref
  16.8 0.6 copy-done.12
  17.4 0.0 copy-done.13
  17.4 0.0 copy-done.14
  17.5 0.2 copy-done.7
  17.7 2.3 %shard_map.88 = (f32[16,1,64,128]{3,2,1,0:T(8,128)}, f32[4,3,64,128]{3,2,1,0:T(8,128)}) custom-call(f32[16,1,64,128]{3,2,1,0:T(8,128)} %get-tuple-element.12.same_ref, f32[16,1,64,128]{3,2,1,0:T(8,128)} %copy-done.7, f32[1,3,64,128]{3,2,1,0:T(8,128)} %bitcast.25, f32[1,3,64,128]{3,2,1,0:T(8,128)} %copy-done.12, f32[1,3,64,128]{3,2,1,0:T(8,128)} %copy-done.13, ...), custom_call_target="tpu_custom_call" | custom-call | bytes 6000000 | tf_op jit(solution)/shard_map/pallas_call | solution.py:431
  20.0 1.5 %collective-permute-start.4 = (f32[4,3,64,128]{3,2,1,0:T(8,128)}, f32[4,3,64,128]{3,2,1,0:T(8,128)S(1)}, u32[]{:S(2)}, u32[]{:S(2)}) collective-permute-start(f32[4,3,64,128]{3,2,1,0:T(8,128)} %get-tuple-element.14.refs_0_), channel_id=1, source_target_pairs={{0,32},{4,12},{8,40},{12,20},{16,48},{20,28},{24,56},{28,4},{32,64... | collective-permute-start | bytes 1179656 | tf_op jit(solution)/shard_map/ppermute | solution.py:439
  21.5 2.7 %collective-permute-start.5 = (f32[4,3,64,128]{3,2,1,0:T(8,128)}, f32[4,3,64,128]{3,2,1,0:T(8,128)S(1)}, u32[]{:S(2)}, u32[]{:S(2)}) collective-permute-start(f32[4,3,64,128]{3,2,1,0:T(8,128)} %get-tuple-element.14.refs_0_), channel_id=1, source_target_pairs={{0,64},{4,20},{8,72},{12,28},{16,80},{20,4},{24,88},{28,12},{32,96... | collective-permute-start | bytes 1179656 | tf_op jit(solution)/shard_map/ppermute | solution.py:439
  24.2 1.4 %collective-permute-start.6 = (f32[4,3,64,128]{3,2,1,0:T(8,128)}, f32[4,3,64,128]{3,2,1,0:T(8,128)S(1)}, u32[]{:S(2)}, u32[]{:S(2)}) collective-permute-start(f32[4,3,64,128]{3,2,1,0:T(8,128)} %get-tuple-element.14.refs_0_), channel_id=1, source_target_pairs={{0,96},{4,28},{8,104},{12,4},{16,112},{20,12},{24,120},{28,20},{32... | collective-permute-start | bytes 1179656 | tf_op jit(solution)/shard_map/ppermute | solution.py:439
  25.6 0.2 select_reduce_fusion
  25.8 0.6 broadcast_add_fusion.1.block_ref
  26.4 3.6 %all-to-all-start = ((f32[16,1,64,128]{3,2,1,0:T(8,128)}), f32[16,1,64,128]{3,2,1,0:T(8,128)S(1)}, u32[]{:S(2)}, u32[]{:S(2)}) async-start(f32[16,1,64,128]{3,2,1,0:T(8,128)} %get-tuple-element.15), calls=%async_computation | async-start | bytes 1048576 | tf_op jit(solution)/shard_map/all_to_all | solution.py:408
  30.0 0.1 select_reduce_fusion.2
  30.1 0.2 collective-permute-start.7
  30.3 0.0 collective-permute-done.4.refs_1_
  30.4 2.7 %collective-permute-start.8 = (f32[4,3,64,128]{3,2,1,0:T(8,128)S(1)}, f32[4,3,64,128]{3,2,1,0:T(8,128)S(1)}, u32[]{:S(2)}, u32[]{:S(2)}) collective-permute-start(f32[4,3,64,128]{3,2,1,0:T(8,128)S(1)} %collective-permute-done.4.refs_1_), channel_id=1, source_target_pairs={{0,4},{4,0},{8,12},{12,8},{16,20},{20,16},{24,28},{28,24},{32,36},... | collective-permute-start | bytes 1179656 | tf_op jit(solution)/shard_map/ppermute | solution.py:451
  33.0 1.4 %collective-permute-done.5.refs_2_ = f32[4,3,64,128]{3,2,1,0:T(8,128)S(1)} collective-permute-done((f32[4,3,64,128]{3,2,1,0:T(8,128)}, f32[4,3,64,128]{3,2,1,0:T(8,128)S(1)}, u32[]{:S(2)}, u32[]{:S(2)}) %collective-permute-start.5) | collective-permute-done | bytes 393248 | tf_op jit(solution)/shard_map/ppermute | solution.py:439
  34.4 2.5 %collective-permute-done.6.refs_3_ = f32[4,3,64,128]{3,2,1,0:T(8,128)S(1)} collective-permute-done((f32[4,3,64,128]{3,2,1,0:T(8,128)}, f32[4,3,64,128]{3,2,1,0:T(8,128)S(1)}, u32[]{:S(2)}, u32[]{:S(2)}) %collective-permute-start.6) | collective-permute-done | bytes 393248 | tf_op jit(solution)/shard_map/ppermute | solution.py:439
  36.9 0.0 collective-permute-start.10
  36.9 3.6 %shard_map.86.refs_0_.words_ref = s32[4,128,128]{2,1,0:T(8,128)} custom-call(s32[544]{0:T(1024)} %broadcast_add_fusion.1.block_ref, s32[512,128]{1,0:T(8,128)} %cell_ref.7), custom_call_target="tpu_custom_call" | custom-call | bytes 6000000 | tf_op jit(solution)/shard_map/pallas_call | solution.py:441
  40.5 0.1 convert_reduce_fusion.2
  40.6 0.6 broadcast_minimum_fusion.refs_1_.pair_ref
  41.2 0.0 collective-permute-done.7.refs_2_.refs_4_
  41.2 1.2 %all-to-all-done.got_ref = f32[16,1,64,128]{3,2,1,0:T(8,128)S(1)} async-done(((f32[16,1,64,128]{3,2,1,0:T(8,128)}), f32[16,1,64,128]{3,2,1,0:T(8,128)S(1)}, u32[]{:S(2)}, u32[]{:S(2)}) %all-to-all-start) | async-done | bytes 524320 | tf_op jit(solution)/shard_map/all_to_all | solution.py:408
  42.4 0.0 collective-permute-done.8.refs_3_.refs_5_
  42.4 0.0 collective-permute-done.9.refs_4_.refs_6_
  42.4 0.0 collective-permute-done.10.refs_5_.refs_7_
  42.4 0.7 copy-done.2
  43.2 0.1 copy-done.4
  43.3 0.1 copy-done.5
  43.5 0.7 copy-done.6
  44.2 2.2 %shard_map.89 = (f32[1,64,128]{2,1,0:T(8,128)}, f32[32,1,64,128]{3,2,1,0:T(8,128)}) custom-call(f32[16,1,64,128]{3,2,1,0:T(8,128)} %copy-done.2, s32[4,128,128]{2,1,0:T(8,128)} %shard_map.86.refs_0_.words_ref, s32[272]{0:T(512)} %broadcast_minimum_fusion.refs_1_.pair_ref, f32[4,3,64,128]{3,2,1,0:T(8,128)} %copy-done.3, f32[4,3,64,128]{3,2,1,0:T(8,128)} %copy-done.4, ...), custom_call_target="tpu_custom_call" | custom-call | bytes 6000000 | tf_op jit(solution)/shard_map/pallas_call | solution.py:452
  46.4 5.2 %all-to-all-start.1 = ((f32[32,1,64,128]{3,2,1,0:T(8,128)}), f32[32,1,64,128]{3,2,1,0:T(8,128)S(1)}, u32[]{:S(2)}, u32[]{:S(2)}) async-start(f32[32,1,64,128]{3,2,1,0:T(8,128)} %get-tuple-element.17), calls=%async_computation.1 | async-start | bytes 2097152 | tf_op jit(solution)/shard_map/all_to_all | solution.py:460
  51.6 14.2 %shard_map.90.here_any = f32[3,512,128]{2,1,0:T(8,128)} custom-call(s32[512]{0:T(512)} %get-tuple-element.37.slot_ref, s32[512,128]{1,0:T(8,128)} %cell_ref.7, f32[4,3,64,128]{3,2,1,0:T(8,128)} %get-tuple-element.14.refs_0_, f32[4,3,64,128]{3,2,1,0:T(8,128)} %copy-done.9, f32[4,3,64,128]{3,2,1,0:T(8,128)} %copy-done.10, f32[4,3,64,128]{3,2,1,0:T(8,128)} %copy-done.11, ...), custom_call_target="tpu_custom_call" | custom-call | bytes 54000000 | tf_op jit(solution)/shard_map/pallas_call | solution.py:462
  65.8 2.4 %all-to-all-done.1.solid_any = f32[32,1,64,128]{3,2,1,0:T(8,128)S(1)} async-done(((f32[32,1,64,128]{3,2,1,0:T(8,128)}), f32[32,1,64,128]{3,2,1,0:T(8,128)S(1)}, u32[]{:S(2)}, u32[]{:S(2)}) %all-to-all-start.1) | async-done | bytes 1048608 | tf_op jit(solution)/shard_map/all_to_all | solution.py:460
  68.3 1.0 copy-done
  69.2 17.3 %shard_map.91 = (f32[3,512,128]{2,1,0:T(8,128)}, f32[16,3,64,128]{3,2,1,0:T(8,128)}, f32[16,3,64,128]{3,2,1,0:T(8,128)}, f32[1,64,128]{2,1,0:T(8,128)}) custom-call(s32[512]{0:T(512)} %bitcast.40, s32[544]{0:T(1024)} %broadcast_add_fusion.1.block_ref, s32[272]{0:T(512)} %broadcast_minimum_fusion.refs_1_.pair_ref, s32[512,128]{1,0:T(8,128)} %cell_ref.7, ...), custom_call_target="tpu_custom_call" | custom-call | bytes 60000000 | tf_op jit(solution)/shard_map/pallas_call | solution.py:477
  86.5 0.5 collective-permute-start.15
  87.0 3.2 %collective-permute-done.15 = f32[16,3,64,128]{3,2,1,0:T(8,128)S(1)} collective-permute-done((f32[16,3,64,128]{3,2,1,0:T(8,128)}, f32[16,3,64,128]{3,2,1,0:T(8,128)S(1)}, u32[]{:S(2)}, u32[]{:S(2)}) %collective-permute-start.15) | collective-permute-done | bytes 1572896 | tf_op jit(solution)/shard_map/ppermute | solution.py:501
  90.2 2.8 %add.155 = f32[16,3,64,128]{3,2,1,0:T(8,128)} add(f32[16,3,64,128]{3,2,1,0:T(8,128)} %get-tuple-element.19, f32[16,3,64,128]{3,2,1,0:T(8,128)S(1)} %collective-permute-done.15) | non-fusion elementwise | flops 393216 | bytes 4718592 | tf_op jit(solution)/shard_map/add | solution.py:501
  93.1 4.6 %all-to-all-start.2 = ((f32[16,3,64,128]{3,2,1,0:T(8,128)}), f32[16,3,64,128]{3,2,1,0:T(8,128)S(1)}, u32[]{:S(2)}, u32[]{:S(2)}) async-start(f32[16,3,64,128]{3,2,1,0:T(8,128)} %add.155), calls=%async_computation.2 | async-start | bytes 3145728 | tf_op jit(solution)/shard_map/all_to_all | solution.py:408
  97.8 3.9 %collective-permute-start.14 = (f32[5,4,1,128]{3,2,1,0:T(1,128)S(1)}, f32[5,4,1,128]{3,2,1,0:T(1,128)S(1)}, u32[]{:S(2)}, u32[]{:S(2)}) collective-permute-start(f32[5,4,1,128]{3,2,1,0:T(1,128)S(1)} %get-tuple-element.34), channel_id=1, source_target_pairs={{0,1},{1,2},{2,3},{4,5},{5,6},{6,7},{8,9},{9,10},{10,11},{12,13},{... | collective-permute-start | bytes 30728 | tf_op jit(solution)/shard_map/ppermute | solution.py:367
  101.6 1.3 %collective-permute-start.13 = (f32[5,4,1,128]{3,2,1,0:T(1,128)S(1)}, f32[5,4,1,128]{3,2,1,0:T(1,128)S(1)}, u32[]{:S(2)}, u32[]{:S(2)}) collective-permute-start(f32[5,4,1,128]{3,2,1,0:T(1,128)S(1)} %get-tuple-element.33), channel_id=1, source_target_pairs={{1,0},{2,1},{3,2},{5,4},{6,5},{7,6},{9,8},{10,9},{11,10},{13,12},{... | collective-permute-start | bytes 30728 | tf_op jit(solution)/shard_map/ppermute | solution.py:368
  102.9 0.1 fusion.23
  103.1 0.1 collective-permute-start.12
  103.1 5.1 %collective-permute-start.11 = (f32[5,1,16,128]{3,2,1,0:T(8,128)S(1)}, f32[5,1,16,128]{3,2,1,0:T(8,128)S(1)}, u32[]{:S(2)}, u32[]{:S(2)}) collective-permute-start(f32[5,1,16,128]{3,2,1,0:T(8,128)S(1)} %get-tuple-element.31), channel_id=1, source_target_pairs={{4,0},{8,4},{12,8},{16,12},{20,16},{24,20},{28,24},{32,28},{36,32}... | collective-permute-start | bytes 122888 | tf_op jit(solution)/shard_map/ppermute | solution.py:368
  108.2 0.0 collective-permute-done.14
  108.2 0.0 collective-permute-done.13
  108.2 12.0 %collective-permute-done.12 = f32[5,1,16,128]{3,2,1,0:T(8,128)S(1)} collective-permute-done((f32[5,1,16,128]{3,2,1,0:T(8,128)S(1)}, f32[5,1,16,128]{3,2,1,0:T(8,128)S(1)}, u32[]{:S(2)}, u32[]{:S(2)}) %collective-permute-start.12) | collective-permute-done | bytes 40992 | tf_op jit(solution)/shard_map/ppermute | solution.py:367
  120.2 1.8 %all-to-all-done.2 = f32[16,3,64,128]{3,2,1,0:T(8,128)S(1)} async-done(((f32[16,3,64,128]{3,2,1,0:T(8,128)}), f32[16,3,64,128]{3,2,1,0:T(8,128)S(1)}, u32[]{:S(2)}, u32[]{:S(2)}) %all-to-all-start.2) | async-done | bytes 1572896 | tf_op jit(solution)/shard_map/all_to_all | solution.py:408
  122.1 0.1 reduce_sum.69
  122.2 0.8 fusion.11
  (36 shorter events, 0.2 us)
Async XLA Ops:
  0.6 16.1 %collective-permute-start.1 = (f32[1,3,64,128]{3,2,1,0:T(8,128)}, f32[1,3,64,128]{3,2,1,0:T(8,128)S(1)}, u32[]{:S(2)}, u32[]{:S(2)}) collective-permute-start(f32[1,3,64,128]{3,2,1,0:T(8,128)} %bitcast.22), channel_id=1, source_target_pairs={{0,8},{4,36},{8,16},{12,44},{16,24},{20,52},{24,0},{28,60},{32,40}... | collective-permute-start | bytes 294920 | tf_op jit(solution)/shard_map/ppermute | solution.py:430
  2.4 14.4 %collective-permute-start.2 = (f32[1,3,64,128]{3,2,1,0:T(8,128)}, f32[1,3,64,128]{3,2,1,0:T(8,128)S(1)}, u32[]{:S(2)}, u32[]{:S(2)}) collective-permute-start(f32[1,3,64,128]{3,2,1,0:T(8,128)} %bitcast.23), channel_id=1, source_target_pairs={{0,16},{4,68},{8,24},{12,76},{16,0},{20,84},{24,8},{28,92},{32,48}... | collective-permute-start | bytes 294920 | tf_op jit(solution)/shard_map/ppermute | solution.py:430
  5.3 11.5 %collective-permute-start.3 = (f32[1,3,64,128]{3,2,1,0:T(8,128)}, f32[1,3,64,128]{3,2,1,0:T(8,128)S(1)}, u32[]{:S(2)}, u32[]{:S(2)}) collective-permute-start(f32[1,3,64,128]{3,2,1,0:T(8,128)} %bitcast.24), channel_id=1, source_target_pairs={{0,24},{4,100},{8,0},{12,108},{16,8},{20,116},{24,16},{28,124},{32... | collective-permute-start | bytes 294920 | tf_op jit(solution)/shard_map/ppermute | solution.py:430
  14.1 2.7 %collective-permute-start = (f32[16,1,64,128]{3,2,1,0:T(8,128)}, f32[16,1,64,128]{3,2,1,0:T(8,128)S(1)}, u32[]{:S(2)}, u32[]{:S(2)}) collective-permute-start(f32[16,1,64,128]{3,2,1,0:T(8,128)} %get-tuple-element.13), channel_id=1, source_target_pairs={{0,4},{4,0},{8,12},{12,8},{16,20},{20,16},{24,28},{28,24},{32,36},... | collective-permute-start | bytes 1572872 | tf_op jit(solution)/shard_map/ppermute | solution.py:429
  16.8 0.6 copy-start.12
  16.8 0.6 copy-start.13
  16.8 0.7 copy-start.14
  16.8 0.8 copy-start.7
  20.0 10.4 %collective-permute-start.4 = (f32[4,3,64,128]{3,2,1,0:T(8,128)}, f32[4,3,64,128]{3,2,1,0:T(8,128)S(1)}, u32[]{:S(2)}, u32[]{:S(2)}) collective-permute-start(f32[4,3,64,128]{3,2,1,0:T(8,128)} %get-tuple-element.14.refs_0_), channel_id=1, source_target_pairs={{0,32},{4,12},{8,40},{12,20},{16,48},{20,28},{24,56},{28,4},{32,64... | collective-permute-start | bytes 1179656 | tf_op jit(solution)/shard_map/ppermute | solution.py:439
  21.5 12.9 %collective-permute-start.5 = (f32[4,3,64,128]{3,2,1,0:T(8,128)}, f32[4,3,64,128]{3,2,1,0:T(8,128)S(1)}, u32[]{:S(2)}, u32[]{:S(2)}) collective-permute-start(f32[4,3,64,128]{3,2,1,0:T(8,128)} %get-tuple-element.14.refs_0_), channel_id=1, source_target_pairs={{0,64},{4,20},{8,72},{12,28},{16,80},{20,4},{24,88},{28,12},{32,96... | collective-permute-start | bytes 1179656 | tf_op jit(solution)/shard_map/ppermute | solution.py:439
  24.2 12.7 %collective-permute-start.6 = (f32[4,3,64,128]{3,2,1,0:T(8,128)}, f32[4,3,64,128]{3,2,1,0:T(8,128)S(1)}, u32[]{:S(2)}, u32[]{:S(2)}) collective-permute-start(f32[4,3,64,128]{3,2,1,0:T(8,128)} %get-tuple-element.14.refs_0_), channel_id=1, source_target_pairs={{0,96},{4,28},{8,104},{12,4},{16,112},{20,12},{24,120},{28,20},{32... | collective-permute-start | bytes 1179656 | tf_op jit(solution)/shard_map/ppermute | solution.py:439
  26.4 16.0 %all-to-all-start = ((f32[16,1,64,128]{3,2,1,0:T(8,128)}), f32[16,1,64,128]{3,2,1,0:T(8,128)S(1)}, u32[]{:S(2)}, u32[]{:S(2)}) async-start(f32[16,1,64,128]{3,2,1,0:T(8,128)} %get-tuple-element.15), calls=%async_computation | async-start | bytes 1048576 | tf_op jit(solution)/shard_map/all_to_all | solution.py:408
  30.1 11.0 %collective-permute-start.7 = (f32[4,3,64,128]{3,2,1,0:T(8,128)}, f32[4,3,64,128]{3,2,1,0:T(8,128)S(1)}, u32[]{:S(2)}, u32[]{:S(2)}) collective-permute-start(f32[4,3,64,128]{3,2,1,0:T(8,128)} %get-tuple-element.14.refs_0_), channel_id=1, source_target_pairs={{0,4},{4,0},{8,12},{12,8},{16,20},{20,16},{24,28},{28,24},{32,36},... | collective-permute-start | bytes 1179656 | tf_op jit(solution)/shard_map/ppermute | solution.py:451
  30.4 16.0 %copy-start.9 = (f32[4,3,64,128]{3,2,1,0:T(8,128)}, f32[4,3,64,128]{3,2,1,0:T(8,128)S(1)}, u32[]{:S(2)}) copy-start(f32[4,3,64,128]{3,2,1,0:T(8,128)S(1)} %collective-permute-done.4.refs_1_) | copy-start | bytes 1179652
  30.4 12.0 %collective-permute-start.8 = (f32[4,3,64,128]{3,2,1,0:T(8,128)S(1)}, f32[4,3,64,128]{3,2,1,0:T(8,128)S(1)}, u32[]{:S(2)}, u32[]{:S(2)}) collective-permute-start(f32[4,3,64,128]{3,2,1,0:T(8,128)S(1)} %collective-permute-done.4.refs_1_), channel_id=1, source_target_pairs={{0,4},{4,0},{8,12},{12,8},{16,20},{20,16},{24,28},{28,24},{32,36},... | collective-permute-start | bytes 1179656 | tf_op jit(solution)/shard_map/ppermute | solution.py:451
  34.4 17.2 %copy-start.10 = (f32[4,3,64,128]{3,2,1,0:T(8,128)}, f32[4,3,64,128]{3,2,1,0:T(8,128)S(1)}, u32[]{:S(2)}) copy-start(f32[4,3,64,128]{3,2,1,0:T(8,128)S(1)} %collective-permute-done.5.refs_2_) | copy-start | bytes 1179652
  34.4 8.0 %collective-permute-start.9 = (f32[4,3,64,128]{3,2,1,0:T(8,128)S(1)}, f32[4,3,64,128]{3,2,1,0:T(8,128)S(1)}, u32[]{:S(2)}, u32[]{:S(2)}) collective-permute-start(f32[4,3,64,128]{3,2,1,0:T(8,128)S(1)} %collective-permute-done.5.refs_2_), channel_id=1, source_target_pairs={{0,4},{4,0},{8,12},{12,8},{16,20},{20,16},{24,28},{28,24},{32,36},... | collective-permute-start | bytes 1179656 | tf_op jit(solution)/shard_map/ppermute | solution.py:451
  36.9 14.8 %copy-start.11 = (f32[4,3,64,128]{3,2,1,0:T(8,128)}, f32[4,3,64,128]{3,2,1,0:T(8,128)S(1)}, u32[]{:S(2)}) copy-start(f32[4,3,64,128]{3,2,1,0:T(8,128)S(1)} %collective-permute-done.6.refs_3_) | copy-start | bytes 1179652
  36.9 5.6 %collective-permute-start.10 = (f32[4,3,64,128]{3,2,1,0:T(8,128)S(1)}, f32[4,3,64,128]{3,2,1,0:T(8,128)S(1)}, u32[]{:S(2)}, u32[]{:S(2)}) collective-permute-start(f32[4,3,64,128]{3,2,1,0:T(8,128)S(1)} %collective-permute-done.6.refs_3_), channel_id=1, source_target_pairs={{0,4},{4,0},{8,12},{12,8},{16,20},{20,16},{24,28},{28,24},{32,36},... | collective-permute-start | bytes 1179656 | tf_op jit(solution)/shard_map/ppermute | solution.py:451
  41.2 1.3 %copy-start.3 = (f32[4,3,64,128]{3,2,1,0:T(8,128)}, f32[4,3,64,128]{3,2,1,0:T(8,128)S(1)}, u32[]{:S(2)}) copy-start(f32[4,3,64,128]{3,2,1,0:T(8,128)S(1)} %collective-permute-done.7.refs_2_.refs_4_) | copy-start | bytes 1179652
  42.4 0.8 copy-start.2
  42.4 0.9 copy-start.4
  42.4 1.0 copy-start.5
  43.5 0.7 copy-start.6
  46.4 21.9 %all-to-all-start.1 = ((f32[32,1,64,128]{3,2,1,0:T(8,128)}), f32[32,1,64,128]{3,2,1,0:T(8,128)S(1)}, u32[]{:S(2)}, u32[]{:S(2)}) async-start(f32[32,1,64,128]{3,2,1,0:T(8,128)} %get-tuple-element.17), calls=%async_computation.1 | async-start | bytes 2097152 | tf_op jit(solution)/shard_map/all_to_all | solution.py:460
  68.2 1.0 copy-start
  86.5 3.7 %collective-permute-start.15 = (f32[16,3,64,128]{3,2,1,0:T(8,128)}, f32[16,3,64,128]{3,2,1,0:T(8,128)S(1)}, u32[]{:S(2)}, u32[]{:S(2)}) collective-permute-start(f32[16,3,64,128]{3,2,1,0:T(8,128)} %get-tuple-element.20), channel_id=1, source_target_pairs={{0,4},{4,0},{8,12},{12,8},{16,20},{20,16},{24,28},{28,24},{32,36},... | collective-permute-start | bytes 4718600 | tf_op jit(solution)/shard_map/ppermute | solution.py:501
  93.1 4.6 %copy-start.15 = (f32[1,64,128]{2,1,0:T(8,128)S(1)}, f32[1,64,128]{2,1,0:T(8,128)}, u32[]{:S(2)}) copy-start(f32[1,64,128]{2,1,0:T(8,128)} %get-tuple-element.18) | copy-start | bytes 98308
  93.1 4.7 %copy-start.1 = (f32[3,4,16,128]{3,2,1,0:T(8,128)S(1)}, f32[3,4,16,128]{3,2,1,0:T(8,128)}, u32[]{:S(2)}) copy-start(f32[3,4,16,128]{3,2,1,0:T(8,128)} %param.7) | copy-start | bytes 294916
  93.1 4.7 %copy-start.8 = (f32[4,16,128]{2,1,0:T(8,128)S(1)}, f32[4,16,128]{2,1,0:T(8,128)}, u32[]{:S(2)}) copy-start(f32[4,16,128]{2,1,0:T(8,128)} %param.8) | copy-start | bytes 98308
  93.1 29.0 %all-to-all-start.2 = ((f32[16,3,64,128]{3,2,1,0:T(8,128)}), f32[16,3,64,128]{3,2,1,0:T(8,128)S(1)}, u32[]{:S(2)}, u32[]{:S(2)}) async-start(f32[16,3,64,128]{3,2,1,0:T(8,128)} %add.155), calls=%async_computation.2 | async-start | bytes 3145728 | tf_op jit(solution)/shard_map/all_to_all | solution.py:408
  97.8 10.4 %collective-permute-start.14 = (f32[5,4,1,128]{3,2,1,0:T(1,128)S(1)}, f32[5,4,1,128]{3,2,1,0:T(1,128)S(1)}, u32[]{:S(2)}, u32[]{:S(2)}) collective-permute-start(f32[5,4,1,128]{3,2,1,0:T(1,128)S(1)} %get-tuple-element.34), channel_id=1, source_target_pairs={{0,1},{1,2},{2,3},{4,5},{5,6},{6,7},{8,9},{9,10},{10,11},{12,13},{... | collective-permute-start | bytes 30728 | tf_op jit(solution)/shard_map/ppermute | solution.py:367
  101.6 6.6 %collective-permute-start.13 = (f32[5,4,1,128]{3,2,1,0:T(1,128)S(1)}, f32[5,4,1,128]{3,2,1,0:T(1,128)S(1)}, u32[]{:S(2)}, u32[]{:S(2)}) collective-permute-start(f32[5,4,1,128]{3,2,1,0:T(1,128)S(1)} %get-tuple-element.33), channel_id=1, source_target_pairs={{1,0},{2,1},{3,2},{5,4},{6,5},{7,6},{9,8},{10,9},{11,10},{13,12},{... | collective-permute-start | bytes 30728 | tf_op jit(solution)/shard_map/ppermute | solution.py:368
  103.1 17.2 %collective-permute-start.12 = (f32[5,1,16,128]{3,2,1,0:T(8,128)S(1)}, f32[5,1,16,128]{3,2,1,0:T(8,128)S(1)}, u32[]{:S(2)}, u32[]{:S(2)}) collective-permute-start(f32[5,1,16,128]{3,2,1,0:T(8,128)S(1)} %get-tuple-element.32), channel_id=1, source_target_pairs={{0,4},{4,8},{8,12},{12,16},{16,20},{20,24},{24,28},{28,32},{32,36}... | collective-permute-start | bytes 122888 | tf_op jit(solution)/shard_map/ppermute | solution.py:367
  103.1 17.1 %collective-permute-start.11 = (f32[5,1,16,128]{3,2,1,0:T(8,128)S(1)}, f32[5,1,16,128]{3,2,1,0:T(8,128)S(1)}, u32[]{:S(2)}, u32[]{:S(2)}) collective-permute-start(f32[5,1,16,128]{3,2,1,0:T(8,128)S(1)} %get-tuple-element.31), channel_id=1, source_target_pairs={{4,0},{8,4},{12,8},{16,12},{20,16},{24,20},{28,24},{32,28},{36,32}... | collective-permute-start | bytes 122888 | tf_op jit(solution)/shard_map/ppermute | solution.py:368

commit v5 on v4

--- a/solution.py
+++ b/solution.py
@@ -133,13 +133,6 @@
     for i, ref in enumerate(tile_refs):
         tiles_ref[pl.ds(i, 1)] = ref[...]
     parts_ref[...] = same_ref[...] + other_ref[...]
-
-
-def owner_kernel(got_ref, *refs):
-    total_ref, tiles_ref = refs[-2:]
-    total = jnp.sum(got_ref[...], axis=0)
-    total_ref[...] = total
-    tiles_ref[...] = jnp.broadcast_to(total[None], tiles_ref.shape)
 
 
 def order_of(slot, tiles):
@@ -449,14 +442,11 @@
     )(block, cell_of)
 
     groups += [lax.ppermute(group, "azim", twin) for group in groups]
-    solid_flat, solid_tiles = pl.pallas_call(
-        owner_kernel,
-        out_shape=(arrays(1, tile_rows, radial), arrays(size, 1, tile_rows, radial)),
-        in_specs=[VMEM_SPEC] + [ANY_SPEC] * (SIDE + 2),
-        out_specs=(VMEM_SPEC, VMEM_SPEC),
-        compiler_params=PARAMS,
-        cost_estimate=cost(2),
-    )(to_owners(dep_parts), words, pair, *groups[SIDE:])
+    got, words, pair, *groups[SIDE:] = lax.optimization_barrier(
+        (to_owners(dep_parts), words, pair, *groups[SIDE:])
+    )
+    solid_flat = jnp.sum(got, axis=0)
+    solid_tiles = jnp.broadcast_to(solid_flat[None], (size,) + solid_flat.shape)
     solid_tiles = lax.all_to_all(solid_tiles, "azim", split_axis=0, concat_axis=0, tiled=True)
 
     here = pl.pallas_call(

time: 124 us -> 121 us (0.976)
  Pallas kernels: 47 us -> 44.8 us
    pallas_call x1 -> x0, Pallas kernels: 2.17 us -> none  [on_device(): pl.pallas_call(owner_kernel, out_shape=(arrays(1, tile_rows, radial), arr...]
    unnamed x32, local copies, waits for them, and re-layouts: 3.59 us -> 1.84 us
    broadcast_in_dim x0 -> x1, local copies, waits for them, and re-layouts: none -> 1.26 us  [on_device(): solid_tiles = jnp.broadcast_to(solid_flat[None], (size,) + solid_flat.shape)]
  transfers between devices with their start and end apart: 19 -> 19, of which waited for: 7 -> 7; matrix products, arithmetic and copies ran while one was open for 3% -> 4% of each run, Pallas kernels for 21% -> 21%
where the time goes in v5:
time: 121 us; the launch traced here: 120 us
  Pallas kernels  44.8 us (37%)
  starting transfers between devices  38.7 us (32%)
  waiting for transfers between devices  24.7 us (20%)
  other arithmetic  7.99 us (7%)
  local copies, waits for them, and re-layouts  3.13 us (3%)
    pallas_call x1, Pallas kernels, on_device(): pl.pallas_call(particle_kernel, out_shape=(arrays(*three), three_sums, th...  17.3 us
    pallas_call x1, Pallas kernels, on_device(): pl.pallas_call(flow_kernel, out_shape=arrays(3, blocks, block_rows), in_s...  14.2 us
    ppermute x2, waiting for transfers between devices, padded_2(): before = lax.ppermute(last, axis, up)  12 us
    all_to_all x2, starting transfers between devices, to_owners(): lax.all_to_all(parts, 'azim', split_axis=0, concat_axis=0, tiled=True, ax...  8.17 us
    pallas_call x1, Pallas kernels, on_device(): pl.pallas_call(deposit_kernel, out_shape=(one_sum, one_sum), in_specs=[SM...  7.51 us
    ppermute x2, starting transfers between devices, padded_2(): after = lax.ppermute(first, axis, down)  6.34 us
    ppermute x3, starting transfers between devices, on_device(): lax.ppermute(flow_tile, 'azim', along(0, k))  5.98 us
    ppermute x3, starting transfers between devices, on_device(): groups = [first] + [lax.ppermute(first, 'azim', along(1, k)) for k in steps]  5.66 us
  transfers between devices with their start and end apart: 19, of which 7 were waited for; matrix products, arithmetic and copies ran while one was open for 4% of the time, Pallas kernels for 21%

profile of v5, /device:TPU:0, one launch (start us, length us, event | category | flops | bytes accessed | tf_op | source)
XLA Modules:
  0.0 120.3 jit_solution(15283256901635053842)
XLA Ops:
  0.6 1.7 %collective-permute-start.1 = (f32[1,3,64,128]{3,2,1,0:T(8,128)}, f32[1,3,64,128]{3,2,1,0:T(8,128)S(1)}, u32[]{:S(2)}, u32[]{:S(2)}) collective-permute-start(f32[1,3,64,128]{3,2,1,0:T(8,128)} %bitcast.23), channel_id=1, source_target_pairs={{0,8},{4,36},{8,16},{12,44},{16,24},{20,52},{24,0},{28,60},{32,40}... | collective-permute-start | bytes 294920 | tf_op jit(solution)/shard_map/ppermute | solution.py:423
  2.4 2.9 %collective-permute-start.2 = (f32[1,3,64,128]{3,2,1,0:T(8,128)}, f32[1,3,64,128]{3,2,1,0:T(8,128)S(1)}, u32[]{:S(2)}, u32[]{:S(2)}) collective-permute-start(f32[1,3,64,128]{3,2,1,0:T(8,128)} %bitcast.24), channel_id=1, source_target_pairs={{0,16},{4,68},{8,24},{12,76},{16,0},{20,84},{24,8},{28,92},{32,48}... | collective-permute-start | bytes 294920 | tf_op jit(solution)/shard_map/ppermute | solution.py:423
  5.3 1.3 %collective-permute-start.3 = (f32[1,3,64,128]{3,2,1,0:T(8,128)}, f32[1,3,64,128]{3,2,1,0:T(8,128)S(1)}, u32[]{:S(2)}, u32[]{:S(2)}) collective-permute-start(f32[1,3,64,128]{3,2,1,0:T(8,128)} %bitcast.25), channel_id=1, source_target_pairs={{0,24},{4,100},{8,0},{12,108},{16,8},{20,116},{24,16},{28,124},{32... | collective-permute-start | bytes 294920 | tf_op jit(solution)/shard_map/ppermute | solution.py:423
  6.6 7.5 %shard_map.86 = (f32[16,1,64,128]{3,2,1,0:T(8,128)}, f32[16,1,64,128]{3,2,1,0:T(8,128)}) custom-call(s32[512]{0:T(512)} %bitcast.41, s32[1]{0:T(128)} %bitcast.2.core_ref, s32[512,128]{1,0:T(8,128)} %cell_ref.7, f32[512,128]{1,0:T(8,128)} %vol_any.1), custom_call_target="tpu_custom_call" | custom-call | bytes 21000000 | tf_op jit(solution)/shard_map/pallas_call | solution.py:407
  14.1 0.1 collective-permute-start
  14.2 0.7 shift-right-arithmetic_add_fusion
  14.9 0.1 convert_reduce_fusion.1
  15.0 0.1 select_reduce_fusion.1
  15.1 1.3 %select_add_fusion = (s32[512]{0:T(512)}, s32[512]{0:T(512)S(1)}) fusion(s32[512]{0:T(512)} %bitcast.42, s32[]{:T(128)S(6)} %select_n.57, s32[]{:T(128)S(6)} %select_n.54, s32[]{:T(128)S(6)} %and.69, s32[]{:T(128)} %select_n.50), kind=kLoop, calls=%fused_computation.98 | loop fusion | flops 31744 | bytes 6160 | tf_op jit(solution)/shard_map/add | solution.py:383
  16.4 0.3 convert_reduce_fusion
  16.8 0.0 collective-permute-done.1.refs_1_
  16.8 0.0 copy-start.12
  16.8 0.0 collective-permute-done.2.refs_2_
  16.8 0.0 collective-permute-done.3.refs_3_
  16.8 0.0 collective-permute-done.other_ref
  16.9 0.6 copy-done.12
  17.4 0.0 copy-done.13
  17.4 0.0 copy-done.14
  17.5 0.2 copy-done.3
  17.7 2.3 %shard_map.87 = (f32[16,1,64,128]{3,2,1,0:T(8,128)}, f32[4,3,64,128]{3,2,1,0:T(8,128)}) custom-call(f32[16,1,64,128]{3,2,1,0:T(8,128)} %get-tuple-element.17.same_ref, f32[16,1,64,128]{3,2,1,0:T(8,128)} %copy-done.3, f32[1,3,64,128]{3,2,1,0:T(8,128)} %bitcast.26, f32[1,3,64,128]{3,2,1,0:T(8,128)} %copy-done.12, f32[1,3,64,128]{3,2,1,0:T(8,128)} %copy-done.13, ...), custom_call_target="tpu_custom_call" | custom-call | bytes 6000000 | tf_op jit(solution)/shard_map/pallas_call | solution.py:424
  19.9 1.5 %collective-permute-start.5 = (f32[4,3,64,128]{3,2,1,0:T(8,128)}, f32[4,3,64,128]{3,2,1,0:T(8,128)S(1)}, u32[]{:S(2)}, u32[]{:S(2)}) collective-permute-start(f32[4,3,64,128]{3,2,1,0:T(8,128)} %get-tuple-element.20.refs_0_), channel_id=1, source_target_pairs={{0,32},{4,12},{8,40},{12,20},{16,48},{20,28},{24,56},{28,4},{32,64... | collective-permute-start | bytes 1179656 | tf_op jit(solution)/shard_map/ppermute | solution.py:432
  21.4 2.7 %collective-permute-start.7 = (f32[4,3,64,128]{3,2,1,0:T(8,128)}, f32[4,3,64,128]{3,2,1,0:T(8,128)S(1)}, u32[]{:S(2)}, u32[]{:S(2)}) collective-permute-start(f32[4,3,64,128]{3,2,1,0:T(8,128)} %get-tuple-element.20.refs_0_), channel_id=1, source_target_pairs={{0,64},{4,20},{8,72},{12,28},{16,80},{20,4},{24,88},{28,12},{32,96... | collective-permute-start | bytes 1179656 | tf_op jit(solution)/shard_map/ppermute | solution.py:432
  24.2 1.4 %collective-permute-start.9 = (f32[4,3,64,128]{3,2,1,0:T(8,128)}, f32[4,3,64,128]{3,2,1,0:T(8,128)S(1)}, u32[]{:S(2)}, u32[]{:S(2)}) collective-permute-start(f32[4,3,64,128]{3,2,1,0:T(8,128)} %get-tuple-element.20.refs_0_), channel_id=1, source_target_pairs={{0,96},{4,28},{8,104},{12,4},{16,112},{20,12},{24,120},{28,20},{32... | collective-permute-start | bytes 1179656 | tf_op jit(solution)/shard_map/ppermute | solution.py:432
  25.6 0.2 select_reduce_fusion
  25.8 0.6 broadcast_add_fusion.1.block_ref
  26.4 3.6 %all-to-all-start = ((f32[16,1,64,128]{3,2,1,0:T(8,128)}), f32[16,1,64,128]{3,2,1,0:T(8,128)S(1)}, u32[]{:S(2)}, u32[]{:S(2)}) async-start(f32[16,1,64,128]{3,2,1,0:T(8,128)} %get-tuple-element.19), calls=%async_computation | async-start | bytes 1048576 | tf_op jit(solution)/shard_map/all_to_all | solution.py:401
  30.0 0.1 select_reduce_fusion.2
  30.1 0.2 collective-permute-start.4
  30.3 0.0 collective-permute-done.5.refs_1_
  30.3 2.7 %collective-permute-start.6 = (f32[4,3,64,128]{3,2,1,0:T(8,128)S(1)}, f32[4,3,64,128]{3,2,1,0:T(8,128)S(1)}, u32[]{:S(2)}, u32[]{:S(2)}) collective-permute-start(f32[4,3,64,128]{3,2,1,0:T(8,128)S(1)} %collective-permute-done.5.refs_1_), channel_id=1, source_target_pairs={{0,4},{4,0},{8,12},{12,8},{16,20},{20,16},{24,28},{28,24},{32,36},... | collective-permute-start | bytes 1179656 | tf_op jit(solution)/shard_map/ppermute | solution.py:444
  33.0 1.4 %collective-permute-done.7.refs_2_ = f32[4,3,64,128]{3,2,1,0:T(8,128)S(1)} collective-permute-done((f32[4,3,64,128]{3,2,1,0:T(8,128)}, f32[4,3,64,128]{3,2,1,0:T(8,128)S(1)}, u32[]{:S(2)}, u32[]{:S(2)}) %collective-permute-start.7) | collective-permute-done | bytes 393248 | tf_op jit(solution)/shard_map/ppermute | solution.py:432
  34.4 0.0 collective-permute-start.8
  34.4 2.5 %collective-permute-done.9.refs_3_ = f32[4,3,64,128]{3,2,1,0:T(8,128)S(1)} collective-permute-done((f32[4,3,64,128]{3,2,1,0:T(8,128)}, f32[4,3,64,128]{3,2,1,0:T(8,128)S(1)}, u32[]{:S(2)}, u32[]{:S(2)}) %collective-permute-start.9) | collective-permute-done | bytes 393248 | tf_op jit(solution)/shard_map/ppermute | solution.py:432
  36.8 0.0 collective-permute-start.10
  36.9 3.6 %shard_map.88.words_ref = s32[4,128,128]{2,1,0:T(8,128)} custom-call(s32[544]{0:T(1024)} %broadcast_add_fusion.1.block_ref, s32[512,128]{1,0:T(8,128)} %cell_ref.7), custom_call_target="tpu_custom_call" | custom-call | bytes 6000000 | tf_op jit(solution)/shard_map/pallas_call | solution.py:434
  40.5 0.1 convert_reduce_fusion.2
  40.5 0.6 broadcast_minimum_fusion.pair_ref
  41.1 0.0 collective-permute-done.4.refs_4_
  41.1 1.2 %all-to-all-done = f32[16,1,64,128]{3,2,1,0:T(8,128)S(1)} async-done(((f32[16,1,64,128]{3,2,1,0:T(8,128)}), f32[16,1,64,128]{3,2,1,0:T(8,128)S(1)}, u32[]{:S(2)}, u32[]{:S(2)}) %all-to-all-start) | async-done | bytes 524320 | tf_op jit(solution)/shard_map/all_to_all | solution.py:401
  42.4 0.0 collective-permute-done.6.refs_5_
  42.4 0.0 collective-permute-done.8.refs_6_
  42.4 0.0 collective-permute-done.10.refs_7_
  42.5 0.0 copy-start.2
  42.5 1.3 %broadcast_in_dim.46 = f32[32,1,64,128]{3,2,1,0:T(8,128)} broadcast(f32[64,128]{1,0:T(8,128)S(1)} %reduce_sum.80), dimensions={2,3} | broadcast | bytes 1081344 | tf_op jit(solution)/shard_map/broadcast_in_dim | solution.py:449
  43.8 5.2 %all-to-all-start.1 = ((f32[32,1,64,128]{3,2,1,0:T(8,128)}), f32[32,1,64,128]{3,2,1,0:T(8,128)S(1)}, u32[]{:S(2)}, u32[]{:S(2)}) async-start(f32[32,1,64,128]{3,2,1,0:T(8,128)} %broadcast_in_dim.46), calls=%async_computation.1 | async-start | bytes 2097152 | tf_op jit(solution)/shard_map/all_to_all | solution.py:450
  49.0 14.2 %shard_map.89.here_any = f32[3,512,128]{2,1,0:T(8,128)} custom-call(s32[512]{0:T(512)} %get-tuple-element.47.slot_ref, s32[512,128]{1,0:T(8,128)} %cell_ref.7, f32[4,3,64,128]{3,2,1,0:T(8,128)} %get-tuple-element.20.refs_0_, f32[4,3,64,128]{3,2,1,0:T(8,128)} %copy-done.5, f32[4,3,64,128]{3,2,1,0:T(8,128)} %copy-done.6, f32[4,3,64,128]{3,2,1,0:T(8,128)} %copy-done.7, ...), custom_call_target="tpu_custom_call" | custom-call | bytes 54000000 | tf_op jit(solution)/shard_map/pallas_call | solution.py:452
  63.1 2.5 %all-to-all-done.1.solid_any = f32[32,1,64,128]{3,2,1,0:T(8,128)S(1)} async-done(((f32[32,1,64,128]{3,2,1,0:T(8,128)}), f32[32,1,64,128]{3,2,1,0:T(8,128)S(1)}, u32[]{:S(2)}, u32[]{:S(2)}) %all-to-all-start.1) | async-done | bytes 1048608 | tf_op jit(solution)/shard_map/all_to_all | solution.py:450
  65.6 1.0 copy-done
  66.6 17.3 %shard_map.90 = (f32[3,512,128]{2,1,0:T(8,128)}, f32[16,3,64,128]{3,2,1,0:T(8,128)}, f32[16,3,64,128]{3,2,1,0:T(8,128)}, f32[1,64,128]{2,1,0:T(8,128)}) custom-call(s32[512]{0:T(512)} %bitcast.43, s32[544]{0:T(1024)} %broadcast_add_fusion.1.block_ref, s32[272]{0:T(512)} %broadcast_minimum_fusion.pair_ref, s32[512,128]{1,0:T(8,128)} %cell_ref.7, ...), custom_call_target="tpu_custom_call" | custom-call | bytes 60000000 | tf_op jit(solution)/shard_map/pallas_call | solution.py:467
  83.8 0.5 collective-permute-start.15
  84.3 3.2 %collective-permute-done.15 = f32[16,3,64,128]{3,2,1,0:T(8,128)S(1)} collective-permute-done((f32[16,3,64,128]{3,2,1,0:T(8,128)}, f32[16,3,64,128]{3,2,1,0:T(8,128)S(1)}, u32[]{:S(2)}, u32[]{:S(2)}) %collective-permute-start.15) | collective-permute-done | bytes 1572896 | tf_op jit(solution)/shard_map/ppermute | solution.py:491
  87.5 2.8 %add.155 = f32[16,3,64,128]{3,2,1,0:T(8,128)} add(f32[16,3,64,128]{3,2,1,0:T(8,128)} %get-tuple-element.29, f32[16,3,64,128]{3,2,1,0:T(8,128)S(1)} %collective-permute-done.15) | non-fusion elementwise | flops 393216 | bytes 4718592 | tf_op jit(solution)/shard_map/add | solution.py:491
  90.4 4.6 %all-to-all-start.2 = ((f32[16,3,64,128]{3,2,1,0:T(8,128)}), f32[16,3,64,128]{3,2,1,0:T(8,128)S(1)}, u32[]{:S(2)}, u32[]{:S(2)}) async-start(f32[16,3,64,128]{3,2,1,0:T(8,128)} %add.155), calls=%async_computation.2 | async-start | bytes 3145728 | tf_op jit(solution)/shard_map/all_to_all | solution.py:401
  95.1 3.9 %collective-permute-start.14 = (f32[5,4,1,128]{3,2,1,0:T(1,128)S(1)}, f32[5,4,1,128]{3,2,1,0:T(1,128)S(1)}, u32[]{:S(2)}, u32[]{:S(2)}) collective-permute-start(f32[5,4,1,128]{3,2,1,0:T(1,128)S(1)} %get-tuple-element.44), channel_id=1, source_target_pairs={{0,1},{1,2},{2,3},{4,5},{5,6},{6,7},{8,9},{9,10},{10,11},{12,13},{... | collective-permute-start | bytes 30728 | tf_op jit(solution)/shard_map/ppermute | solution.py:360
  98.9 1.3 %collective-permute-start.13 = (f32[5,4,1,128]{3,2,1,0:T(1,128)S(1)}, f32[5,4,1,128]{3,2,1,0:T(1,128)S(1)}, u32[]{:S(2)}, u32[]{:S(2)}) collective-permute-start(f32[5,4,1,128]{3,2,1,0:T(1,128)S(1)} %get-tuple-element.43), channel_id=1, source_target_pairs={{1,0},{2,1},{3,2},{5,4},{6,5},{7,6},{9,8},{10,9},{11,10},{13,12},{... | collective-permute-start | bytes 30728 | tf_op jit(solution)/shard_map/ppermute | solution.py:361
  100.3 0.1 fusion.23
  100.4 0.1 collective-permute-start.12
  100.4 5.1 %collective-permute-start.11 = (f32[5,1,16,128]{3,2,1,0:T(8,128)S(1)}, f32[5,1,16,128]{3,2,1,0:T(8,128)S(1)}, u32[]{:S(2)}, u32[]{:S(2)}) collective-permute-start(f32[5,1,16,128]{3,2,1,0:T(8,128)S(1)} %get-tuple-element.41), channel_id=1, source_target_pairs={{4,0},{8,4},{12,8},{16,12},{20,16},{24,20},{28,24},{32,28},{36,32}... | collective-permute-start | bytes 122888 | tf_op jit(solution)/shard_map/ppermute | solution.py:361
  105.5 0.0 collective-permute-done.14
  105.5 12.0 %collective-permute-done.12 = f32[5,1,16,128]{3,2,1,0:T(8,128)S(1)} collective-permute-done((f32[5,1,16,128]{3,2,1,0:T(8,128)S(1)}, f32[5,1,16,128]{3,2,1,0:T(8,128)S(1)}, u32[]{:S(2)}, u32[]{:S(2)}) %collective-permute-start.12) | collective-permute-done | bytes 40992 | tf_op jit(solution)/shard_map/ppermute | solution.py:360
  117.5 0.0 collective-permute-done.11
  117.6 1.8 %all-to-all-done.2 = f32[16,3,64,128]{3,2,1,0:T(8,128)S(1)} async-done(((f32[16,3,64,128]{3,2,1,0:T(8,128)}), f32[16,3,64,128]{3,2,1,0:T(8,128)S(1)}, u32[]{:S(2)}, u32[]{:S(2)}) %all-to-all-start.2) | async-done | bytes 1572896 | tf_op jit(solution)/shard_map/all_to_all | solution.py:401
  119.4 0.1 reduce_sum.82
  119.5 0.8 fusion.11
  (37 shorter events, 0.2 us)
Async XLA Ops:
  0.6 16.1 %collective-permute-start.1 = (f32[1,3,64,128]{3,2,1,0:T(8,128)}, f32[1,3,64,128]{3,2,1,0:T(8,128)S(1)}, u32[]{:S(2)}, u32[]{:S(2)}) collective-permute-start(f32[1,3,64,128]{3,2,1,0:T(8,128)} %bitcast.23), channel_id=1, source_target_pairs={{0,8},{4,36},{8,16},{12,44},{16,24},{20,52},{24,0},{28,60},{32,40}... | collective-permute-start | bytes 294920 | tf_op jit(solution)/shard_map/ppermute | solution.py:423
  2.4 14.4 %collective-permute-start.2 = (f32[1,3,64,128]{3,2,1,0:T(8,128)}, f32[1,3,64,128]{3,2,1,0:T(8,128)S(1)}, u32[]{:S(2)}, u32[]{:S(2)}) collective-permute-start(f32[1,3,64,128]{3,2,1,0:T(8,128)} %bitcast.24), channel_id=1, source_target_pairs={{0,16},{4,68},{8,24},{12,76},{16,0},{20,84},{24,8},{28,92},{32,48}... | collective-permute-start | bytes 294920 | tf_op jit(solution)/shard_map/ppermute | solution.py:423
  5.3 11.6 %collective-permute-start.3 = (f32[1,3,64,128]{3,2,1,0:T(8,128)}, f32[1,3,64,128]{3,2,1,0:T(8,128)S(1)}, u32[]{:S(2)}, u32[]{:S(2)}) collective-permute-start(f32[1,3,64,128]{3,2,1,0:T(8,128)} %bitcast.25), channel_id=1, source_target_pairs={{0,24},{4,100},{8,0},{12,108},{16,8},{20,116},{24,16},{28,124},{32... | collective-permute-start | bytes 294920 | tf_op jit(solution)/shard_map/ppermute | solution.py:423
  14.1 2.7 %collective-permute-start = (f32[16,1,64,128]{3,2,1,0:T(8,128)}, f32[16,1,64,128]{3,2,1,0:T(8,128)S(1)}, u32[]{:S(2)}, u32[]{:S(2)}) collective-permute-start(f32[16,1,64,128]{3,2,1,0:T(8,128)} %get-tuple-element.18), channel_id=1, source_target_pairs={{0,4},{4,0},{8,12},{12,8},{16,20},{20,16},{24,28},{28,24},{32,36},... | collective-permute-start | bytes 1572872 | tf_op jit(solution)/shard_map/ppermute | solution.py:422
  16.8 0.6 copy-start.12
  16.8 0.6 copy-start.13
  16.8 0.7 copy-start.14
  16.8 0.8 copy-start.3
  19.9 10.4 %collective-permute-start.5 = (f32[4,3,64,128]{3,2,1,0:T(8,128)}, f32[4,3,64,128]{3,2,1,0:T(8,128)S(1)}, u32[]{:S(2)}, u32[]{:S(2)}) collective-permute-start(f32[4,3,64,128]{3,2,1,0:T(8,128)} %get-tuple-element.20.refs_0_), channel_id=1, source_target_pairs={{0,32},{4,12},{8,40},{12,20},{16,48},{20,28},{24,56},{28,4},{32,64... | collective-permute-start | bytes 1179656 | tf_op jit(solution)/shard_map/ppermute | solution.py:432
  21.4 12.9 %collective-permute-start.7 = (f32[4,3,64,128]{3,2,1,0:T(8,128)}, f32[4,3,64,128]{3,2,1,0:T(8,128)S(1)}, u32[]{:S(2)}, u32[]{:S(2)}) collective-permute-start(f32[4,3,64,128]{3,2,1,0:T(8,128)} %get-tuple-element.20.refs_0_), channel_id=1, source_target_pairs={{0,64},{4,20},{8,72},{12,28},{16,80},{20,4},{24,88},{28,12},{32,96... | collective-permute-start | bytes 1179656 | tf_op jit(solution)/shard_map/ppermute | solution.py:432
  24.2 12.7 %collective-permute-start.9 = (f32[4,3,64,128]{3,2,1,0:T(8,128)}, f32[4,3,64,128]{3,2,1,0:T(8,128)S(1)}, u32[]{:S(2)}, u32[]{:S(2)}) collective-permute-start(f32[4,3,64,128]{3,2,1,0:T(8,128)} %get-tuple-element.20.refs_0_), channel_id=1, source_target_pairs={{0,96},{4,28},{8,104},{12,4},{16,112},{20,12},{24,120},{28,20},{32... | collective-permute-start | bytes 1179656 | tf_op jit(solution)/shard_map/ppermute | solution.py:432
  26.4 16.0 %all-to-all-start = ((f32[16,1,64,128]{3,2,1,0:T(8,128)}), f32[16,1,64,128]{3,2,1,0:T(8,128)S(1)}, u32[]{:S(2)}, u32[]{:S(2)}) async-start(f32[16,1,64,128]{3,2,1,0:T(8,128)} %get-tuple-element.19), calls=%async_computation | async-start | bytes 1048576 | tf_op jit(solution)/shard_map/all_to_all | solution.py:401
  30.1 11.0 %collective-permute-start.4 = (f32[4,3,64,128]{3,2,1,0:T(8,128)}, f32[4,3,64,128]{3,2,1,0:T(8,128)S(1)}, u32[]{:S(2)}, u32[]{:S(2)}) collective-permute-start(f32[4,3,64,128]{3,2,1,0:T(8,128)} %get-tuple-element.20.refs_0_), channel_id=1, source_target_pairs={{0,4},{4,0},{8,12},{12,8},{16,20},{20,16},{24,28},{28,24},{32,36},... | collective-permute-start | bytes 1179656 | tf_op jit(solution)/shard_map/ppermute | solution.py:444
  30.3 13.4 %copy-start.5 = (f32[4,3,64,128]{3,2,1,0:T(8,128)}, f32[4,3,64,128]{3,2,1,0:T(8,128)S(1)}, u32[]{:S(2)}) copy-start(f32[4,3,64,128]{3,2,1,0:T(8,128)S(1)} %collective-permute-done.5.refs_1_) | copy-start | bytes 1179652
  30.3 12.0 %collective-permute-start.6 = (f32[4,3,64,128]{3,2,1,0:T(8,128)S(1)}, f32[4,3,64,128]{3,2,1,0:T(8,128)S(1)}, u32[]{:S(2)}, u32[]{:S(2)}) collective-permute-start(f32[4,3,64,128]{3,2,1,0:T(8,128)S(1)} %collective-permute-done.5.refs_1_), channel_id=1, source_target_pairs={{0,4},{4,0},{8,12},{12,8},{16,20},{20,16},{24,28},{28,24},{32,36},... | collective-permute-start | bytes 1179656 | tf_op jit(solution)/shard_map/ppermute | solution.py:444
  34.4 9.4 %copy-start.6 = (f32[4,3,64,128]{3,2,1,0:T(8,128)}, f32[4,3,64,128]{3,2,1,0:T(8,128)S(1)}, u32[]{:S(2)}) copy-start(f32[4,3,64,128]{3,2,1,0:T(8,128)S(1)} %collective-permute-done.7.refs_2_) | copy-start | bytes 1179652
  34.4 8.0 %collective-permute-start.8 = (f32[4,3,64,128]{3,2,1,0:T(8,128)S(1)}, f32[4,3,64,128]{3,2,1,0:T(8,128)S(1)}, u32[]{:S(2)}, u32[]{:S(2)}) collective-permute-start(f32[4,3,64,128]{3,2,1,0:T(8,128)S(1)} %collective-permute-done.7.refs_2_), channel_id=1, source_target_pairs={{0,4},{4,0},{8,12},{12,8},{16,20},{20,16},{24,28},{28,24},{32,36},... | collective-permute-start | bytes 1179656 | tf_op jit(solution)/shard_map/ppermute | solution.py:444
  36.8 6.9 %copy-start.7 = (f32[4,3,64,128]{3,2,1,0:T(8,128)}, f32[4,3,64,128]{3,2,1,0:T(8,128)S(1)}, u32[]{:S(2)}) copy-start(f32[4,3,64,128]{3,2,1,0:T(8,128)S(1)} %collective-permute-done.9.refs_3_) | copy-start | bytes 1179652
  36.8 5.6 %collective-permute-start.10 = (f32[4,3,64,128]{3,2,1,0:T(8,128)S(1)}, f32[4,3,64,128]{3,2,1,0:T(8,128)S(1)}, u32[]{:S(2)}, u32[]{:S(2)}) collective-permute-start(f32[4,3,64,128]{3,2,1,0:T(8,128)S(1)} %collective-permute-done.9.refs_3_), channel_id=1, source_target_pairs={{0,4},{4,0},{8,12},{12,8},{16,20},{20,16},{24,28},{28,24},{32,36},... | collective-permute-start | bytes 1179656 | tf_op jit(solution)/shard_map/ppermute | solution.py:444
  41.1 2.6 %copy-start.8 = (f32[4,3,64,128]{3,2,1,0:T(8,128)}, f32[4,3,64,128]{3,2,1,0:T(8,128)S(1)}, u32[]{:S(2)}) copy-start(f32[4,3,64,128]{3,2,1,0:T(8,128)S(1)} %collective-permute-done.4.refs_4_) | copy-start | bytes 1179652
  42.4 1.4 %copy-start.9 = (f32[4,3,64,128]{3,2,1,0:T(8,128)}, f32[4,3,64,128]{3,2,1,0:T(8,128)S(1)}, u32[]{:S(2)}) copy-start(f32[4,3,64,128]{3,2,1,0:T(8,128)S(1)} %collective-permute-done.6.refs_5_) | copy-start | bytes 1179652
  42.4 1.4 %copy-start.10 = (f32[4,3,64,128]{3,2,1,0:T(8,128)}, f32[4,3,64,128]{3,2,1,0:T(8,128)S(1)}, u32[]{:S(2)}) copy-start(f32[4,3,64,128]{3,2,1,0:T(8,128)S(1)} %collective-permute-done.8.refs_6_) | copy-start | bytes 1179652
  42.4 1.3 %copy-start.11 = (f32[4,3,64,128]{3,2,1,0:T(8,128)}, f32[4,3,64,128]{3,2,1,0:T(8,128)S(1)}, u32[]{:S(2)}) copy-start(f32[4,3,64,128]{3,2,1,0:T(8,128)S(1)} %collective-permute-done.10.refs_7_) | copy-start | bytes 1179652
  42.5 1.3 %copy-start.2 = (f32[64,128]{1,0:T(8,128)}, f32[64,128]{1,0:T(8,128)S(1)}, u32[]{:S(2)}) copy-start(f32[64,128]{1,0:T(8,128)S(1)} %reduce_sum.80) | copy-start | bytes 98308
  43.8 21.8 %all-to-all-start.1 = ((f32[32,1,64,128]{3,2,1,0:T(8,128)}), f32[32,1,64,128]{3,2,1,0:T(8,128)S(1)}, u32[]{:S(2)}, u32[]{:S(2)}) async-start(f32[32,1,64,128]{3,2,1,0:T(8,128)} %broadcast_in_dim.46), calls=%async_computation.1 | async-start | bytes 2097152 | tf_op jit(solution)/shard_map/all_to_all | solution.py:450
  65.6 1.0 copy-start
  83.8 3.7 %collective-permute-start.15 = (f32[16,3,64,128]{3,2,1,0:T(8,128)}, f32[16,3,64,128]{3,2,1,0:T(8,128)S(1)}, u32[]{:S(2)}, u32[]{:S(2)}) collective-permute-start(f32[16,3,64,128]{3,2,1,0:T(8,128)} %get-tuple-element.30), channel_id=1, source_target_pairs={{0,4},{4,0},{8,12},{12,8},{16,20},{20,16},{24,28},{28,24},{32,36},... | collective-permute-start | bytes 4718600 | tf_op jit(solution)/shard_map/ppermute | solution.py:491
  90.4 4.6 %copy-start.15 = (f32[1,64,128]{2,1,0:T(8,128)S(1)}, f32[1,64,128]{2,1,0:T(8,128)}, u32[]{:S(2)}) copy-start(f32[1,64,128]{2,1,0:T(8,128)} %get-tuple-element.28) | copy-start | bytes 98308
  90.4 4.6 %copy-start.1 = (f32[3,4,16,128]{3,2,1,0:T(8,128)S(1)}, f32[3,4,16,128]{3,2,1,0:T(8,128)}, u32[]{:S(2)}) copy-start(f32[3,4,16,128]{3,2,1,0:T(8,128)} %param.7) | copy-start | bytes 294916
  90.4 4.7 %copy-start.4 = (f32[4,16,128]{2,1,0:T(8,128)S(1)}, f32[4,16,128]{2,1,0:T(8,128)}, u32[]{:S(2)}) copy-start(f32[4,16,128]{2,1,0:T(8,128)} %param.8) | copy-start | bytes 98308
  90.4 29.0 %all-to-all-start.2 = ((f32[16,3,64,128]{3,2,1,0:T(8,128)}), f32[16,3,64,128]{3,2,1,0:T(8,128)S(1)}, u32[]{:S(2)}, u32[]{:S(2)}) async-start(f32[16,3,64,128]{3,2,1,0:T(8,128)} %add.155), calls=%async_computation.2 | async-start | bytes 3145728 | tf_op jit(solution)/shard_map/all_to_all | solution.py:401
  95.1 10.4 %collective-permute-start.14 = (f32[5,4,1,128]{3,2,1,0:T(1,128)S(1)}, f32[5,4,1,128]{3,2,1,0:T(1,128)S(1)}, u32[]{:S(2)}, u32[]{:S(2)}) collective-permute-start(f32[5,4,1,128]{3,2,1,0:T(1,128)S(1)} %get-tuple-element.44), channel_id=1, source_target_pairs={{0,1},{1,2},{2,3},{4,5},{5,6},{6,7},{8,9},{9,10},{10,11},{12,13},{... | collective-permute-start | bytes 30728 | tf_op jit(solution)/shard_map/ppermute | solution.py:360
  98.9 6.6 %collective-permute-start.13 = (f32[5,4,1,128]{3,2,1,0:T(1,128)S(1)}, f32[5,4,1,128]{3,2,1,0:T(1,128)S(1)}, u32[]{:S(2)}, u32[]{:S(2)}) collective-permute-start(f32[5,4,1,128]{3,2,1,0:T(1,128)S(1)} %get-tuple-element.43), channel_id=1, source_target_pairs={{1,0},{2,1},{3,2},{5,4},{6,5},{7,6},{9,8},{10,9},{11,10},{13,12},{... | collective-permute-start | bytes 30728 | tf_op jit(solution)/shard_map/ppermute | solution.py:361
  100.4 17.2 %collective-permute-start.12 = (f32[5,1,16,128]{3,2,1,0:T(8,128)S(1)}, f32[5,1,16,128]{3,2,1,0:T(8,128)S(1)}, u32[]{:S(2)}, u32[]{:S(2)}) collective-permute-start(f32[5,1,16,128]{3,2,1,0:T(8,128)S(1)} %get-tuple-element.42), channel_id=1, source_target_pairs={{0,4},{4,8},{8,12},{12,16},{16,20},{20,24},{24,28},{28,32},{32,36}... | collective-permute-start | bytes 122888 | tf_op jit(solution)/shard_map/ppermute | solution.py:360
  100.4 17.1 %collective-permute-start.11 = (f32[5,1,16,128]{3,2,1,0:T(8,128)S(1)}, f32[5,1,16,128]{3,2,1,0:T(8,128)S(1)}, u32[]{:S(2)}, u32[]{:S(2)}) collective-permute-start(f32[5,1,16,128]{3,2,1,0:T(8,128)S(1)} %get-tuple-element.41), channel_id=1, source_target_pairs={{4,0},{8,4},{12,8},{16,12},{20,16},{24,20},{28,24},{32,28},{36,32}... | collective-permute-start | bytes 122888 | tf_op jit(solution)/shard_map/ppermute | solution.py:361
